TPU v7x, 32 devices: a whole 2x2x4 slice. The times are simulated.
32 devices in a mesh: groups: 2 (over y), zone: 4 (over z), scen: 2 (over x), hour: 2 (over core).
Axes of the slice: x: 2, y: 2, z: 4, core: 2. Of those that a mesh axis runs over, the one named last changes fastest.
Arguments:
- forcing: bfloat16 [1024, 48, 64], P(('groups', 'zone', 'scen', 'hour')), parts along dimension 0, may hold values from -3 to 3
- response: bfloat16 [48, 64, 8192], P('hour', None, ('groups', 'zone')), parts along dimension 2, may hold values from -0.75 to 0.75
- window_params: float32 [128, 64], P('groups'), parts along dimension 0, may hold values from 0.5 to 1.5
- building_map: int32 [8192], P(('groups', 'zone')), parts along dimension 0, may hold values from 0 to 1023
- owner_ids: int32 [2048], P('groups'), parts along dimension 0, may hold values from 0 to 63
- band_ids: int32 [48, 8192], P('hour', ('groups', 'zone')), parts along dimension 1, may hold values from 0 to 7
- floor_area: float32 [8192], P(('groups', 'zone')), parts along dimension 0, may hold values from 0.5 to 18, as said below
Outputs:
- sensitivity: float32 [128, 64], P(('groups', 'zone', 'scen', 'hour')), parts along dimension 0
- objective: float32 [2], P('groups'), parts along dimension 0
There are 2 independent parts, one for each index of `groups`. A program takes and returns all parts, laid end to end along the dimension named above; each array names one. Nothing has to cross between parts.
Inputs may be any that keep to these rules, and one draw needn't show every extreme that they name: `floor_area`: floor areas are positive.
All inputs are finite; a program needn't handle non-finite values.
Results may differ from a plain program's by a relative error of at most 0.0006.
Values may be sent and summed in bfloat16 or wider, within the bound.
No kernel may reach another device: no remote copies, remote signals or barrier semaphores. Data moves between devices by JAX's collectives and lax.ppermute only.
A program may use at most 128 MiB of HBM per device.

v0:
```python
import math

import jax
import jax.numpy as jnp
from jax import lax
from jax.sharding import PartitionSpec as P

SHARPNESS = 200.0


def joined(value, axis, join):
    pieces = jax.tree.map(lambda part: lax.all_gather(part, axis), value)
    head = jax.tree.map(lambda part: part[0], pieces)
    tail = jax.tree.map(lambda part: part[1:], pieces)
    running, _ = lax.scan(lambda running, share: (join(running, share), None), head, tail)
    return running


def merge_softmax(first, second):
    highest = jnp.maximum(first[0], second[0])
    return (
        highest,
        first[1] * jnp.exp(first[0] - highest) + second[1] * jnp.exp(second[0] - highest),
    )


def on_device(forcing, response, window_params, building_map, owner_ids, band_ids, floor_area):
    hour_local = response.shape[0]
    width = response.shape[1]
    zone_local = response.shape[2]
    hours_total = hour_local * lax.axis_size("hour")
    hour_first = lax.axis_index("hour") * hour_local
    positions = (hour_first + jnp.arange(hour_local)).astype(jnp.float32)
    occupant_level = 1.0 + 2.0 * positions / (hours_total - 1)
    candidate_plan = jnp.take(owner_ids, building_map)
    zone_parameters = jnp.take(window_params, candidate_plan, axis=0)
    coeff = (response.astype(jnp.float32) * zone_parameters.T[None, :, :]).astype(jnp.bfloat16)
    band_low = 0.25 * (band_ids.astype(jnp.float32) - 3.5) - 0.5
    band_high = band_low + 1.0
    zone_weight = occupant_level[:, None] * floor_area[None, :]
    block_count = hour_local // 8
    mine = lax.all_to_all(forcing, "hour", split_axis=1, concat_axis=0, tiled=True)

    def inside_climate_state(outlook_records, initial_clock_time):
        record_elements = lax.slice_in_dim(
            outlook_records, initial_clock_time, initial_clock_time + 8, axis=1
        )
        thermal_demand = jnp.einsum(
            "shp,hpz->hsz",
            record_elements,
            coeff[initial_clock_time : initial_clock_time + 8],
            preferred_element_type=jnp.float32,
        )
        return (thermal_demand, record_elements)

    weight_part = (jnp.sum(floor_area) * jnp.sum(occupant_level)).reshape(1)
    outlook_records = lax.all_gather(mine, "zone", axis=0, tiled=True)
    sums = jnp.zeros((outlook_records.shape[0],), jnp.float32)
    for hour_block in range(block_count):
        initial_clock_time = hour_block * 8
        thermal_demand, record_elements = inside_climate_state(outlook_records, initial_clock_time)
        low = band_low[initial_clock_time : initial_clock_time + 8][:, None, :]
        high = band_high[initial_clock_time : initial_clock_time + 8][:, None, :]
        penalty = jax.nn.softplus(thermal_demand - high) + jax.nn.softplus(low - thermal_demand)
        sums = sums + jnp.sum(
            penalty * zone_weight[initial_clock_time : initial_clock_time + 8][:, None, :],
            axis=(0, 2),
        )
    loss_sum, weight_total = lax.psum((sums, weight_part), ("zone", "hour"))
    scores = SHARPNESS * loss_sum / weight_total[0]
    local_peak = jnp.max(scores)
    peak_score, exp_total = joined(
        (local_peak, jnp.sum(jnp.exp(scores - local_peak))), "scen", merge_softmax
    )
    objective = ((peak_score + jnp.log(exp_total)) / SHARPNESS).reshape(1)
    scen_weight = jnp.exp(scores - peak_score) / exp_total / weight_total[0]
    empty = jnp.zeros((width, zone_local), jnp.float32)
    accumulated = empty
    outlook_records = lax.all_gather(mine, "zone", axis=0, tiled=True)
    for hour_block in range(block_count):
        initial_clock_time = hour_block * 8
        thermal_demand, record_elements = inside_climate_state(outlook_records, initial_clock_time)
        low = band_low[initial_clock_time : initial_clock_time + 8][:, None, :]
        high = band_high[initial_clock_time : initial_clock_time + 8][:, None, :]
        slope = jax.nn.sigmoid(thermal_demand - high) - jax.nn.sigmoid(low - thermal_demand)
        adjoint = (
            slope
            * scen_weight[None, :, None]
            * zone_weight[initial_clock_time : initial_clock_time + 8][:, None, :]
        ).astype(jnp.bfloat16)
        mixed = jnp.einsum(
            "shp,hsz->hpz", record_elements, adjoint, preferred_element_type=jnp.float32
        )
        accumulated = accumulated + jnp.sum(
            response[initial_clock_time : initial_clock_time + 8].astype(jnp.float32) * mixed,
            axis=0,
        )
    zones_all = zone_local * lax.axis_size("zone")
    designs = window_params.shape[0]
    gain = math.sqrt(width * zones_all * hours_total * designs)
    zone_rows = accumulated.T
    owners_local = designs // (
        lax.axis_size("zone") * lax.axis_size("scen") * lax.axis_size("hour")
    )
    onehot = (
        candidate_plan[:, None]
        == jnp.arange(owners_local * lax.axis_size(("zone", "scen", "hour")))[None, :]
    ).astype(jnp.float32)
    sensitivity = lax.psum_scatter(
        gain * jnp.dot(onehot.T, zone_rows, precision=lax.Precision.HIGHEST),
        ("zone", "scen", "hour"),
        scatter_dimension=0,
        tiled=True,
    )
    return (sensitivity, objective)


def solution(mesh):
    in_specs = (
        P(("groups", "zone", "scen", "hour"), None, None),
        P("hour", None, ("groups", "zone")),
        P("groups", None),
        P(("groups", "zone")),
        P("groups"),
        P("hour", ("groups", "zone")),
        P(("groups", "zone")),
    )
    out_specs = (P(("groups", "zone", "scen", "hour"), None), P("groups"))
    return jax.shard_map(
        on_device, mesh=mesh, in_specs=in_specs, out_specs=out_specs, check_vma=False
    )
```

profile of v0, /device:TPU:0, one launch (start us, length us, event | category | flops | bytes accessed | tf_op | source)
XLA Modules:
  0.0 207.4 jit_solution(13071616913442641954)
XLA Ops:
  0.7 1.2 copy.37
  1.8 1.0 reshape.77
  2.9 3.4 %all-to-all-start = ((bf16[2,2,24576]{2,1,0:T(2,128)(2,1)}), bf16[2,2,24576]{2,1,0:T(2,128)(2,1)S(1)}, u32[]{:S(2)}, u32[]{:S(2)}) async-start(bf16[2,2,24576]{2,1,0:T(2,128)(2,1)} %reshape.77), calls=%async_computation | async-start | bytes 393216 | tf_op jit(solution)/shard_map/all_to_all | solution.py:42
  6.3 1.5 all-to-all-done
  7.8 0.3 reshape.78
  8.2 31.7 %all_gather.16 = bf16[256,24,64]{2,1,0:T(8,128)(2,1)S(1)} all-gather(bf16[64,24,64]{2,1,0:T(8,128)(2,1)S(1)} %bitcast.231), channel_id=1, replica_groups=mesh['groups'=2,'zone'=4,'scen'=2,'hour'=2] {'zone'}, dimensions={0}, use_global_device_ids=true | all-gather | bytes 983040 | tf_op jit(solution)/shard_map/all_gather | solution.py:79
  40.2 0.3 copy.35
  40.6 0.6 multiply_add_fusion
  41.3 4.5 %gather_fusion = s32[1024]{0:T(1024)S(1)} fusion(s32[1024]{0:T(1024)S(1)} %copy-done.1, s32[1024]{0:T(1024)S(1)} %fusion.88), kind=kCustom, calls=%fused_computation | custom fusion | bytes 12288 | tf_op jit(solution)/shard_map/jit(_take)/gather | solution.py:35
  45.9 2.8 %gather_fusion.1 = f32[1024,64]{1,0:T(8,128)S(1)} fusion(f32[64,64]{1,0:T(8,128)S(1)} %copy-done, s32[1024]{0:T(1024)S(1)} %fusion.89), kind=kCustom, calls=%fused_computation.1 | custom fusion | bytes 528384 | tf_op jit(solution)/shard_map/jit(_take)/gather | solution.py:36
  49.1 0.3 copy.33
  49.5 0.3 copy.34
  49.8 0.6 reduce_sum.84
  51.7 13.8 %fusion.8 = (f32[256]{0:T(256)S(1)}, f32[8,1024,256]{2,1,0:T(8,128)}) fusion(f32[8,1024]{1,0:T(8,128)S(1)} %get-tuple-element.35, f32[8,1024]{1,0:T(8,128)S(1)} %get-tuple-element.52, f32[8,1024]{1,0:T(8,128)S(1)} %get-tuple-element.29, bf16[256,8,64]{0,2,1:T(8,128)(2,1)S(1)} %copy.35, bf16[24,64,1024]{2,1,0:T(8,128)(2,1)} %param.8, f32[64,1024]{1,0:T(8,128)S(1)} %copy.19), kind=kOutput, calls=%fused_computation.16 | convolution fusion | flops 308805376 | bytes 12157952 | tf_op jit(solution)/shard_map/shp,hpz->hsz/dot_general | solution.py:48
  65.5 13.3 %fusion.2 = (f32[256]{0:T(256)S(1)}, f32[8,1024,256]{2,1,0:T(8,128)}) fusion(f32[8,1024]{1,0:T(8,128)S(1)} %get-tuple-element.36, f32[8,1024]{1,0:T(8,128)S(1)} %get-tuple-element.51, f32[8,1024]{1,0:T(8,128)S(1)} %get-tuple-element.30, bf16[256,8,64]{0,2,1:T(8,128)(2,1)S(1)} %copy.33, bf16[24,64,1024]{2,1,0:T(8,128)(2,1)S(1)} %copy-done.5, ...), kind=kOutput, calls=%fused_computation.10 | convolution fusion | flops 308805376 | bytes 12157952 | tf_op jit(solution)/shard_map/shp,hpz->hsz/dot_general | solution.py:48
  78.8 13.2 %fusion.5 = (f32[256]{0:T(256)S(1)}, f32[8,1024,256]{2,1,0:T(8,128)}) fusion(f32[8,1024]{1,0:T(8,128)S(1)} %get-tuple-element.34, f32[8,1024]{1,0:T(8,128)S(1)} %get-tuple-element.53, f32[8,1024]{1,0:T(8,128)S(1)} %get-tuple-element.28, bf16[256,8,64]{0,2,1:T(8,128)(2,1)S(1)} %copy.34, bf16[24,64,1024]{2,1,0:T(8,128)(2,1)S(1)} %copy-done.5, ...), kind=kOutput, calls=%fused_computation.13 | convolution fusion | flops 308805376 | bytes 12157952 | tf_op jit(solution)/shard_map/shp,hpz->hsz/dot_general | solution.py:48
  92.0 16.5 %all-reduce.3 = (f32[256]{0:T(256)S(1)}, f32[]{:T(128)}) all-reduce(f32[256]{0:T(256)S(1)} %add_add_fusion, f32[]{:T(128)S(6)} %mul.142), channel_id=1, replica_groups=mesh['groups'=2,'zone'=4,'scen'=2,'hour'=2] {'zone','hour'}, use_global_device_ids=true, to_apply=%region_3.4 | all-reduce | flops 257 | bytes 2056 | tf_op jit(solution)/shard_map/psum | solution.py:69
  108.5 1.2 fusion.94
  109.8 1.3 exponential_reduce_fusion
  111.0 0.6 dynamic-slice
  111.6 1.3 dynamic-update-slice.1
  112.9 1.3 dynamic-update-slice
  114.2 5.1 %all-reduce.4 = (f32[2]{0:T(128)S(1)}, f32[2]{0:T(128)S(1)}) all-reduce(f32[2]{0:T(128)S(1)} %dynamic-update-slice.1, f32[2]{0:T(128)S(1)} %dynamic-update-slice), channel_id=1, replica_groups=mesh['groups'=2,'zone'=4,'scen'=2,'hour'=2] {'scen'}, use_global_device_ids=true, to_apply=%add.1 | all-reduce | flops 4 | bytes 32
  119.3 0.6 fusion.100
  122.5 0.6 fusion.99
  125.1 8.3 %fusion.72 = f32[64,1024]{1,0:T(8,128)S(1)} fusion(bf16[256,8,64]{0,2,1:T(8,128)(2,1)S(1)} %copy.35, f32[8,1024,256]{2,1,0:T(8,128)} %get-tuple-element.44, f32[256]{0:T(256)S(1)} %exponential_divide_fusion, f32[8,1024]{1,0:T(8,128)S(1)} %get-tuple-element.35, f32[8,1024]{1,0:T(8,128)S(1)} %get-tuple-element.52, f32[8,1024]{1,0:T(8,128)S(1)} %get-tuple-element.29, ...), kind=kOutput, calls=%fused_computation.97 | convolution fusion | flops 295108608 | bytes 10060800 | tf_op jit(solution)/shard_map/shp,hsz->hpz/dot_general | solution.py:91
  133.5 6.3 %fusion.74 = f32[64,1024]{1,0:T(8,128)S(1)} fusion(bf16[256,8,64]{0,2,1:T(8,128)(2,1)S(1)} %copy.33, f32[8,1024,256]{2,1,0:T(8,128)S(1)} %copy-done.9, f32[256]{0:T(256)S(1)} %exponential_divide_fusion, f32[8,1024]{1,0:T(8,128)S(1)} %get-tuple-element.36, f32[8,1024]{1,0:T(8,128)S(1)} %get-tuple-element.51, f32[8,1024]{1,0:T(8,128)S(1)} %get-tuple-element.30, ...), kind=kOutput, calls=%fused_computation.101 | convolution fusion | flops 295108608 | bytes 10060800 | tf_op jit(solution)/shard_map/shp,hsz->hpz/dot_general | solution.py:91
  139.9 6.3 %fusion.73 = f32[64,1024]{1,0:T(8,128)S(1)} fusion(bf16[256,8,64]{0,2,1:T(8,128)(2,1)S(1)} %copy.34, f32[8,1024,256]{2,1,0:T(8,128)S(1)} %bitcast.233, f32[256]{0:T(256)S(1)} %exponential_divide_fusion, f32[8,1024]{1,0:T(8,128)S(1)} %get-tuple-element.34, f32[8,1024]{1,0:T(8,128)S(1)} %get-tuple-element.53, f32[8,1024]{1,0:T(8,128)S(1)} %get-tuple-element.28, ...), kind=kOutput, calls=%fused_computation.99 | convolution fusion | flops 295108608 | bytes 10060800 | tf_op jit(solution)/shard_map/shp,hsz->hpz/dot_general | solution.py:91
  146.2 0.6 convolution_multiply_fusion
  146.8 57.6 %all-reduce.2 = f32[64,64]{1,0:T(8,128)S(1)} all-reduce(f32[64,64]{1,0:T(8,128)S(1)} %convolution_multiply_fusion), channel_id=2, replica_groups=mesh['groups'=2,'zone'=4,'scen'=2,'hour'=2] {'zone','scen','hour'}, use_global_device_ids=true, to_apply=%region_12.13.clone | all-reduce | flops 4096 | bytes 32768
  204.4 0.6 dynamic-slice.2
  205.7 0.6 constant_dynamic-slice_fusion
  (40 shorter events, 1.0 us)
Async XLA Ops:
  0.6 45.3 %copy-start = (f32[64,64]{1,0:T(8,128)S(1)}, f32[64,64]{1,0:T(8,128)}, u32[]{:S(2)}) copy-start(f32[64,64]{1,0:T(8,128)} %param.9) | copy-start | bytes 49156
  0.6 40.5 %copy-start.3 = (f32[1024]{0:T(1024)S(1)}, f32[1024]{0:T(1024)}, u32[]{:S(2)}) copy-start(f32[1024]{0:T(1024)} %param.13) | copy-start | bytes 12292
  0.7 40.6 %copy-start.2 = (s32[24,1024]{1,0:T(8,128)S(1)}, s32[24,1024]{1,0:T(8,128)}, u32[]{:S(2)}) copy-start(s32[24,1024]{1,0:T(8,128)} %param.12) | copy-start | bytes 294916
  0.7 40.6 %copy-start.4 = (s32[1024]{0:T(1024)S(1)}, s32[1024]{0:T(1024)}, u32[]{:S(2)}) copy-start(s32[1024]{0:T(1024)} %param.10) | copy-start | bytes 12292
  0.7 40.7 %copy-start.1 = (s32[1024]{0:T(1024)S(1)}, s32[1024]{0:T(1024)}, u32[]{:S(2)}) copy-start(s32[1024]{0:T(1024)} %param.11) | copy-start | bytes 12292
  2.9 4.9 %all-to-all-start = ((bf16[2,2,24576]{2,1,0:T(2,128)(2,1)}), bf16[2,2,24576]{2,1,0:T(2,128)(2,1)S(1)}, u32[]{:S(2)}, u32[]{:S(2)}) async-start(bf16[2,2,24576]{2,1,0:T(2,128)(2,1)} %reshape.77), calls=%async_computation | async-start | bytes 393216 | tf_op jit(solution)/shard_map/all_to_all | solution.py:42
  51.7 13.8 %copy-start.5 = (bf16[24,64,1024]{2,1,0:T(8,128)(2,1)S(1)}, bf16[24,64,1024]{2,1,0:T(8,128)(2,1)}, u32[]{:S(2)}) copy-start(bf16[24,64,1024]{2,1,0:T(8,128)(2,1)} %param.8) | copy-start | bytes 9437188
  78.8 32.3 %copy-start.8 = (u32[32]{0:T(128)S(1)}, u32[32]{0:T(128)}, u32[]{:S(2)}) copy-start(u32[32]{0:T(128)} %constant.81) | copy-start | bytes 388
  125.1 8.4 %copy-start.6 = (bf16[24,64,1024]{2,1,0:T(8,128)(2,1)S(1)}, bf16[24,64,1024]{2,1,0:T(8,128)(2,1)}, u32[]{:S(2)}) copy-start(bf16[24,64,1024]{2,1,0:T(8,128)(2,1)} %param.8) | copy-start | bytes 9437188
  125.1 8.3 %copy-start.9 = (f32[8,1024,256]{2,1,0:T(8,128)S(1)}, f32[8,1024,256]{2,1,0:T(8,128)}, u32[]{:S(2)}) copy-start(f32[8,1024,256]{2,1,0:T(8,128)} %get-tuple-element.46) | copy-start | bytes 25165828
  125.1 14.7 %slice-start = ((s8[8388608]{0:T(1024)(128)(4,1)}), s8[4194304]{0:T(1024)(128)(4,1)S(1)}, s32[]{:S(2)}) async-start(s8[8388608]{0:T(1024)(128)(4,1)} %bitcast.232), calls=%async_computation.1 | async-start | bytes 8388608
  133.5 6.4 %slice-start.1 = ((s8[8388608]{0:T(1024)(128)(4,1)}), s8[4194304]{0:T(1024)(128)(4,1)S(1)}, s32[]{:S(2)}) async-start(s8[8388608]{0:T(1024)(128)(4,1)} %bitcast.232), calls=%async_computation.2 | async-start | bytes 8388608
  139.9 64.6 %copy-start.7 = (u32[32]{0:T(128)S(1)}, u32[32]{0:T(128)}, u32[]{:S(2)}) copy-start(u32[32]{0:T(128)} %constant.93) | copy-start | bytes 388
where the time goes:
time: 208 us; the launch traced here: 207 us
  blocking collectives  111 us (53%)
  matrix products  61.8 us (30%)
  local copies, waits for them, and re-layouts  17 us (8%)
  between operations  8.65 us (4%)
  other arithmetic  4.05 us (2%)
  starting transfers between devices  3.43 us (2%)
    unnamed x2, blocking collectives  62.7 us
    dot_general x3, matrix products, inside_climate_state(): jnp.einsum('shp,hpz->hsz', record_elements, coeff[initial_clock_time:init...  40.3 us
    all_gather x1, blocking collectives, on_device(): outlook_records = lax.all_gather(mine, 'zone', axis=0, tiled=True)  31.7 us
    dot_general x3, matrix products, on_device(): jnp.einsum('shp,hsz->hpz', record_elements, adjoint, preferred_element_ty...  20.9 us
    psum x1, blocking collectives, on_device(): loss_sum, weight_total = lax.psum((sums, weight_part), ('zone', 'hour'))  16.5 us
    unnamed x37, local copies, waits for them, and re-layouts  7.84 us
    gather x1, local copies, waits for them, and re-layouts, on_device(): candidate_plan = jnp.take(owner_ids, building_map)  4.53 us
  transfers between devices with their start and end apart: 1, of which 1 were waited for; matrix products, arithmetic and copies ran while one was open for 0% of the time, Pallas kernels for 0%

commit v1 on v0

v1 whole, which is shorter than its diff:
```python
import functools
import math

import jax
import jax.numpy as jnp
from jax import lax
from jax.experimental import pallas as pl
from jax.experimental.pallas import tpu as pltpu
from jax.sharding import PartitionSpec as P

SHARPNESS = 200.0
MINUS_LOG2_E = -1.0 / math.log(2.0)
EDGE = 2.0 * math.cosh(0.5)
LANES = 128
DEPTH = 128
ZONE_TILE = 256
VMEM = pl.BlockSpec(memory_space=pltpu.VMEM)
SMEM = pl.BlockSpec(memory_space=pltpu.SMEM)
F32 = jnp.float32
BF16 = jnp.bfloat16


def params(**kw):
    return pltpu.CompilerParams(vmem_limit_bytes=56 * 2**20, **kw)


def coeff_kernel(map_ref, owner_ref, wp_ref, band_ref, resp_ref, rhs_ref, plan_ref, zp_ref):
    width = wp_ref.shape[1]
    zones = resp_ref.shape[2]

    @pl.when(pl.program_id(0) == 0)
    def _():
        place = map_ref[...]
        row, lane = place // LANES, place % LANES

        def look(i, found):
            table = jnp.broadcast_to(owner_ref[pl.ds(i, 1), :], place.shape)
            here = jnp.take_along_axis(table, lane, axis=1, mode="promise_in_bounds")
            return jnp.where(row == i, here, found)

        plan = lax.fori_loop(0, owner_ref.shape[0], look, jnp.zeros_like(place))
        for r in range(plan.shape[0]):
            plan_ref[:, r * LANES : (r + 1) * LANES] = plan[r : r + 1, :]
        designs = wp_ref.shape[0]
        onehot = (
            lax.broadcasted_iota(jnp.int32, (designs, zones), 0) == plan_ref[...]
        ).astype(F32).astype(BF16)
        rest = wp_ref[...]
        total = jnp.zeros((width, zones), F32)
        for _ in range(3):
            part = rest.astype(BF16)
            rest = rest - part.astype(F32)
            total = total + lax.dot_general(
                part, onehot, (((0,), (0,)), ((), ())), preferred_element_type=F32
            )
        zp_ref[...] = total

    extra = lax.broadcasted_iota(jnp.int32, (DEPTH - width, zones), 0)
    for h in range(resp_ref.shape[0]):
        rhs_ref[h, :width, :] = (resp_ref[h].astype(F32) * zp_ref[...]).astype(BF16)
        middle = 0.25 * (band_ref[h].astype(F32) - 3.5)
        tail = jnp.where(extra == 0, -middle, jnp.where(extra == 1, 1.0, 0.0))
        rhs_ref[h, width:, :] = tail.astype(BF16)


def coefficients(building_map, owner_ids, window_params, band_ids, response):
    hours, width, zones = response.shape
    step = 6
    return pl.pallas_call(
        coeff_kernel,
        grid=(hours // step,),
        in_specs=[
            VMEM,
            VMEM,
            VMEM,
            pl.BlockSpec((step, 1, zones), lambda i: (i, 0, 0)),
            pl.BlockSpec((step, width, zones), lambda i: (i, 0, 0)),
        ],
        out_specs=[
            pl.BlockSpec((step, DEPTH, zones), lambda i: (i, 0, 0)),
            pl.BlockSpec((1, zones), lambda i: (0, 0)),
        ],
        out_shape=[
            jax.ShapeDtypeStruct((hours, DEPTH, zones), BF16),
            jax.ShapeDtypeStruct((1, zones), jnp.int32),
        ],
        scratch_shapes=[pltpu.VMEM((width, zones), F32)],
        compiler_params=params(),
        name="coefficients",
    )(
        building_map.reshape(-1, LANES),
        owner_ids.reshape(-1, LANES),
        window_params,
        band_ids.reshape(hours, 1, zones),
        response,
    )


def drivers(pair, second, fill):
    half = pair.shape[1] // 2
    lane = lax.broadcasted_iota(jnp.int32, pair.shape, 1)
    if second:
        pair = pltpu.roll(pair.astype(F32), half, 1).astype(BF16)
    rest = jnp.zeros(pair.shape, F32)
    for spot, value in enumerate(fill):
        rest = jnp.where(lane == half + spot, value, rest)
    return jnp.where(lane < half, pair, rest.astype(BF16))


def occupancy(hour, hours_total):
    return 1.0 + 2.0 * hour.astype(F32) / (hours_total - 1)


def loss_kernel(hours_total, last, core_ref, f_ref, rhs_ref, area_ref, *rest):
    if last:
        prior_ref, out_ref, acc_ref = rest
    else:
        out_ref, acc_ref = rest
    step = pl.program_id(0)
    hours_step = rhs_ref.shape[0]
    zones = rhs_ref.shape[2]
    hours_local = hours_step * pl.num_programs(0)
    core = core_ref[0]

    @pl.when(step == 0)
    def _():
        acc_ref[...] = jnp.zeros_like(acc_ref)

    def pair_step(j, carry):
        pair = f_ref[:, pl.ds(pl.multiple_of(j * LANES, LANES), LANES)]
        for k in range(2):
            h = 2 * j + k
            lhs = drivers(pair, k == 1, (1.0,))
            occ = occupancy(core * hours_local + step * hours_step + h, hours_total)
            for z in range(0, zones, ZONE_TILE):
                v = jnp.dot(lhs, rhs_ref[h, :, z : z + ZONE_TILE], preferred_element_type=F32)
                a = jnp.abs(v) * MINUS_LOG2_E
                q = jnp.exp2(a)
                pen = jnp.log2((q + EDGE) * q + 1.0) - a
                pen = pen * (area_ref[:, z : z + ZONE_TILE] * occ)
                part = pen[:, :LANES]
                for c in range(LANES, ZONE_TILE, LANES):
                    part = part + pen[:, c : c + LANES]
                acc_ref[...] += part
        return carry

    lax.fori_loop(0, hours_step // 2, pair_step, 0)

    @pl.when(step == pl.num_programs(0) - 1)
    def _():
        row = jnp.sum(acc_ref[...].T, axis=0, keepdims=True)
        if not last:
            out_ref[...] = jnp.broadcast_to(row, out_ref.shape)
        else:
            index = lax.broadcasted_iota(jnp.int32, out_ref.shape[1:], 0)
            first_hour = core * hours_local
            occ_sum = hours_local * 1.0 + (
                2.0 * (first_hour * hours_local + hours_local * (hours_local - 1) // 2)
            ).astype(F32) / (hours_total - 1)
            weight = jnp.sum(area_ref[...]) * occ_sum
            message = jnp.where(
                index == core,
                prior_ref[0:1, :],
                jnp.where(index == 1 - core, row, jnp.where(index == 2, weight, 0.0)),
            )
            for d in range(out_ref.shape[0]):
                out_ref[d] = message


def losses(core, f, offset, rhs, area, hours_total, prior=None, copies=0):
    hours, _, zones = rhs.shape
    step = 6
    rows = f.shape[0]
    last = prior is not None
    if last:
        out_shape = jax.ShapeDtypeStruct((copies, 8, rows), F32)
        out_spec = pl.BlockSpec((copies, 8, rows), lambda i, *_: (0, 0, 0))
    else:
        out_shape = jax.ShapeDtypeStruct((8, rows), F32)
        out_spec = pl.BlockSpec((8, rows), lambda i, *_: (0, 0))
    steps = hours // step
    return pl.pallas_call(
        functools.partial(loss_kernel, hours_total, last),
        grid_spec=pltpu.PrefetchScalarGridSpec(
            num_scalar_prefetch=1,
            grid=(steps,),
            in_specs=[
                pl.BlockSpec((rows, step * 64), lambda i, c: (0, c[0] * steps * offset + i)),
                pl.BlockSpec((step, DEPTH, zones), lambda i, c: (i, 0, 0)),
                pl.BlockSpec((1, zones), lambda i, c: (0, 0)),
            ]
            + ([pl.BlockSpec((8, rows), lambda i, c: (0, 0))] if last else []),
            out_specs=out_spec,
            scratch_shapes=[pltpu.VMEM((rows, LANES), F32)],
        ),
        out_shape=out_shape,
        compiler_params=params(),
        name="losses",
    )(core, f, rhs, area, *((prior,) if last else ()))


def slope_kernel(core_ref, f0_ref, f1_ref, rhs_ref, slope_ref, ft_ref):
    zones = rhs_ref.shape[2]
    rows = f0_ref.shape[0]
    for j in range(rhs_ref.shape[0] // 2):
        for b, f_ref in enumerate((f0_ref, f1_ref)):
            pair = f_ref[:, j * LANES : (j + 1) * LANES]
            ft_ref[j * LANES : (j + 1) * LANES, b * rows : (b + 1) * rows] = pair.T

    def pair_step(j, carry):
        at = pl.ds(pl.multiple_of(j * LANES, LANES), LANES)
        pair = jnp.concatenate([f0_ref[:, at], f1_ref[:, at]], axis=0)
        for k in range(2):
            h = 2 * j + k
            lhs = drivers((pair.astype(F32) * 0.5).astype(BF16), k == 1, (0.5, 0.25))
            for z in range(0, zones, ZONE_TILE):
                v = jnp.dot(lhs, rhs_ref[h, :, z : z + ZONE_TILE], preferred_element_type=F32)
                slope = jnp.tanh(v) + jnp.tanh(v - 0.5)
                slope_ref[h, :, z : z + ZONE_TILE] = slope.astype(BF16)
        return carry

    lax.fori_loop(0, rhs_ref.shape[0] // 2, pair_step, 0)


def slopes(core, straight, crossed, rhs):
    hours, _, zones = rhs.shape
    step = 4
    steps = hours // step
    rows = straight.shape[0]
    return pl.pallas_call(
        slope_kernel,
        grid_spec=pltpu.PrefetchScalarGridSpec(
            num_scalar_prefetch=1,
            grid=(steps,),
            in_specs=[
                pl.BlockSpec((rows, step * 64), lambda i, c: (0, c[0] * steps + i)),
                pl.BlockSpec((rows, step * 64), lambda i, c: (0, i)),
                pl.BlockSpec((step, DEPTH, zones), lambda i, c: (i, 0, 0)),
            ],
            out_specs=[
                pl.BlockSpec((step, 2 * rows, zones), lambda i, c: (i, 0, 0)),
                pl.BlockSpec((step * 64, 2 * rows), lambda i, c: (i, 0)),
            ],
        ),
        out_shape=[
            jax.ShapeDtypeStruct((hours, 2 * rows, zones), BF16),
            jax.ShapeDtypeStruct((hours * 64, 2 * rows), BF16),
        ],
        compiler_params=params(),
        name="slopes",
    )(core, straight, crossed, rhs)


def gradient_kernel(
    hours_total, gain, owners, core_ref, msg_ref, ft_ref, slope_ref, resp_ref, area_ref, plan_ref,
    out_ref, acc_ref, e_ref, scale_ref,
):
    step = pl.program_id(0)
    hours_step, width, zones = resp_ref.shape
    hours_local = hours_step * pl.num_programs(0)
    core = core_ref[0]

    @pl.when(step == 0)
    def _():
        acc_ref[...] = jnp.zeros_like(acc_ref)
        total = jnp.sum(msg_ref[...], axis=0)
        weight = jnp.max(total[2:3, :])
        score = total[0:2, :] * (SHARPNESS * math.log(2.0) / weight)
        peak = jnp.max(score)
        e = jnp.exp(score - peak)
        rows = e.shape[1]
        e_ref[:, :rows] = jnp.where(core == 0, e[0:1, :], e[1:2, :])
        e_ref[:, rows:] = jnp.where(core == 0, e[1:2, :], e[0:1, :])
        scale_ref[0] = peak
        scale_ref[1] = jnp.sum(e)
        scale_ref[2] = weight

    def hour_step(h, carry):
        occ = occupancy(core * hours_local + step * hours_step + h, hours_total)
        ft = ft_ref[pl.ds(pl.multiple_of(h * width, width), width), :].astype(F32)
        ft = ft * (e_ref[...] * occ)
        high = ft.astype(BF16)
        low = (ft - high.astype(F32)).astype(BF16)
        both = jnp.concatenate([high, low], axis=0)
        for z in range(0, zones, ZONE_TILE):
            at = slice(z, z + ZONE_TILE)
            mixed = jnp.dot(both, slope_ref[h, :, at], preferred_element_type=F32)
            mixed = mixed[:width] + mixed[width:]
            acc_ref[:, at] += resp_ref[h, :, at].astype(F32) * mixed
        return carry

    lax.fori_loop(0, hours_step, hour_step, 0)

    @pl.when(step == pl.num_programs(0) - 1)
    def _():
        grad = acc_ref[...] * area_ref[...]
        blocks = out_ref.shape[0]
        pad = out_ref.shape[1]
        index = lax.broadcasted_iota(jnp.int32, (blocks * pad, zones), 0)
        within = index % pad
        design = jnp.where(within < owners, (index // pad) * owners + within, -1)
        onehot = (design == plan_ref[...]).astype(F32)
        sens = lax.dot_general(
            onehot,
            grad,
            (((1,), (1,)), ((), ())),
            precision=lax.Precision.HIGHEST,
            preferred_element_type=F32,
        )
        sens = sens * (0.5 * gain / scale_ref[2])
        out_ref[:, :, :width] = sens.reshape(blocks, pad, width)
        lane = lax.broadcasted_iota(jnp.int32, (blocks, pad, LANES - width), 2)
        out_ref[:, :, width:] = jnp.where(lane == 0, scale_ref[0], scale_ref[1])


def gradient(core, msg, ft, slope, response, area, plan, hours_total, gain, devices, owners):
    hours, width, zones = response.shape
    step = 4
    scen = slope.shape[1]
    pad = -(-owners // 8) * 8
    return pl.pallas_call(
        functools.partial(gradient_kernel, hours_total, gain, owners),
        grid_spec=pltpu.PrefetchScalarGridSpec(
            num_scalar_prefetch=1,
            grid=(hours // step,),
            in_specs=[
                pl.BlockSpec(msg.shape, lambda i, c: (0, 0, 0)),
                pl.BlockSpec((step * width, scen), lambda i, c: (i, 0)),
                pl.BlockSpec((step, scen, zones), lambda i, c: (i, 0, 0)),
                pl.BlockSpec((step, width, zones), lambda i, c: (i, 0, 0)),
                pl.BlockSpec((1, zones), lambda i, c: (0, 0)),
                pl.BlockSpec((1, zones), lambda i, c: (0, 0)),
            ],
            out_specs=pl.BlockSpec((devices, pad, LANES), lambda i, c: (0, 0, 0)),
            scratch_shapes=[
                pltpu.VMEM((width, zones), F32),
                pltpu.VMEM((1, scen), F32),
                pltpu.SMEM((4,), F32),
            ],
        ),
        out_shape=jax.ShapeDtypeStruct((devices, pad, LANES), F32),
        compiler_params=params(),
        name="gradient",
    )(core, msg, ft, slope, response, area, plan)


def finish_kernel(scen_parts, width, parts_ref, sens_ref, objective_ref):
    parts = parts_ref[...]
    devices = parts.shape[0]
    peaks = parts[:, :, width : width + 1]
    totals = parts[:, :, width + 1 : width + 2]
    peak = jnp.max(peaks)
    scale = jnp.exp(peaks - peak)
    total = jnp.sum((scale * totals)[:, 0:1, :]) * (scen_parts / devices)
    summed = jnp.sum(parts[:, :, :width] * scale, axis=0) / total
    sens_ref[...] = summed[: sens_ref.shape[0]]
    log_total = jnp.max(jnp.log(jnp.full((8, LANES), total, F32)))
    objective_ref[0] = (peak + log_total) / SHARPNESS - 0.5


def on_device(forcing, response, window_params, building_map, owner_ids, band_ids, floor_area):
    hours, width, zones = response.shape
    hour_parts = lax.axis_size("hour")
    zone_parts = lax.axis_size("zone")
    scen_parts = lax.axis_size("scen")
    hours_total = hours * hour_parts
    core = lax.axis_index("hour").astype(jnp.int32).reshape(1)
    area = floor_area.reshape(1, zones)

    everyone = forcing.reshape(forcing.shape[0], hours_total * width)
    gathered = lax.all_gather(everyone, "zone", axis=0, tiled=True)
    half = hours * width
    leaving = lax.dynamic_slice_in_dim(gathered, (1 - core[0]) * half, half, axis=1)
    crossed = lax.ppermute(leaving, "hour", [(0, 1), (1, 0)])

    rhs, plan = coefficients(building_map, owner_ids, window_params, band_ids, response)
    first = losses(core, gathered, 1, rhs, area, hours_total)
    message = losses(
        core, crossed, 0, rhs, area, hours_total, prior=first, copies=zone_parts * hour_parts
    )
    slope, ft = slopes(core, gathered, crossed, rhs)
    shared = lax.all_to_all(message, ("zone", "hour"), split_axis=0, concat_axis=0, tiled=True)

    designs = window_params.shape[0]
    devices = zone_parts * scen_parts * hour_parts
    owners = designs // devices
    gain = math.sqrt(width * zones * zone_parts * hours_total * designs)
    parts = gradient(
        core, shared, ft, slope, response, area, plan, hours_total, gain, devices, owners
    )
    parts = lax.all_to_all(
        parts, ("zone", "scen", "hour"), split_axis=0, concat_axis=0, tiled=True
    )
    sensitivity, objective = pl.pallas_call(
        functools.partial(finish_kernel, scen_parts, width),
        in_specs=[VMEM],
        out_specs=[VMEM, SMEM],
        out_shape=[
            jax.ShapeDtypeStruct((owners, width), F32),
            jax.ShapeDtypeStruct((1,), F32),
        ],
        compiler_params=params(),
        name="finish",
    )(parts)
    return (sensitivity, objective)


def solution(mesh):
    in_specs = (
        P(("groups", "zone", "scen", "hour"), None, None),
        P("hour", None, ("groups", "zone")),
        P("groups", None),
        P(("groups", "zone")),
        P("groups"),
        P("hour", ("groups", "zone")),
        P(("groups", "zone")),
    )
    out_specs = (P(("groups", "zone", "scen", "hour"), None), P("groups"))
    return jax.shard_map(
        on_device, mesh=mesh, in_specs=in_specs, out_specs=out_specs, check_vma=False
    )
```

time: 208 us -> 93 us (0.45)
  blocking collectives: 111 us -> 34.3 us
  matrix products: 61.8 us -> 0 us
  Pallas kernels: 0 us -> 49.4 us
  local copies, waits for them, and re-layouts: 17 us -> 4.42 us
  between operations: 8.65 us -> 0.67 us
  other arithmetic: 4.05 us -> 0 us
    unnamed x2 -> x0, blocking collectives: 62.7 us -> none
    dot_general x7 -> x0, matrix products: 61.8 us -> none  [the longest x3 40.3 us: inside_climate_state(): jnp.einsum('shp,hpz->hsz', record_elements, coeff[initial_clock_time:init...]
    pallas_call x0 -> x6, Pallas kernels: none -> 49.4 us  [the longest x2 16.9 us: losses(): pl.pallas_call(functools.partial(loss_kernel, hours_total, last), grid_sp...]
    psum x1 -> x0, blocking collectives: 16.5 us -> none  [on_device(): loss_sum, weight_total = lax.psum((sums, weight_part), ('zone', 'hour'))]
    all_to_all x0 -> x1, blocking collectives: none -> 13 us  [on_device(): lax.all_to_all(parts, ('zone', 'scen', 'hour'), split_axis=0, concat_axis...]
    all_gather x1, blocking collectives: 31.7 us -> 21.3 us  [on_device(): gathered = lax.all_gather(everyone, 'zone', axis=0, tiled=True)]
    gather x2 -> x0, local copies, waits for them, and re-layouts: 7.34 us -> none  [the longest x1 4.53 us: on_device(): candidate_plan = jnp.take(owner_ids, building_map)]
    unnamed x37 -> x6, local copies, waits for them, and re-layouts: 7.84 us -> 1.37 us
  transfers between devices with their start and end apart: 1 -> 2, of which waited for: 1 -> 0; matrix products, arithmetic and copies ran while one was open for 0% -> 2% of each run, Pallas kernels for 0% -> 30%
where the time goes in v1:
time: 93 us; the launch traced here: 92.2 us
  Pallas kernels  49.4 us (53%)
  blocking collectives  34.3 us (37%)
  local copies, waits for them, and re-layouts  4.42 us (5%)
  starting transfers between devices  3.4 us (4%)
    all_gather x1, blocking collectives, on_device(): gathered = lax.all_gather(everyone, 'zone', axis=0, tiled=True)  21.3 us
    pallas_call x2, Pallas kernels, losses(): pl.pallas_call(functools.partial(loss_kernel, hours_total, last), grid_sp...  16.9 us
    pallas_call x1, Pallas kernels, slopes(): pl.pallas_call(slope_kernel, grid_spec=pltpu.PrefetchScalarGridSpec(num_s...  13.1 us
    all_to_all x1, blocking collectives, on_device(): lax.all_to_all(parts, ('zone', 'scen', 'hour'), split_axis=0, concat_axis...  13 us
    pallas_call x1, Pallas kernels, gradient(): pl.pallas_call(functools.partial(gradient_kernel, hours_total, gain, owne...  11.5 us
    pallas_call x1, Pallas kernels, coefficients(): pl.pallas_call(coeff_kernel, grid=(hours // step,), in_specs=[VMEM, VMEM,...  6.16 us
    all_to_all x1, starting transfers between devices, on_device(): lax.all_to_all(message, ('zone', 'hour'), split_axis=0, concat_axis=0, ti...  3.33 us
  transfers between devices with their start and end apart: 2, of which 0 were waited for; matrix products, arithmetic and copies ran while one was open for 2% of the time, Pallas kernels for 30%

profile of v1, /device:TPU:0, one launch (start us, length us, event | category | flops | bytes accessed | tf_op | source)
XLA Modules:
  0.0 92.2 jit_solution(148329270155770066)
XLA Ops:
  0.6 1.3 %reshape.23 = bf16[32,3072]{1,0:T(8,128)(2,1)S(1)} reshape(bf16[32,48,64]{2,1,0:T(8,128)(2,1)} %param.7) | data formatting | bytes 393216 | tf_op jit(solution)/shard_map/reshape | solution.py:370
  2.0 21.3 %all_gather.3.f_ref.f0_ref = bf16[128,3072]{1,0:T(8,128)(2,1)S(1)} all-gather(bf16[32,3072]{1,0:T(8,128)(2,1)S(1)} %reshape.23), channel_id=1, replica_groups=mesh['groups'=2,'zone'=4,'scen'=2,'hour'=2] {'zone'}, dimensions={0}, use_global_device_ids=true | all-gather | bytes 983040 | tf_op jit(solution)/shard_map/all_gather | solution.py:371
  23.2 0.0 copy-start
  23.3 0.1 collective-permute-start
  23.4 1.7 %reshape.26.band_ref = s32[24,1,1024]{2,1,0:T(1,128)} reshape(s32[24,1024]{1,0:T(8,128)} %param.12) | data formatting | bytes 196608 | tf_op jit(solution)/shard_map/reshape | solution.py:94
  25.1 6.2 %coefficients.1 = (bf16[24,128,1024]{2,1,0:T(8,128)(2,1)}, s32[1,1024]{1,0:T(1,128)}) custom-call(s32[8,128]{1,0:T(8,128)} %bitcast.7, s32[8,128]{1,0:T(8,128)} %bitcast.8, f32[64,64]{1,0:T(8,128)} %wp_ref.1, s32[24,1,1024]{2,1,0:T(1,128)} %reshape.26.band_ref, bf16[24,64,1024]{2,1,0:T(8,128)(2,1)} %resp_ref.3), custom_call_target="tpu_custom_call" | custom-call | tf_op jit(solution)/shard_map/coefficients/pallas_call | solution.py:69
  31.2 0.0 copy-done
  31.2 8.4 %losses.2.rest_0_ = f32[8,128]{1,0:T(8,128)} custom-call(s32[1]{0:T(128)} %bitcast.core_ref, bf16[128,3072]{1,0:T(8,128)(2,1)} %copy-done, bf16[24,128,1024]{2,1,0:T(8,128)(2,1)} %get-tuple-element.6.rhs_ref, f32[1,1024]{1,0:T(1,128)} %bitcast.4), custom_call_target="tpu_custom_call" | custom-call | tf_op jit(solution)/shard_map/losses/pallas_call | solution.py:182
  39.7 0.0 collective-permute-done.f_ref.f1_ref
  39.7 0.0 copy-start.1
  39.7 0.8 copy-done.1
  40.4 8.5 %losses.3 = f32[8,8,128]{2,1,0:T(8,128)} custom-call(s32[1]{0:T(128)} %bitcast.core_ref, bf16[128,1536]{1,0:T(8,128)(2,1)} %copy-done.1, bf16[24,128,1024]{2,1,0:T(8,128)(2,1)} %get-tuple-element.6.rhs_ref, f32[1,1024]{1,0:T(1,128)} %bitcast.5, f32[8,128]{1,0:T(8,128)} %losses.2.rest_0_), custom_call_target="tpu_custom_call" | custom-call | tf_op jit(solution)/shard_map/losses/pallas_call | solution.py:182
  48.9 3.3 %all-to-all-start = ((f32[8,8,128]{2,1,0:T(8,128)}), f32[8,8,128]{2,1,0:T(8,128)S(1)}, u32[]{:S(2)}, u32[]{:S(2)}) async-start(f32[8,8,128]{2,1,0:T(8,128)} %losses.3), calls=%async_computation | async-start | bytes 65536 | tf_op jit(solution)/shard_map/all_to_all | solution.py:382
  52.2 13.1 %slopes.1 = (bf16[24,256,1024]{2,1,0:T(8,128)(2,1)}, bf16[1536,256]{1,0:T(8,128)(2,1)}) custom-call(s32[1]{0:T(128)} %bitcast.core_ref, bf16[128,3072]{1,0:T(8,128)(2,1)} %copy-done, bf16[128,1536]{1,0:T(8,128)(2,1)} %copy-done.1, bf16[24,128,1024]{2,1,0:T(8,128)(2,1)} %get-tuple-element.6.rhs_ref), custom_call_target="tpu_custom_call" | custom-call | tf_op jit(solution)/shard_map/slopes/pallas_call | solution.py:230
  65.3 0.0 all-to-all-done.msg_ref
  65.3 0.0 copy-start.2
  65.3 0.6 copy-done.2
  65.9 11.5 %gradient.1 = f32[16,8,128]{2,1,0:T(8,128)} custom-call(s32[1]{0:T(128)} %bitcast.core_ref, f32[8,8,128]{2,1,0:T(8,128)} %copy-done.2, bf16[1536,256]{1,0:T(8,128)(2,1)} %get-tuple-element.7.ft_ref, bf16[24,256,1024]{2,1,0:T(8,128)(2,1)} %get-tuple-element.8.slope_ref, bf16[24,64,1024]{2,1,0:T(8,128)(2,1)} %resp_ref.3, f32[1,1024]{1,0:T(1,128)} %bitcast.6, ...), custom_call_target="tpu_custom_call" | custom-call | tf_op jit(solution)/shard_map/gradient/pallas_call | solution.py:321
  77.4 13.0 %all_to_all.10.parts_ref = f32[16,8,128]{2,1,0:T(8,128)} all-to-all(f32[16,8,128]{2,1,0:T(8,128)} %gradient.1), channel_id=1, replica_groups=mesh['groups'=2,'zone'=4,'scen'=2,'hour'=2] {'zone','scen','hour'}, dimensions={0} | all-to-all | bytes 131072 | tf_op jit(solution)/shard_map/all_to_all | solution.py:391
  90.4 1.8 %finish.1 = (f32[4,64]{1,0:T(4,128)}, f32[1]{0:T(128)}) custom-call(f32[16,8,128]{2,1,0:T(8,128)} %all_to_all.10.parts_ref), custom_call_target="tpu_custom_call" | custom-call | tf_op jit(solution)/shard_map/finish/pallas_call | solution.py:394
  (1 shorter events, 0.0 us)
Async XLA Ops:
  23.2 8.0 %copy-start = (bf16[128,3072]{1,0:T(8,128)(2,1)}, bf16[128,3072]{1,0:T(8,128)(2,1)S(1)}, u32[]{:S(2)}) copy-start(bf16[128,3072]{1,0:T(8,128)(2,1)S(1)} %all_gather.3.f_ref.f0_ref) | copy-start | bytes 2359300
  23.3 16.4 %collective-permute-start = (bf16[128,1536]{1,0:T(8,128)(2,1)S(1)}, bf16[128,1536]{1,0:T(8,128)(2,1)S(1)}, u32[]{:S(2)}, u32[]{:S(2)}) collective-permute-start(bf16[128,1536]{1,0:T(8,128)(2,1)S(1)} %constant_dynamic-slice_fusion), channel_id=1, source_target_pairs={{0,1},{1,0},{2,3},{3,2},{4,5},{5,4},{6,7},{7,6},{8,9},{9,8},{10,11... | collective-permute-start | bytes 1179656 | tf_op jit(solution)/shard_map/ppermute | solution.py:374
  39.7 0.8 copy-start.1
  48.9 16.4 %all-to-all-start = ((f32[8,8,128]{2,1,0:T(8,128)}), f32[8,8,128]{2,1,0:T(8,128)S(1)}, u32[]{:S(2)}, u32[]{:S(2)}) async-start(f32[8,8,128]{2,1,0:T(8,128)} %losses.3), calls=%async_computation | async-start | bytes 65536 | tf_op jit(solution)/shard_map/all_to_all | solution.py:382
  65.3 0.6 copy-start.2

commit v2 on v0

v2 whole, which is shorter than its diff:
```python
import functools
import math

import jax
import jax.numpy as jnp
from jax import lax
from jax.experimental import pallas as pl
from jax.experimental.pallas import tpu as pltpu
from jax.sharding import PartitionSpec as P

SHARPNESS = 200.0
MINUS_LOG2_E = -1.0 / math.log(2.0)
EDGE = 2.0 * math.cosh(0.5)
LANES = 128
DEPTH = 128
ZONE_TILE = 256
VMEM = pl.BlockSpec(memory_space=pltpu.VMEM)
SMEM = pl.BlockSpec(memory_space=pltpu.SMEM)
F32 = jnp.float32
BF16 = jnp.bfloat16


def params():
    return pltpu.CompilerParams(vmem_limit_bytes=20 * 2**20)


def near(x):
    return pltpu.with_memory_space_constraint(x, pltpu.VMEM)


def call(kernel, name, outs, args, scratch=()):
    return pl.pallas_call(
        kernel,
        in_specs=[SMEM] + [VMEM] * (len(args) - 1),
        out_specs=[VMEM] * len(outs),
        out_shape=[pltpu.MemorySpace.VMEM(shape, kind) for shape, kind in outs],
        scratch_shapes=list(scratch),
        compiler_params=params(),
        name=name,
    )(args[0], *[near(a) for a in args[1:]])


def coeff_kernel(place_ref, map_ref, owner_ref, wp_ref, band_ref, resp_ref, rhs_ref, plan_ref, zp_ref):
    hours, width, zones = resp_ref.shape
    place = map_ref[...]
    row, lane = place // LANES, place % LANES

    def look(i, found):
        table = jnp.broadcast_to(owner_ref[pl.ds(i, 1), :], place.shape)
        here = jnp.take_along_axis(table, lane, axis=1, mode="promise_in_bounds")
        return jnp.where(row == i, here, found)

    plan = lax.fori_loop(0, owner_ref.shape[0], look, jnp.zeros_like(place))
    for r in range(plan.shape[0]):
        plan_ref[:, r * LANES : (r + 1) * LANES] = plan[r : r + 1, :]
    designs = wp_ref.shape[0]
    onehot = (
        lax.broadcasted_iota(jnp.int32, (designs, zones), 0) == plan_ref[...]
    ).astype(F32).astype(BF16)
    rest = wp_ref[...]
    total = jnp.zeros((width, zones), F32)
    for _ in range(3):
        part = rest.astype(BF16)
        rest = rest - part.astype(F32)
        total = total + lax.dot_general(
            part, onehot, (((0,), (0,)), ((), ())), preferred_element_type=F32
        )
    zp_ref[...] = total
    extra = lax.broadcasted_iota(jnp.int32, (16, zones), 0)
    blank = jnp.zeros((DEPTH - width - 16, zones), BF16)

    def hour_step(h, carry):
        rhs_ref[h, :width, :] = (resp_ref[h].astype(F32) * zp_ref[...]).astype(BF16)
        middle = 0.25 * (band_ref[pl.ds(h, 1), :].astype(F32) - 3.5)
        tail = jnp.where(extra == 0, -middle, jnp.where(extra == 1, 1.0, 0.0))
        rhs_ref[h, width : width + 16, :] = tail.astype(BF16)
        rhs_ref[h, width + 16 :, :] = blank
        return carry

    lax.fori_loop(0, hours, hour_step, 0)


def coefficients(place, building_map, owner_ids, window_params, band_ids, response):
    hours, width, zones = response.shape
    return call(
        coeff_kernel,
        "coefficients",
        [((hours, DEPTH, zones), BF16), ((1, zones), jnp.int32)],
        [
            place,
            building_map.reshape(-1, LANES),
            owner_ids.reshape(-1, LANES),
            window_params,
            band_ids,
            response,
        ],
        [pltpu.VMEM((width, zones), F32)],
    )


def drivers(pair, second, fill):
    half = pair.shape[1] // 2
    lane = lax.broadcasted_iota(jnp.int32, pair.shape, 1)
    if second:
        pair = pltpu.roll(pair.astype(F32), half, 1).astype(BF16)
    rest = jnp.zeros(pair.shape, F32)
    for spot, value in enumerate(fill):
        rest = jnp.where(lane == half + spot, value, rest)
    return jnp.where(lane < half, pair, rest.astype(BF16))


def occupancy(hour, hours_total):
    return 1.0 + 2.0 * hour.astype(F32) / (hours_total - 1)


def scan_kernel(kind, hours_total, chunks, zone_parts, copies, place_ref, *refs):
    with_loss, with_slope = "loss" in kind, "slope" in kind
    f_refs, refs = refs[:chunks], refs[chunks:]
    rhs_ref, area_ref, refs = refs[0], refs[1], refs[2:]
    if copies:
        prior_ref, refs = refs[0], refs[1:]
    if with_loss:
        out_ref, refs = refs[0], refs[1:]
    if with_slope:
        slope_ref, ft_ref, refs = refs[0], refs[1], refs[2:]
    if with_loss:
        acc_ref = refs[0]
        acc_ref[...] = jnp.zeros_like(acc_ref)
    hours, _, zones = rhs_ref.shape
    core = place_ref[0]

    def pair_step(j, carry):
        at = pl.ds(pl.multiple_of(j * LANES, LANES), LANES)
        pair = [f_ref[:, at] for f_ref in f_refs]
        pair = pair[0] if chunks == 1 else jnp.concatenate(pair, axis=0)
        if with_slope:
            ft_ref[at, :] = pair.T
        gathered = None
        for k in range(2):
            h = 2 * j + k
            if with_loss:
                lhs = drivers(pair, k == 1, (1.0,))
                occ = occupancy(core * hours + h, hours_total)
            else:
                lhs = drivers((pair.astype(F32) * 0.5).astype(BF16), k == 1, (0.5, 0.25))
            summed = None
            for z in range(0, zones, ZONE_TILE):
                v = jnp.dot(lhs, rhs_ref[h, :, z : z + ZONE_TILE], preferred_element_type=F32)
                if with_loss:
                    a = jnp.abs(v) * MINUS_LOG2_E
                    q = jnp.exp2(a)
                    pen = jnp.log2((q + EDGE) * q + 1.0) - a
                    pen = pen * area_ref[:, z : z + ZONE_TILE]
                    for c in range(0, ZONE_TILE, LANES):
                        piece = pen[:, c : c + LANES]
                        summed = piece if summed is None else summed + piece
                if with_slope:
                    x = v * 0.5 + 0.25 if with_loss else v
                    slope = jnp.tanh(x) + jnp.tanh(x - 0.5)
                    slope_ref[h, :, z : z + ZONE_TILE] = slope.astype(BF16)
            if with_loss:
                summed = summed * occ
                gathered = summed if gathered is None else gathered + summed
        if with_loss:
            acc_ref[...] += gathered
        return carry

    lax.fori_loop(0, hours // 2, pair_step, 0, unroll=2)

    if with_loss:
        row = jnp.sum(acc_ref[...].T, axis=0, keepdims=True)
        if not copies:
            out_ref[...] = jnp.broadcast_to(row, out_ref.shape)
        else:
            zone = place_ref[1]
            half_zones = zone_parts // 2
            chunk = row.shape[1] // half_zones
            occ_sum = hours * 1.0 + (
                2.0 * (core * hours * hours + hours * (hours - 1) // 2)
            ).astype(F32) / (hours_total - 1)
            weight = jnp.sum(area_ref[...]) * occ_sum
            message = jnp.zeros(out_ref.shape[1:], F32) + weight
            index = lax.broadcasted_iota(jnp.int32, message.shape, 0)
            blank = jnp.zeros((1, LANES - chunk), F32)
            for k in range(zone_parts):
                source = prior_ref[0:1, :] if k < half_zones else row
                first = (k % half_zones) * chunk
                piece = jnp.concatenate([source[:, first : first + chunk], blank], axis=1)
                message = jnp.where(index == (zone ^ k), piece, message)
            for d in range(copies):
                out_ref[d] = message


def scan(kind, place, drivers_in, rhs, area, hours_total, zone_parts, prior=None, copies=0):
    hours, _, zones = rhs.shape
    rows = sum(f.shape[0] for f in drivers_in)
    outs = []
    scratch = []
    if "loss" in kind:
        sublanes = -(-(zone_parts + 1) // 8) * 8
        outs.append(((copies, sublanes, LANES) if copies else (8, rows), F32))
        scratch.append(pltpu.VMEM((rows, LANES), F32))
    if "slope" in kind:
        outs.append(((hours, rows, zones), BF16))
        outs.append(((drivers_in[0].shape[1], rows), BF16))
    return call(
        functools.partial(scan_kernel, kind, hours_total, len(drivers_in), zone_parts, copies),
        kind,
        outs,
        [place, *drivers_in, rhs, area] + ([prior] if copies else []),
        scratch,
    )


def gradient_kernel(
    hours_total, gain, owners, zone_parts, place_ref, msg_ref, ft0_ref, ft1_ref, slope0_ref, slope1_ref,
    resp_ref, area_ref, plan_ref, out_ref, acc_ref, score_ref, e_ref,
):
    hours, width, zones = resp_ref.shape
    core, zone = place_ref[0], place_ref[1]
    chunk = e_ref.shape[1] // zone_parts
    total = jnp.sum(msg_ref[...], axis=0)
    weight = jnp.max(total[zone_parts : zone_parts + 1, :])
    score = total * (SHARPNESS * math.log(2.0) / weight)
    rows = lax.broadcasted_iota(jnp.int32, score.shape, 0)
    lanes = lax.broadcasted_iota(jnp.int32, score.shape, 1)
    valid = (rows < zone_parts) & (lanes < chunk)
    peak = jnp.max(jnp.where(valid, score, -jnp.inf))
    e = jnp.where(valid, jnp.exp(jnp.where(valid, score - peak, 0.0)), 0.0)
    exp_total = jnp.sum(e)
    score_ref[...] = e
    for k in range(zone_parts):
        piece = score_ref[pl.ds(zone ^ k, 1), :]
        e_ref[:, k * chunk : (k + 1) * chunk] = piece[:, :chunk]
    acc_ref[...] = jnp.zeros_like(acc_ref)

    def hour_step(h, carry):
        occ = occupancy(core * hours + h, hours_total)
        at = pl.ds(pl.multiple_of(h * width, width), width)
        ft = jnp.concatenate([ft0_ref[at, :], ft1_ref[at, :]], axis=1).astype(F32)
        ft = ft * (e_ref[...] * occ)
        high = ft.astype(BF16)
        low = (ft - high.astype(F32)).astype(BF16)
        both = jnp.concatenate([high, low], axis=0)
        for z in range(0, zones, ZONE_TILE):
            at = slice(z, z + ZONE_TILE)
            kept = jnp.concatenate([slope0_ref[h, :, at], slope1_ref[h, :, at]], axis=0)
            mixed = jnp.dot(both, kept, preferred_element_type=F32)
            mixed = mixed[:width] + mixed[width:]
            acc_ref[:, at] += resp_ref[h, :, at].astype(F32) * mixed
        return carry

    lax.fori_loop(0, hours, hour_step, 0, unroll=2)

    grad = acc_ref[...] * area_ref[...]
    blocks, pad, _ = out_ref.shape
    index = lax.broadcasted_iota(jnp.int32, (blocks * pad, zones), 0)
    within = index % pad
    design = jnp.where(within < owners, (index // pad) * owners + within, -1)
    onehot = (design == plan_ref[...]).astype(F32).astype(BF16)
    sens = jnp.zeros((blocks * pad, width), F32)
    for _ in range(3):
        part = grad.astype(BF16)
        grad = grad - part.astype(F32)
        sens = sens + lax.dot_general(
            onehot, part, (((1,), (1,)), ((), ())), preferred_element_type=F32
        )
    sens = sens * (0.5 * gain / weight)
    out_ref[:, :, :width] = sens.reshape(blocks, pad, width)
    lane = lax.broadcasted_iota(jnp.int32, (blocks, pad, LANES - width), 2)
    out_ref[:, :, width:] = jnp.where(lane == 0, peak, exp_total)


def finish_kernel(scen_parts, width, parts_ref, sens_ref, objective_ref):
    parts = parts_ref[...]
    devices = parts.shape[0]
    peaks = parts[:, :, width : width + 1]
    totals = parts[:, :, width + 1 : width + 2]
    peak = jnp.max(peaks)
    scale = jnp.exp(peaks - peak)
    total = jnp.sum((scale * totals)[:, 0:1, :]) * (scen_parts / devices)
    summed = jnp.sum(parts[:, :, :width] * scale, axis=0) / total
    sens_ref[...] = summed[: sens_ref.shape[0]]
    log_total = jnp.max(jnp.log(jnp.full((8, LANES), total, F32)))
    objective_ref[0] = (peak + log_total) / SHARPNESS - 0.5


def swapped(x, axis, size, step):
    return lax.ppermute(x, axis, [(i, i ^ step) for i in range(size)])


def on_device(forcing, response, window_params, building_map, owner_ids, band_ids, floor_area):
    hours, width, zones = response.shape
    hour_parts = lax.axis_size("hour")
    zone_parts = lax.axis_size("zone")
    scen_parts = lax.axis_size("scen")
    hours_total = hours * hour_parts
    core, zone = lax.axis_index("hour"), lax.axis_index("zone")
    place = jnp.stack([core, zone]).astype(jnp.int32)
    area = floor_area.reshape(1, zones)

    half = hours * width
    everyone = forcing.reshape(forcing.shape[0], hours_total * width)
    keep = lax.dynamic_slice_in_dim(everyone, core * half, half, axis=1)
    leave = lax.dynamic_slice_in_dim(everyone, (1 - core) * half, half, axis=1)
    came = swapped(leave, "hour", hour_parts, 1)
    mine = jnp.concatenate(
        [jnp.where(core == 0, keep, came), jnp.where(core == 0, came, keep)], axis=0
    )
    if zone_parts == 4:
        halves = (
            [mine, swapped(mine, "zone", 4, 1)],
            [swapped(mine, "zone", 4, 2), swapped(mine, "zone", 4, 3)],
        )
    else:
        gathered = lax.all_gather(mine, "zone", axis=0)
        ordered = jnp.take(gathered, zone ^ jnp.arange(zone_parts), axis=0).reshape(2, -1, half)
        halves = ([ordered[0]], [ordered[1]])

    rhs, plan = coefficients(place, building_map, owner_ids, window_params, band_ids, response)
    common = (rhs, area, hours_total, zone_parts)
    first, slope0, ft0 = scan("loss_slope", place, halves[0], *common)
    (message,) = scan(
        "loss", place, halves[1], *common, prior=first, copies=zone_parts * hour_parts
    )
    shared = lax.all_to_all(message, ("zone", "hour"), split_axis=0, concat_axis=0, tiled=True)
    slope1, ft1 = scan("slope", place, halves[1], *common)

    designs = window_params.shape[0]
    devices = zone_parts * scen_parts * hour_parts
    owners = designs // devices
    pad = -(-owners // 8) * 8
    gain = math.sqrt(width * zones * zone_parts * hours_total * designs)
    (parts,) = call(
        functools.partial(gradient_kernel, hours_total, gain, owners, zone_parts),
        "gradient",
        [((devices, pad, LANES), F32)],
        [place, shared, ft0, ft1, slope0, slope1, response, area, plan],
        [
            pltpu.VMEM((width, zones), F32),
            pltpu.VMEM(shared.shape[1:], F32),
            pltpu.VMEM((1, ft0.shape[1] + ft1.shape[1]), F32),
        ],
    )
    parts = lax.all_to_all(
        parts, ("zone", "scen", "hour"), split_axis=0, concat_axis=0, tiled=True
    )
    sensitivity, objective = pl.pallas_call(
        functools.partial(finish_kernel, scen_parts, width),
        in_specs=[VMEM],
        out_specs=[VMEM, SMEM],
        out_shape=[
            jax.ShapeDtypeStruct((owners, width), F32),
            jax.ShapeDtypeStruct((1,), F32),
        ],
        compiler_params=params(),
        name="finish",
    )(near(parts))
    return (sensitivity, objective)


def solution(mesh):
    in_specs = (
        P(("groups", "zone", "scen", "hour"), None, None),
        P("hour", None, ("groups", "zone")),
        P("groups", None),
        P(("groups", "zone")),
        P("groups"),
        P("hour", ("groups", "zone")),
        P(("groups", "zone")),
    )
    out_specs = (P(("groups", "zone", "scen", "hour"), None), P("groups"))
    return jax.shard_map(
        on_device, mesh=mesh, in_specs=in_specs, out_specs=out_specs, check_vma=False
    )
```

time: 208 us -> 78.7 us (0.38)
  blocking collectives: 111 us -> 12.8 us
  matrix products: 61.8 us -> 0 us
  Pallas kernels: 0 us -> 28.3 us
  between operations: 8.65 us -> 0.77 us
  local copies, waits for them, and re-layouts: 17 us -> 24.7 us
  starting transfers between devices: 3.43 us -> 10.3 us
  other arithmetic: 4.05 us -> 0.13 us
    unnamed x2 -> x0, blocking collectives: 62.7 us -> none
    dot_general x7 -> x0, matrix products: 61.8 us -> none  [the longest x3 40.3 us: inside_climate_state(): jnp.einsum('shp,hpz->hsz', record_elements, coeff[initial_clock_time:init...]
    all_gather x1 -> x0, blocking collectives: 31.7 us -> none  [on_device(): outlook_records = lax.all_gather(mine, 'zone', axis=0, tiled=True)]
    pallas_call x0 -> x6, Pallas kernels: none -> 28.3 us  [the longest x5 27.3 us: call(): pl.pallas_call(kernel, in_specs=[SMEM] + [VMEM] * (len(args) - 1), out_sp...]
    psum x1 -> x0, blocking collectives: 16.5 us -> none  [on_device(): loss_sum, weight_total = lax.psum((sums, weight_part), ('zone', 'hour'))]
    unnamed x37 -> x38, local copies, waits for them, and re-layouts: 7.84 us -> 23.4 us
    all_to_all x0 -> x1, blocking collectives: none -> 12.8 us  [on_device(): lax.all_to_all(parts, ('zone', 'scen', 'hour'), split_axis=0, concat_axis...]
    gather x2 -> x0, local copies, waits for them, and re-layouts: 7.34 us -> none  [the longest x1 4.53 us: on_device(): candidate_plan = jnp.take(owner_ids, building_map)]
  transfers between devices with their start and end apart: 1 -> 5, of which waited for: 1 -> 1; matrix products, arithmetic and copies ran while one was open for 0% -> 0% of each run, Pallas kernels for 0% -> 20%
where the time goes in v2:
time: 78.7 us; the launch traced here: 77.9 us
  Pallas kernels  28.3 us (36%)
  local copies, waits for them, and re-layouts  24.7 us (31%)
  blocking collectives  12.8 us (16%)
  starting transfers between devices  10.3 us (13%)
  waiting for transfers between devices  0.95 us (1%)
    pallas_call x5, Pallas kernels, call(): pl.pallas_call(kernel, in_specs=[SMEM] + [VMEM] * (len(args) - 1), out_sp...  27.3 us
    unnamed x38, local copies, waits for them, and re-layouts  23.4 us
    all_to_all x1, blocking collectives, on_device(): lax.all_to_all(parts, ('zone', 'scen', 'hour'), split_axis=0, concat_axis...  12.8 us
    ppermute x4, starting transfers between devices, swapped(): return lax.ppermute(x, axis, [(i, i ^ step) for i in range(size)])  6.1 us
    all_to_all x1, starting transfers between devices, on_device(): lax.all_to_all(message, ('zone', 'hour'), split_axis=0, concat_axis=0, ti...  4.22 us
  transfers between devices with their start and end apart: 5, of which 1 were waited for; matrix products, arithmetic and copies ran while one was open for 0% of the time, Pallas kernels for 20%

profile of v2, /device:TPU:0, one launch (start us, length us, event | category | flops | bytes accessed | tf_op | source)
XLA Modules:
  0.0 77.9 jit_solution(3208369723622484487)
XLA Ops:
  0.6 1.3 %reshape.16 = bf16[32,3072]{1,0:T(8,128)(2,1)S(1)} reshape(bf16[32,48,64]{2,1,0:T(8,128)(2,1)} %param.7) | data formatting | bytes 393216 | tf_op jit(solution)/shard_map/reshape | solution.py:303
  2.0 0.5 collective-permute-start
  2.5 0.9 %collective-permute-done = bf16[32,1536]{1,0:T(8,128)(2,1)S(1)} collective-permute-done((bf16[32,1536]{1,0:T(8,128)(2,1)S(1)}, bf16[32,1536]{1,0:T(8,128)(2,1)S(1)}, u32[]{:S(2)}, u32[]{:S(2)}) %collective-permute-start) | collective-permute-done | bytes 98336 | tf_op jit(solution)/shard_map/ppermute | solution.py:289
  3.5 3.0 %collective-permute-start.3 = (bf16[64,1536]{1,0:T(8,128)(2,1)S(1)}, bf16[64,1536]{1,0:T(8,128)(2,1)S(1)}, u32[]{:S(2)}, u32[]{:S(2)}) collective-permute-start(bf16[64,1536]{1,0:T(8,128)(2,1)S(1)} %pad_maximum_fusion.refs_0_), channel_id=1, source_target_pairs={{0,4},{4,0},{8,12},{12,8},{1,5},{5,1},{9,13},{13,9},{2,6},{6,2},{1... | collective-permute-start | bytes 589832 | tf_op jit(solution)/shard_map/ppermute | solution.py:289
  6.5 2.5 %collective-permute-start.2 = (bf16[64,1536]{1,0:T(8,128)(2,1)S(1)}, bf16[64,1536]{1,0:T(8,128)(2,1)S(1)}, u32[]{:S(2)}, u32[]{:S(2)}) collective-permute-start(bf16[64,1536]{1,0:T(8,128)(2,1)S(1)} %pad_maximum_fusion.refs_0_), channel_id=1, source_target_pairs={{0,12},{4,8},{8,4},{12,0},{1,13},{5,9},{9,5},{13,1},{2,14},{6,10},... | collective-permute-start | bytes 589832 | tf_op jit(solution)/shard_map/ppermute | solution.py:289
  9.0 0.1 collective-permute-start.1
  9.1 0.1 pad_add_fusion.place_ref
  9.2 1.9 %copy-done.2 = bf16[24,64,1024]{2,1,0:T(8,128)(2,1)S(1)} copy-done((bf16[24,64,1024]{2,1,0:T(8,128)(2,1)S(1)}, bf16[24,64,1024]{2,1,0:T(8,128)(2,1)}, u32[]{:S(2)}) %copy-start.2) | copy-done | bytes 3145752
  11.1 0.9 %copy-done.13 = s32[24,1024]{1,0:T(8,128)S(1)} copy-done((s32[24,1024]{1,0:T(8,128)S(1)}, s32[24,1024]{1,0:T(8,128)}, u32[]{:S(2)}) %copy-start.13) | copy-done | bytes 98328
  11.9 0.8 copy-done.16
  12.7 0.7 copy-done.17
  13.4 0.7 copy-done.18
  14.1 2.2 %coefficients.1 = (bf16[24,128,1024]{2,1,0:T(8,128)(2,1)S(1)}, s32[1,1024]{1,0:T(1,128)S(1)}) custom-call(s32[2]{0:T(128)S(1)} %pad_add_fusion.place_ref, s32[8,128]{1,0:T(8,128)S(1)} %bitcast.9, s32[8,128]{1,0:T(8,128)S(1)} %bitcast.10, f32[64,64]{1,0:T(8,128)S(1)} %copy-done.16, s32[24,1024]{1,0:T(8,128)S(1)} %copy-done.13, bf16[24,64,1024]{2,1,0:T(8,128)(2,1)S(1)} %copy-done.2), custom_call_target="tpu_custom_call" | custom-call | tf_op jit(solution)/shard_map/coefficients/pallas_call | solution.py:32
  16.3 0.0 copy-start.14
  16.3 0.7 copy-done.14
  17.0 8.7 %loss_slope.1 = (f32[8,128]{1,0:T(8,128)S(1)}, bf16[24,128,1024]{2,1,0:T(8,128)(2,1)S(1)}, bf16[1536,128]{1,0:T(8,128)(2,1)S(1)}) custom-call(s32[2]{0:T(128)S(1)} %pad_add_fusion.place_ref, bf16[64,1536]{1,0:T(8,128)(2,1)S(1)} %pad_maximum_fusion.refs_0_, bf16[64,1536]{1,0:T(8,128)(2,1)S(1)} %collective-permute-done.3.refs_1_, ...), custom_call_target="tpu_custom_call" | custom-call | tf_op jit(solution)/shard_map/loss_slope/pallas_call | solution.py:32
  25.7 2.6 %copy-done.4 = bf16[24,128,1024]{2,1,0:T(8,128)(2,1)} copy-done((bf16[24,128,1024]{2,1,0:T(8,128)(2,1)}, bf16[24,128,1024]{2,1,0:T(8,128)(2,1)S(1)}, u32[]{:S(2)}) %copy-start.4) | copy-done | bytes 6291480
  28.4 0.8 copy-done.8
  29.2 6.3 %loss.1 = f32[8,8,128]{2,1,0:T(8,128)S(1)} custom-call(s32[2]{0:T(128)S(1)} %pad_add_fusion.place_ref, bf16[64,1536]{1,0:T(8,128)(2,1)S(1)} %collective-permute-done.1.refs_0_, bf16[64,1536]{1,0:T(8,128)(2,1)S(1)} %collective-permute-done.2.refs_1_, bf16[24,128,1024]{2,1,0:T(8,128)(2,1)S(1)} %get-tuple-element.9.refs_2_, f32[1,1024]{1,0:T(1,128)S(1)} %bitcast.6, ...), custom_call_target="tpu_custom_call" | custom-call | tf_op jit(solution)/shard_map/loss/pallas_call | solution.py:32
  35.4 0.6 copy-done.12
  36.1 4.2 %all-to-all-start = ((f32[8,8,128]{2,1,0:T(8,128)}), f32[8,8,128]{2,1,0:T(8,128)}, u32[]{:S(2)}, u32[]{:S(2)}) async-start(f32[8,8,128]{2,1,0:T(8,128)} %copy-done.12), calls=%async_computation | async-start | bytes 65536 | tf_op jit(solution)/shard_map/all_to_all | solution.py:326
  40.3 2.8 %copy-done.1 = bf16[24,128,1024]{2,1,0:T(8,128)(2,1)S(1)} copy-done((bf16[24,128,1024]{2,1,0:T(8,128)(2,1)S(1)}, bf16[24,128,1024]{2,1,0:T(8,128)(2,1)}, u32[]{:S(2)}) %copy-start.1) | copy-done | bytes 6291480
  43.1 4.9 %slope.1 = (bf16[24,128,1024]{2,1,0:T(8,128)(2,1)S(1)}, bf16[1536,128]{1,0:T(8,128)(2,1)S(1)}) custom-call(s32[2]{0:T(128)S(1)} %pad_add_fusion.place_ref, bf16[64,1536]{1,0:T(8,128)(2,1)S(1)} %collective-permute-done.1.refs_0_, bf16[64,1536]{1,0:T(8,128)(2,1)S(1)} %collective-permute-done.2.refs_1_, bf16[24,128,1024]{2,1,0:T(8,128)(2,1)S(1)} %copy-done.1, ...), custom_call_target="tpu_custom_call" | custom-call | tf_op jit(solution)/shard_map/slope/pallas_call | solution.py:32
  47.9 2.6 %copy-done.6 = bf16[24,128,1024]{2,1,0:T(8,128)(2,1)} copy-done((bf16[24,128,1024]{2,1,0:T(8,128)(2,1)}, bf16[24,128,1024]{2,1,0:T(8,128)(2,1)S(1)}, u32[]{:S(2)}) %copy-start.6) | copy-done | bytes 6291480
  50.5 0.8 copy-done.10
  51.3 2.8 %copy-done.5 = bf16[24,128,1024]{2,1,0:T(8,128)(2,1)S(1)} copy-done((bf16[24,128,1024]{2,1,0:T(8,128)(2,1)S(1)}, bf16[24,128,1024]{2,1,0:T(8,128)(2,1)}, u32[]{:S(2)}) %copy-start.5) | copy-done | bytes 6291480
  54.1 2.8 %copy-done.7 = bf16[24,128,1024]{2,1,0:T(8,128)(2,1)S(1)} copy-done((bf16[24,128,1024]{2,1,0:T(8,128)(2,1)S(1)}, bf16[24,128,1024]{2,1,0:T(8,128)(2,1)}, u32[]{:S(2)}) %copy-start.7) | copy-done | bytes 6291480
  56.9 1.0 %copy-done.9 = bf16[1536,128]{1,0:T(8,128)(2,1)S(1)} copy-done((bf16[1536,128]{1,0:T(8,128)(2,1)S(1)}, bf16[1536,128]{1,0:T(8,128)(2,1)}, u32[]{:S(2)}) %copy-start.9) | copy-done | bytes 393240
  57.9 1.0 %copy-done.11 = bf16[1536,128]{1,0:T(8,128)(2,1)S(1)} copy-done((bf16[1536,128]{1,0:T(8,128)(2,1)S(1)}, bf16[1536,128]{1,0:T(8,128)(2,1)}, u32[]{:S(2)}) %copy-start.11) | copy-done | bytes 393240
  58.9 5.3 %gradient.1 = f32[16,8,128]{2,1,0:T(8,128)S(1)} custom-call(s32[2]{0:T(128)S(1)} %pad_add_fusion.place_ref, f32[8,8,128]{2,1,0:T(8,128)} %all-to-all-done.msg_ref, bf16[1536,128]{1,0:T(8,128)(2,1)S(1)} %copy-done.9, bf16[1536,128]{1,0:T(8,128)(2,1)S(1)} %copy-done.11, bf16[24,128,1024]{2,1,0:T(8,128)(2,1)S(1)} %copy-done.5, ...), custom_call_target="tpu_custom_call" | custom-call | tf_op jit(solution)/shard_map/gradient/pallas_call | solution.py:32
  64.2 12.8 %all_to_all.10.parts_ref = f32[16,8,128]{2,1,0:T(8,128)S(1)} all-to-all(f32[16,8,128]{2,1,0:T(8,128)S(1)} %gradient.1), channel_id=1, replica_groups=mesh['groups'=2,'zone'=4,'scen'=2,'hour'=2] {'zone','scen','hour'}, dimensions={0} | all-to-all | bytes 131072 | tf_op jit(solution)/shard_map/all_to_all | solution.py:345
  77.0 0.9 %finish.1 = (f32[4,64]{1,0:T(4,128)}, f32[1]{0:T(128)}) custom-call(f32[16,8,128]{2,1,0:T(8,128)S(1)} %all_to_all.10.parts_ref), custom_call_target="tpu_custom_call" | custom-call | tf_op jit(solution)/shard_map/finish/pallas_call | solution.py:348
  (28 shorter events, 0.1 us)
Async XLA Ops:
  2.0 1.5 %collective-permute-start = (bf16[32,1536]{1,0:T(8,128)(2,1)S(1)}, bf16[32,1536]{1,0:T(8,128)(2,1)S(1)}, u32[]{:S(2)}, u32[]{:S(2)}) collective-permute-start(bf16[32,1536]{1,0:T(8,128)(2,1)S(1)} %constant_dynamic-slice_fusion), channel_id=1, source_target_pairs={{0,1},{1,0},{2,3},{3,2},{4,5},{5,4},{6,7},{7,6},{8,9},{9,8},{10,11... | collective-permute-start | bytes 294920 | tf_op jit(solution)/shard_map/ppermute | solution.py:289
  3.5 12.8 %collective-permute-start.3 = (bf16[64,1536]{1,0:T(8,128)(2,1)S(1)}, bf16[64,1536]{1,0:T(8,128)(2,1)S(1)}, u32[]{:S(2)}, u32[]{:S(2)}) collective-permute-start(bf16[64,1536]{1,0:T(8,128)(2,1)S(1)} %pad_maximum_fusion.refs_0_), channel_id=1, source_target_pairs={{0,4},{4,0},{8,12},{12,8},{1,5},{5,1},{9,13},{13,9},{2,6},{6,2},{1... | collective-permute-start | bytes 589832 | tf_op jit(solution)/shard_map/ppermute | solution.py:289
  6.5 22.7 %collective-permute-start.2 = (bf16[64,1536]{1,0:T(8,128)(2,1)S(1)}, bf16[64,1536]{1,0:T(8,128)(2,1)S(1)}, u32[]{:S(2)}, u32[]{:S(2)}) collective-permute-start(bf16[64,1536]{1,0:T(8,128)(2,1)S(1)} %pad_maximum_fusion.refs_0_), channel_id=1, source_target_pairs={{0,12},{4,8},{8,4},{12,0},{1,13},{5,9},{9,5},{13,1},{2,14},{6,10},... | collective-permute-start | bytes 589832 | tf_op jit(solution)/shard_map/ppermute | solution.py:289
  9.0 20.2 %collective-permute-start.1 = (bf16[64,1536]{1,0:T(8,128)(2,1)S(1)}, bf16[64,1536]{1,0:T(8,128)(2,1)S(1)}, u32[]{:S(2)}, u32[]{:S(2)}) collective-permute-start(bf16[64,1536]{1,0:T(8,128)(2,1)S(1)} %pad_maximum_fusion.refs_0_), channel_id=1, source_target_pairs={{0,8},{4,12},{8,0},{12,4},{1,9},{5,13},{9,1},{13,5},{2,10},{6,14},... | collective-permute-start | bytes 589832 | tf_op jit(solution)/shard_map/ppermute | solution.py:289
  9.2 1.9 %copy-start.2 = (bf16[24,64,1024]{2,1,0:T(8,128)(2,1)S(1)}, bf16[24,64,1024]{2,1,0:T(8,128)(2,1)}, u32[]{:S(2)}) copy-start(bf16[24,64,1024]{2,1,0:T(8,128)(2,1)} %resp_ref.3) | copy-start | bytes 9437188
  11.1 0.9 %copy-start.13 = (s32[24,1024]{1,0:T(8,128)S(1)}, s32[24,1024]{1,0:T(8,128)}, u32[]{:S(2)}) copy-start(s32[24,1024]{1,0:T(8,128)} %band_ref.1) | copy-start | bytes 294916
  11.9 0.8 copy-start.16
  12.7 0.7 copy-start.17
  13.4 0.7 copy-start.18
  16.3 12.9 %copy-start = (bf16[24,128,1024]{2,1,0:T(8,128)(2,1)}, bf16[24,128,1024]{2,1,0:T(8,128)(2,1)S(1)}, u32[]{:S(2)}) copy-start(bf16[24,128,1024]{2,1,0:T(8,128)(2,1)S(1)} %get-tuple-element.9.refs_2_) | copy-start | bytes 18874372
  16.3 0.7 copy-start.14
  17.0 23.3 %copy-start.15 = (f32[1024]{0:T(1024)S(1)}, f32[1024]{0:T(1024)}, u32[]{:S(2)}) copy-start(f32[1024]{0:T(1024)} %param.13) | copy-start | bytes 12292
  25.7 2.6 %copy-start.4 = (bf16[24,128,1024]{2,1,0:T(8,128)(2,1)}, bf16[24,128,1024]{2,1,0:T(8,128)(2,1)S(1)}, u32[]{:S(2)}) copy-start(bf16[24,128,1024]{2,1,0:T(8,128)(2,1)S(1)} %get-tuple-element.13.slope0_ref) | copy-start | bytes 18874372
  28.4 0.8 %copy-start.8 = (bf16[1536,128]{1,0:T(8,128)(2,1)}, bf16[1536,128]{1,0:T(8,128)(2,1)S(1)}, u32[]{:S(2)}) copy-start(bf16[1536,128]{1,0:T(8,128)(2,1)S(1)} %get-tuple-element.11.ft0_ref) | copy-start | bytes 1179652
  29.2 22.1 %copy-start.3 = (bf16[24,64,1024]{2,1,0:T(8,128)(2,1)S(1)}, bf16[24,64,1024]{2,1,0:T(8,128)(2,1)}, u32[]{:S(2)}) copy-start(bf16[24,64,1024]{2,1,0:T(8,128)(2,1)} %resp_ref.3) | copy-start | bytes 9437188
  35.4 0.6 copy-start.12
  36.1 15.3 %all-to-all-start = ((f32[8,8,128]{2,1,0:T(8,128)}), f32[8,8,128]{2,1,0:T(8,128)}, u32[]{:S(2)}, u32[]{:S(2)}) async-start(f32[8,8,128]{2,1,0:T(8,128)} %copy-done.12), calls=%async_computation | async-start | bytes 65536 | tf_op jit(solution)/shard_map/all_to_all | solution.py:326
  40.3 2.8 %copy-start.1 = (bf16[24,128,1024]{2,1,0:T(8,128)(2,1)S(1)}, bf16[24,128,1024]{2,1,0:T(8,128)(2,1)}, u32[]{:S(2)}) copy-start(bf16[24,128,1024]{2,1,0:T(8,128)(2,1)} %copy-done) | copy-start | bytes 18874372
  47.9 2.6 %copy-start.6 = (bf16[24,128,1024]{2,1,0:T(8,128)(2,1)}, bf16[24,128,1024]{2,1,0:T(8,128)(2,1)S(1)}, u32[]{:S(2)}) copy-start(bf16[24,128,1024]{2,1,0:T(8,128)(2,1)S(1)} %get-tuple-element.14.slope1_ref) | copy-start | bytes 18874372
  50.5 0.8 copy-start.10
  51.3 2.8 %copy-start.5 = (bf16[24,128,1024]{2,1,0:T(8,128)(2,1)S(1)}, bf16[24,128,1024]{2,1,0:T(8,128)(2,1)}, u32[]{:S(2)}) copy-start(bf16[24,128,1024]{2,1,0:T(8,128)(2,1)} %copy-done.4) | copy-start | bytes 18874372
  54.1 2.8 %copy-start.7 = (bf16[24,128,1024]{2,1,0:T(8,128)(2,1)S(1)}, bf16[24,128,1024]{2,1,0:T(8,128)(2,1)}, u32[]{:S(2)}) copy-start(bf16[24,128,1024]{2,1,0:T(8,128)(2,1)} %copy-done.6) | copy-start | bytes 18874372
  56.9 1.0 %copy-start.9 = (bf16[1536,128]{1,0:T(8,128)(2,1)S(1)}, bf16[1536,128]{1,0:T(8,128)(2,1)}, u32[]{:S(2)}) copy-start(bf16[1536,128]{1,0:T(8,128)(2,1)} %copy-done.8) | copy-start | bytes 1179652
  57.9 1.0 %copy-start.11 = (bf16[1536,128]{1,0:T(8,128)(2,1)S(1)}, bf16[1536,128]{1,0:T(8,128)(2,1)}, u32[]{:S(2)}) copy-start(bf16[1536,128]{1,0:T(8,128)(2,1)} %copy-done.10) | copy-start | bytes 1179652

commit v3 on v2

--- a/solution.py
+++ b/solution.py
@@ -40,8 +40,36 @@
     )(args[0], *[near(a) for a in args[1:]])
 
 
-def coeff_kernel(place_ref, map_ref, owner_ref, wp_ref, band_ref, resp_ref, rhs_ref, plan_ref, zp_ref):
+def coeff_kernel(
+    map_hbm, owner_hbm, wp_hbm, band_hbm, area_hbm, resp_hbm, rhs_ref, plan_ref, area_ref, resp_ref,
+    map_ref, owner_ref, wp_ref, band_ref, zp_ref, sems, resp_sems,
+):
     hours, width, zones = resp_ref.shape
+    pieces = resp_sems.shape[0]
+    span = hours // pieces
+    small = [
+        pltpu.make_async_copy(source, target, sems.at[i])
+        for i, (source, target) in enumerate(
+            (
+                (map_hbm, map_ref),
+                (owner_hbm, owner_ref),
+                (wp_hbm, wp_ref),
+                (band_hbm, band_ref),
+                (area_hbm, area_ref),
+            )
+        )
+    ]
+    for copy in small:
+        copy.start()
+    large = []
+    for i in range(pieces):
+        part = pl.ds(i * span, span)
+        large.append(
+            pltpu.make_async_copy(resp_hbm.at[part], resp_ref.at[part], resp_sems.at[i])
+        )
+        large[-1].start()
+    for copy in small:
+        copy.wait()
     place = map_ref[...]
     row, lane = place // LANES, place % LANES
 
@@ -77,25 +105,41 @@
         rhs_ref[h, width + 16 :, :] = blank
         return carry
 
-    lax.fori_loop(0, hours, hour_step, 0)
-
-
-def coefficients(place, building_map, owner_ids, window_params, band_ids, response):
+    for i in range(pieces):
+        large[i].wait()
+        lax.fori_loop(i * span, (i + 1) * span, hour_step, 0)
+
+
+def coefficients(building_map, owner_ids, window_params, band_ids, floor_area, response):
     hours, width, zones = response.shape
-    return call(
+    args = [
+        building_map.reshape(-1, LANES),
+        owner_ids.reshape(-1, LANES),
+        window_params,
+        band_ids,
+        floor_area.reshape(1, zones),
+        response,
+    ]
+    outs = [
+        ((hours, DEPTH, zones), BF16),
+        ((1, zones), jnp.int32),
+        ((1, zones), F32),
+        (response.shape, BF16),
+    ]
+    return pl.pallas_call(
         coeff_kernel,
-        "coefficients",
-        [((hours, DEPTH, zones), BF16), ((1, zones), jnp.int32)],
-        [
-            place,
-            building_map.reshape(-1, LANES),
-            owner_ids.reshape(-1, LANES),
-            window_params,
-            band_ids,
-            response,
+        in_specs=[pl.BlockSpec(memory_space=pl.ANY)] * len(args),
+        out_specs=[VMEM] * len(outs),
+        out_shape=[pltpu.MemorySpace.VMEM(shape, kind) for shape, kind in outs],
+        scratch_shapes=[pltpu.VMEM(a.shape, a.dtype) for a in args[:4]]
+        + [
+            pltpu.VMEM((width, zones), F32),
+            pltpu.SemaphoreType.DMA((5,)),
+            pltpu.SemaphoreType.DMA((4,)),
         ],
-        [pltpu.VMEM((width, zones), F32)],
-    )
+        compiler_params=params(),
+        name="coefficients",
+    )(*[pltpu.with_memory_space_constraint(a, pltpu.HBM) for a in args])
 
 
 def drivers(pair, second, fill):
@@ -113,11 +157,11 @@
     return 1.0 + 2.0 * hour.astype(F32) / (hours_total - 1)
 
 
-def scan_kernel(kind, hours_total, chunks, zone_parts, copies, place_ref, *refs):
+def scan_kernel(kind, hours_total, chunks, sources, last, place_ref, *refs):
     with_loss, with_slope = "loss" in kind, "slope" in kind
     f_refs, refs = refs[:chunks], refs[chunks:]
     rhs_ref, area_ref, refs = refs[0], refs[1], refs[2:]
-    if copies:
+    if last:
         prior_ref, refs = refs[0], refs[1:]
     if with_loss:
         out_ref, refs = refs[0], refs[1:]
@@ -169,69 +213,77 @@
 
     if with_loss:
         row = jnp.sum(acc_ref[...].T, axis=0, keepdims=True)
-        if not copies:
+        if not last:
             out_ref[...] = jnp.broadcast_to(row, out_ref.shape)
         else:
-            zone = place_ref[1]
-            half_zones = zone_parts // 2
-            chunk = row.shape[1] // half_zones
+            me = place_ref[1]
+            per_half = sources // 2
+            chunk = row.shape[1] // per_half
             occ_sum = hours * 1.0 + (
                 2.0 * (core * hours * hours + hours * (hours - 1) // 2)
             ).astype(F32) / (hours_total - 1)
             weight = jnp.sum(area_ref[...]) * occ_sum
-            message = jnp.zeros(out_ref.shape[1:], F32) + weight
+            message = jnp.zeros(out_ref.shape, F32) + weight
             index = lax.broadcasted_iota(jnp.int32, message.shape, 0)
             blank = jnp.zeros((1, LANES - chunk), F32)
-            for k in range(zone_parts):
-                source = prior_ref[0:1, :] if k < half_zones else row
-                first = (k % half_zones) * chunk
+            for m in range(sources):
+                source = prior_ref[0:1, :] if m < per_half else row
+                first = (m % per_half) * chunk
                 piece = jnp.concatenate([source[:, first : first + chunk], blank], axis=1)
-                message = jnp.where(index == (zone ^ k), piece, message)
-            for d in range(copies):
-                out_ref[d] = message
-
-
-def scan(kind, place, drivers_in, rhs, area, hours_total, zone_parts, prior=None, copies=0):
+                message = jnp.where(index == (me ^ m), piece, message)
+            out_ref[...] = message
+
+
+def scan(kind, place, drivers_in, rhs, area, hours_total, sources, prior=None):
     hours, _, zones = rhs.shape
     rows = sum(f.shape[0] for f in drivers_in)
     outs = []
     scratch = []
     if "loss" in kind:
-        sublanes = -(-(zone_parts + 1) // 8) * 8
-        outs.append(((copies, sublanes, LANES) if copies else (8, rows), F32))
+        sublanes = -(-(sources + 1) // 8) * 8
+        outs.append(((8, rows) if prior is None else (sublanes, LANES), F32))
         scratch.append(pltpu.VMEM((rows, LANES), F32))
     if "slope" in kind:
         outs.append(((hours, rows, zones), BF16))
         outs.append(((drivers_in[0].shape[1], rows), BF16))
     return call(
-        functools.partial(scan_kernel, kind, hours_total, len(drivers_in), zone_parts, copies),
+        functools.partial(
+            scan_kernel, kind, hours_total, len(drivers_in), sources, prior is not None
+        ),
         kind,
         outs,
-        [place, *drivers_in, rhs, area] + ([prior] if copies else []),
+        [place, *drivers_in, rhs, area] + ([] if prior is None else [prior]),
         scratch,
     )
 
 
 def gradient_kernel(
-    hours_total, gain, owners, zone_parts, place_ref, msg_ref, ft0_ref, ft1_ref, slope0_ref, slope1_ref,
-    resp_ref, area_ref, plan_ref, out_ref, acc_ref, score_ref, e_ref,
+    hours_total, gain, owners, sources, messages, place_ref, *refs
 ):
+    msg_refs, refs = refs[:messages], refs[messages:]
+    (
+        ft0_ref, ft1_ref, slope0_ref, slope1_ref, resp_ref, area_ref, plan_ref,
+        out_ref, acc_ref, score_ref, e_ref,
+    ) = refs
     hours, width, zones = resp_ref.shape
-    core, zone = place_ref[0], place_ref[1]
-    chunk = e_ref.shape[1] // zone_parts
-    total = jnp.sum(msg_ref[...], axis=0)
-    weight = jnp.max(total[zone_parts : zone_parts + 1, :])
+    core, me = place_ref[0], place_ref[1]
+    chunk = e_ref.shape[1] // sources
+    total = [msg_ref[...] for msg_ref in msg_refs]
+    while len(total) > 1:
+        total = [first + second for first, second in zip(total[::2], total[1::2])]
+    total = total[0]
+    weight = jnp.max(total[sources : sources + 1, :])
     score = total * (SHARPNESS * math.log(2.0) / weight)
     rows = lax.broadcasted_iota(jnp.int32, score.shape, 0)
     lanes = lax.broadcasted_iota(jnp.int32, score.shape, 1)
-    valid = (rows < zone_parts) & (lanes < chunk)
+    valid = (rows < sources) & (lanes < chunk)
     peak = jnp.max(jnp.where(valid, score, -jnp.inf))
     e = jnp.where(valid, jnp.exp(jnp.where(valid, score - peak, 0.0)), 0.0)
     exp_total = jnp.sum(e)
     score_ref[...] = e
-    for k in range(zone_parts):
-        piece = score_ref[pl.ds(zone ^ k, 1), :]
-        e_ref[:, k * chunk : (k + 1) * chunk] = piece[:, :chunk]
+    for m in range(sources):
+        piece = score_ref[pl.ds(me ^ m, 1), :]
+        e_ref[:, m * chunk : (m + 1) * chunk] = piece[:, :chunk]
     acc_ref[...] = jnp.zeros_like(acc_ref)
 
     def hour_step(h, carry):
@@ -285,45 +337,49 @@
     objective_ref[0] = (peak + log_total) / SHARPNESS - 0.5
 
 
-def swapped(x, axis, size, step):
-    return lax.ppermute(x, axis, [(i, i ^ step) for i in range(size)])
-
-
 def on_device(forcing, response, window_params, building_map, owner_ids, band_ids, floor_area):
     hours, width, zones = response.shape
     hour_parts = lax.axis_size("hour")
     zone_parts = lax.axis_size("zone")
     scen_parts = lax.axis_size("scen")
     hours_total = hours * hour_parts
-    core, zone = lax.axis_index("hour"), lax.axis_index("zone")
-    place = jnp.stack([core, zone]).astype(jnp.int32)
-    area = floor_area.reshape(1, zones)
+    core = lax.axis_index("hour")
+    me = lax.axis_index(("zone", "hour"))
+    sources = zone_parts * hour_parts
+    place = jnp.stack([core, me]).astype(jnp.int32)
 
     half = hours * width
     everyone = forcing.reshape(forcing.shape[0], hours_total * width)
     keep = lax.dynamic_slice_in_dim(everyone, core * half, half, axis=1)
     leave = lax.dynamic_slice_in_dim(everyone, (1 - core) * half, half, axis=1)
-    came = swapped(leave, "hour", hour_parts, 1)
-    mine = jnp.concatenate(
-        [jnp.where(core == 0, keep, came), jnp.where(core == 0, came, keep)], axis=0
-    )
+    pairs = [[(i, i ^ m) for i in range(sources)] for m in range(sources)]
+    if sources == 8:
+        came = {
+            m: lax.ppermute(leave if m % 2 else keep, ("zone", "hour"), pairs[m])
+            for m in (4, 5, 6, 7, 1, 2, 3)
+        }
+        came[0] = keep
+        halves = ([came[m] for m in range(4)], [came[m] for m in range(4, 8)])
+    else:
+        other = lax.ppermute(leave, "hour", [(0, 1), (1, 0)])
+        both = jnp.where(core == 0, jnp.stack([keep, other]), jnp.stack([other, keep]))
+        gathered = lax.all_gather(both, "zone", axis=0, tiled=True)
+        ordered = jnp.take(gathered, me ^ jnp.arange(sources), axis=0).reshape(2, -1, half)
+        halves = ([ordered[0]], [ordered[1]])
+
+    rhs, plan, area, near_response = coefficients(
+        building_map, owner_ids, window_params, band_ids, floor_area, response
+    )
+    common = (rhs, area, hours_total, sources)
+    first, slope0, ft0 = scan("loss_slope", place, halves[0], *common)
+    (message,) = scan("loss", place, halves[1], *common, prior=first)
+    message = message + lax.ppermute(message, "hour", [(0, 1), (1, 0)])
     if zone_parts == 4:
-        halves = (
-            [mine, swapped(mine, "zone", 4, 1)],
-            [swapped(mine, "zone", 4, 2), swapped(mine, "zone", 4, 3)],
-        )
+        messages = [message] + [
+            lax.ppermute(message, "zone", [(i, i ^ k) for i in range(4)]) for k in (1, 2, 3)
+        ]
     else:
-        gathered = lax.all_gather(mine, "zone", axis=0)
-        ordered = jnp.take(gathered, zone ^ jnp.arange(zone_parts), axis=0).reshape(2, -1, half)
-        halves = ([ordered[0]], [ordered[1]])
-
-    rhs, plan = coefficients(place, building_map, owner_ids, window_params, band_ids, response)
-    common = (rhs, area, hours_total, zone_parts)
-    first, slope0, ft0 = scan("loss_slope", place, halves[0], *common)
-    (message,) = scan(
-        "loss", place, halves[1], *common, prior=first, copies=zone_parts * hour_parts
-    )
-    shared = lax.all_to_all(message, ("zone", "hour"), split_axis=0, concat_axis=0, tiled=True)
+        messages = [lax.psum(message, "zone")]
     slope1, ft1 = scan("slope", place, halves[1], *common)
 
     designs = window_params.shape[0]
@@ -332,13 +388,13 @@
     pad = -(-owners // 8) * 8
     gain = math.sqrt(width * zones * zone_parts * hours_total * designs)
     (parts,) = call(
-        functools.partial(gradient_kernel, hours_total, gain, owners, zone_parts),
+        functools.partial(gradient_kernel, hours_total, gain, owners, sources, len(messages)),
         "gradient",
         [((devices, pad, LANES), F32)],
-        [place, shared, ft0, ft1, slope0, slope1, response, area, plan],
+        [place, *messages, ft0, ft1, slope0, slope1, near_response, area, plan],
         [
             pltpu.VMEM((width, zones), F32),
-            pltpu.VMEM(shared.shape[1:], F32),
+            pltpu.VMEM(message.shape, F32),
             pltpu.VMEM((1, ft0.shape[1] + ft1.shape[1]), F32),
         ],
     )

time: 78.7 us -> 60.6 us (0.77)
  local copies, waits for them, and re-layouts: 24.7 us -> 1.34 us
  starting transfers between devices: 10.3 us -> 14.4 us
  waiting for transfers between devices: 0.95 us -> 2.55 us
  Pallas kernels: 28.3 us -> 29.2 us
    unnamed x38 -> x0, local copies, waits for them, and re-layouts: 23.4 us -> none
    ppermute x4 -> x11, starting transfers between devices: 6.1 us -> 14.4 us  [the longest x7 9.85 us: on_device(): lax.ppermute(leave if m % 2 else keep, ('zone', 'hour'), pairs[m])]
    all_to_all x1 -> x0, starting transfers between devices: 4.22 us -> none  [on_device(): lax.all_to_all(message, ('zone', 'hour'), split_axis=0, concat_axis=0, ti...]
    pallas_call x0 -> x1, Pallas kernels: none -> 3.28 us  [coefficients(): pl.pallas_call(coeff_kernel, in_specs=[pl.BlockSpec(memory_space=pl.ANY)]...]
    pallas_call x5 -> x4, Pallas kernels: 27.3 us -> 24.9 us  [call(): pl.pallas_call(kernel, in_specs=[SMEM] + [VMEM] * (len(args) - 1), out_sp...]
    ppermute x4 -> x11, waiting for transfers between devices: 0.95 us -> 2.55 us  [the longest x7 1.48 us: on_device(): lax.ppermute(leave if m % 2 else keep, ('zone', 'hour'), pairs[m])]
  transfers between devices with their start and end apart: 5 -> 11, of which waited for: 1 -> 2; matrix products, arithmetic and copies ran while one was open for 0% -> 0% of each run, Pallas kernels for 20% -> 28%
where the time goes in v3:
time: 60.6 us; the launch traced here: 60.3 us
  Pallas kernels  29.2 us (48%)
  starting transfers between devices  14.4 us (24%)
  blocking collectives  12.1 us (20%)
  waiting for transfers between devices  2.55 us (4%)
  local copies, waits for them, and re-layouts  1.34 us (2%)
  between operations  0.74 us (1%)
    pallas_call x4, Pallas kernels, call(): pl.pallas_call(kernel, in_specs=[SMEM] + [VMEM] * (len(args) - 1), out_sp...  24.9 us
    all_to_all x1, blocking collectives, on_device(): lax.all_to_all(parts, ('zone', 'scen', 'hour'), split_axis=0, concat_axis...  12.1 us
    ppermute x7, starting transfers between devices, on_device(): lax.ppermute(leave if m % 2 else keep, ('zone', 'hour'), pairs[m])  9.85 us
    ppermute x3, starting transfers between devices, on_device(): lax.ppermute(message, 'zone', [(i, i ^ k) for i in range(4)])  4.39 us
    pallas_call x1, Pallas kernels, coefficients(): pl.pallas_call(coeff_kernel, in_specs=[pl.BlockSpec(memory_space=pl.ANY)]...  3.28 us
    ppermute x7, waiting for transfers between devices, on_device(): lax.ppermute(leave if m % 2 else keep, ('zone', 'hour'), pairs[m])  1.48 us
    reshape x1, local copies, waits for them, and re-layouts, on_device(): everyone = forcing.reshape(forcing.shape[0], hours_total * width)  1.32 us
  transfers between devices with their start and end apart: 11, of which 2 were waited for; matrix products, arithmetic and copies ran while one was open for 0% of the time, Pallas kernels for 28%

profile of v3, /device:TPU:0, one launch (start us, length us, event | category | flops | bytes accessed | tf_op | source)
XLA Modules:
  0.0 60.3 jit_solution(4066443349041059606)
XLA Ops:
  0.6 1.3 %reshape.16 = bf16[32,3072]{1,0:T(8,128)(2,1)S(1)} reshape(bf16[32,48,64]{2,1,0:T(8,128)(2,1)} %param.7) | data formatting | bytes 393216 | tf_op jit(solution)/shard_map/reshape | solution.py:352
  2.0 2.5 %collective-permute-start.6 = (bf16[32,1536]{1,0:T(8,128)(2,1)S(1)}, bf16[32,1536]{1,0:T(8,128)(2,1)S(1)}, u32[]{:S(2)}, u32[]{:S(2)}) collective-permute-start(bf16[32,1536]{1,0:T(8,128)(2,1)S(1)} %get-tuple-element.20), channel_id=1, source_target_pairs={{0,5},{1,4},{4,1},{5,0},{8,13},{9,12},{12,9},{13,8},{2,7},{3,6},{6... | collective-permute-start | bytes 294920 | tf_op jit(solution)/shard_map/ppermute | solution.py:358
  4.5 0.7 %collective-permute-start.4 = (bf16[32,1536]{1,0:T(8,128)(2,1)S(1)}, bf16[32,1536]{1,0:T(8,128)(2,1)S(1)}, u32[]{:S(2)}, u32[]{:S(2)}) collective-permute-start(bf16[32,1536]{1,0:T(8,128)(2,1)S(1)} %get-tuple-element.20), channel_id=1, source_target_pairs={{0,1},{1,0},{4,5},{5,4},{8,9},{9,8},{12,13},{13,12},{2,3},{3,2},{6... | collective-permute-start | bytes 294920 | tf_op jit(solution)/shard_map/ppermute | solution.py:358
  5.2 2.1 %collective-permute-start.3 = (bf16[32,1536]{1,0:T(8,128)(2,1)S(1)}, bf16[32,1536]{1,0:T(8,128)(2,1)S(1)}, u32[]{:S(2)}, u32[]{:S(2)}) collective-permute-start(bf16[32,1536]{1,0:T(8,128)(2,1)S(1)} %get-tuple-element.20), channel_id=1, source_target_pairs={{0,13},{1,12},{4,9},{5,8},{8,5},{9,4},{12,1},{13,0},{2,15},{3,14},... | collective-permute-start | bytes 294920 | tf_op jit(solution)/shard_map/ppermute | solution.py:358
  7.3 0.1 collective-permute-start.1
  7.4 1.9 %collective-permute-start.5 = (bf16[32,1536]{1,0:T(8,128)(2,1)S(1)}, bf16[32,1536]{1,0:T(8,128)(2,1)S(1)}, u32[]{:S(2)}, u32[]{:S(2)}) collective-permute-start(bf16[32,1536]{1,0:T(8,128)(2,1)S(1)} %get-tuple-element.21.refs_0_), channel_id=1, source_target_pairs={{0,4},{1,5},{4,0},{5,1},{8,12},{9,13},{12,8},{13,9},{2,6},{3,7},{6... | collective-permute-start | bytes 294920 | tf_op jit(solution)/shard_map/ppermute | solution.py:358
  9.3 3.3 %coefficients.1 = (bf16[24,128,1024]{2,1,0:T(8,128)(2,1)S(1)}, s32[1,1024]{1,0:T(1,128)S(1)}, f32[1,1024]{1,0:T(1,128)S(1)}, bf16[24,64,1024]{2,1,0:T(8,128)(2,1)S(1)}) custom-call(s32[8,128]{1,0:T(8,128)} %bitcast.5, s32[8,128]{1,0:T(8,128)} %bitcast.6, f32[64,64]{1,0:T(8,128)} %wp_hbm.1, s32[24,1024]{1,0:T(8,128)} %band_hbm.1, f32[1,1024]{1,0:T(1,128)} %bitcast.7, ...), custom_call_target="tpu_custom_call" | custom-call | tf_op jit(solution)/shard_map/coefficients/pallas_call | solution.py:129
  12.6 0.0 collective-permute-done.6.refs_3_
  12.6 2.5 %collective-permute-start.2 = (bf16[32,1536]{1,0:T(8,128)(2,1)S(1)}, bf16[32,1536]{1,0:T(8,128)(2,1)S(1)}, u32[]{:S(2)}, u32[]{:S(2)}) collective-permute-start(bf16[32,1536]{1,0:T(8,128)(2,1)S(1)} %get-tuple-element.21.refs_0_), channel_id=1, source_target_pairs={{0,12},{1,13},{4,8},{5,9},{8,4},{9,5},{12,0},{13,1},{2,14},{3,15},... | collective-permute-start | bytes 294920 | tf_op jit(solution)/shard_map/ppermute | solution.py:358
  15.1 0.0 collective-permute-done.4.refs_1_
  15.1 0.0 collective-permute-start
  15.1 0.1 pad_add_fusion.place_ref
  15.2 0.0 collective-permute-done.5.refs_2_
  15.2 8.7 %loss_slope.1 = (f32[8,128]{1,0:T(8,128)S(1)}, bf16[24,128,1024]{2,1,0:T(8,128)(2,1)S(1)}, bf16[1536,128]{1,0:T(8,128)(2,1)S(1)}) custom-call(s32[2]{0:T(128)S(1)} %pad_add_fusion.place_ref, bf16[32,1536]{1,0:T(8,128)(2,1)S(1)} %get-tuple-element.21.refs_0_, bf16[32,1536]{1,0:T(8,128)(2,1)S(1)} %collective-permute-done.4.refs_1_, ...), custom_call_target="tpu_custom_call" | custom-call | tf_op jit(solution)/shard_map/loss_slope/pallas_call | solution.py:32
  23.9 0.0 collective-permute-done.3.refs_3_
  24.0 0.0 collective-permute-done.1.refs_1_
  24.0 0.0 collective-permute-done.2.refs_2_
  24.0 1.5 %collective-permute-done.refs_0_ = bf16[32,1536]{1,0:T(8,128)(2,1)S(1)} collective-permute-done((bf16[32,1536]{1,0:T(8,128)(2,1)S(1)}, bf16[32,1536]{1,0:T(8,128)(2,1)S(1)}, u32[]{:S(2)}, u32[]{:S(2)}) %collective-permute-start) | collective-permute-done | bytes 98336 | tf_op jit(solution)/shard_map/ppermute | solution.py:358
  25.4 6.3 %loss.1 = f32[16,128]{1,0:T(8,128)S(1)} custom-call(s32[2]{0:T(128)S(1)} %pad_add_fusion.place_ref, bf16[32,1536]{1,0:T(8,128)(2,1)S(1)} %collective-permute-done.refs_0_, bf16[32,1536]{1,0:T(8,128)(2,1)S(1)} %collective-permute-done.1.refs_1_, bf16[32,1536]{1,0:T(8,128)(2,1)S(1)} %collective-permute-done.2.refs_2_, ...), custom_call_target="tpu_custom_call" | custom-call | tf_op jit(solution)/shard_map/loss/pallas_call | solution.py:32
  31.7 0.1 collective-permute-start.7
  31.8 1.1 %collective-permute-done.7 = f32[16,128]{1,0:T(8,128)S(1)} collective-permute-done((f32[16,128]{1,0:T(8,128)S(1)}, f32[16,128]{1,0:T(8,128)S(1)}, u32[]{:S(2)}, u32[]{:S(2)}) %collective-permute-start.7) | collective-permute-done | bytes 8224 | tf_op jit(solution)/shard_map/ppermute | solution.py:376
  32.9 3.1 %collective-permute-start.10 = (f32[16,128]{1,0:T(8,128)S(1)}, f32[16,128]{1,0:T(8,128)S(1)}, u32[]{:S(2)}, u32[]{:S(2)}) collective-permute-start(f32[16,128]{1,0:T(8,128)S(1)} %add.15.refs_0_), channel_id=1, source_target_pairs={{0,12},{4,8},{8,4},{12,0},{1,13},{5,9},{9,5},{13,1},{2,14},{6,10},... | collective-permute-start | bytes 24584 | tf_op jit(solution)/shard_map/ppermute | solution.py:379
  36.0 0.0 collective-permute-start.9
  36.0 1.3 %collective-permute-start.8 = (f32[16,128]{1,0:T(8,128)S(1)}, f32[16,128]{1,0:T(8,128)S(1)}, u32[]{:S(2)}, u32[]{:S(2)}) collective-permute-start(f32[16,128]{1,0:T(8,128)S(1)} %add.15.refs_0_), channel_id=1, source_target_pairs={{0,4},{4,0},{8,12},{12,8},{1,5},{5,1},{9,13},{13,9},{2,6},{6,2},{1... | collective-permute-start | bytes 24584 | tf_op jit(solution)/shard_map/ppermute | solution.py:379
  37.3 4.9 %slope.1 = (bf16[24,128,1024]{2,1,0:T(8,128)(2,1)S(1)}, bf16[1536,128]{1,0:T(8,128)(2,1)S(1)}) custom-call(s32[2]{0:T(128)S(1)} %pad_add_fusion.place_ref, bf16[32,1536]{1,0:T(8,128)(2,1)S(1)} %collective-permute-done.refs_0_, bf16[32,1536]{1,0:T(8,128)(2,1)S(1)} %collective-permute-done.1.refs_1_, bf16[32,1536]{1,0:T(8,128)(2,1)S(1)} %collective-permute-done.2.refs_2_, ...), custom_call_target="tpu_custom_call" | custom-call | tf_op jit(solution)/shard_map/slope/pallas_call | solution.py:32
  42.2 0.0 collective-permute-done.10.refs_3_
  42.2 0.0 collective-permute-done.9.refs_2_
  42.2 0.0 collective-permute-done.8.refs_1_
  42.2 5.1 %gradient.1 = f32[16,8,128]{2,1,0:T(8,128)S(1)} custom-call(s32[2]{0:T(128)S(1)} %pad_add_fusion.place_ref, f32[16,128]{1,0:T(8,128)S(1)} %add.15.refs_0_, f32[16,128]{1,0:T(8,128)S(1)} %collective-permute-done.8.refs_1_, f32[16,128]{1,0:T(8,128)S(1)} %collective-permute-done.9.refs_2_, f32[16,128]{1,0:T(8,128)S(1)} %collective-permute-done.10.refs_3_, ...), custom_call_target="tpu_custom_call" | custom-call | tf_op jit(solution)/shard_map/gradient/pallas_call | solution.py:32
  47.3 12.1 %all_to_all.5.parts_ref = f32[16,8,128]{2,1,0:T(8,128)S(1)} all-to-all(f32[16,8,128]{2,1,0:T(8,128)S(1)} %gradient.1), channel_id=1, replica_groups=mesh['groups'=2,'zone'=4,'scen'=2,'hour'=2] {'zone','scen','hour'}, dimensions={0} | all-to-all | bytes 131072 | tf_op jit(solution)/shard_map/all_to_all | solution.py:401
  59.4 0.9 %finish.1 = (f32[4,64]{1,0:T(4,128)}, f32[1]{0:T(128)}) custom-call(f32[16,8,128]{2,1,0:T(8,128)S(1)} %all_to_all.5.parts_ref), custom_call_target="tpu_custom_call" | custom-call | tf_op jit(solution)/shard_map/finish/pallas_call | solution.py:404
  (2 shorter events, 0.0 us)
Async XLA Ops:
  2.0 10.6 %collective-permute-start.6 = (bf16[32,1536]{1,0:T(8,128)(2,1)S(1)}, bf16[32,1536]{1,0:T(8,128)(2,1)S(1)}, u32[]{:S(2)}, u32[]{:S(2)}) collective-permute-start(bf16[32,1536]{1,0:T(8,128)(2,1)S(1)} %get-tuple-element.20), channel_id=1, source_target_pairs={{0,5},{1,4},{4,1},{5,0},{8,13},{9,12},{12,9},{13,8},{2,7},{3,6},{6... | collective-permute-start | bytes 294920 | tf_op jit(solution)/shard_map/ppermute | solution.py:358
  4.5 10.6 %collective-permute-start.4 = (bf16[32,1536]{1,0:T(8,128)(2,1)S(1)}, bf16[32,1536]{1,0:T(8,128)(2,1)S(1)}, u32[]{:S(2)}, u32[]{:S(2)}) collective-permute-start(bf16[32,1536]{1,0:T(8,128)(2,1)S(1)} %get-tuple-element.20), channel_id=1, source_target_pairs={{0,1},{1,0},{4,5},{5,4},{8,9},{9,8},{12,13},{13,12},{2,3},{3,2},{6... | collective-permute-start | bytes 294920 | tf_op jit(solution)/shard_map/ppermute | solution.py:358
  5.2 18.8 %collective-permute-start.3 = (bf16[32,1536]{1,0:T(8,128)(2,1)S(1)}, bf16[32,1536]{1,0:T(8,128)(2,1)S(1)}, u32[]{:S(2)}, u32[]{:S(2)}) collective-permute-start(bf16[32,1536]{1,0:T(8,128)(2,1)S(1)} %get-tuple-element.20), channel_id=1, source_target_pairs={{0,13},{1,12},{4,9},{5,8},{8,5},{9,4},{12,1},{13,0},{2,15},{3,14},... | collective-permute-start | bytes 294920 | tf_op jit(solution)/shard_map/ppermute | solution.py:358
  7.3 16.7 %collective-permute-start.1 = (bf16[32,1536]{1,0:T(8,128)(2,1)S(1)}, bf16[32,1536]{1,0:T(8,128)(2,1)S(1)}, u32[]{:S(2)}, u32[]{:S(2)}) collective-permute-start(bf16[32,1536]{1,0:T(8,128)(2,1)S(1)} %get-tuple-element.20), channel_id=1, source_target_pairs={{0,9},{1,8},{4,13},{5,12},{8,1},{9,0},{12,5},{13,4},{2,11},{3,10},... | collective-permute-start | bytes 294920 | tf_op jit(solution)/shard_map/ppermute | solution.py:358
  7.4 7.8 %collective-permute-start.5 = (bf16[32,1536]{1,0:T(8,128)(2,1)S(1)}, bf16[32,1536]{1,0:T(8,128)(2,1)S(1)}, u32[]{:S(2)}, u32[]{:S(2)}) collective-permute-start(bf16[32,1536]{1,0:T(8,128)(2,1)S(1)} %get-tuple-element.21.refs_0_), channel_id=1, source_target_pairs={{0,4},{1,5},{4,0},{5,1},{8,12},{9,13},{12,8},{13,9},{2,6},{3,7},{6... | collective-permute-start | bytes 294920 | tf_op jit(solution)/shard_map/ppermute | solution.py:358
  12.6 11.4 %collective-permute-start.2 = (bf16[32,1536]{1,0:T(8,128)(2,1)S(1)}, bf16[32,1536]{1,0:T(8,128)(2,1)S(1)}, u32[]{:S(2)}, u32[]{:S(2)}) collective-permute-start(bf16[32,1536]{1,0:T(8,128)(2,1)S(1)} %get-tuple-element.21.refs_0_), channel_id=1, source_target_pairs={{0,12},{1,13},{4,8},{5,9},{8,4},{9,5},{12,0},{13,1},{2,14},{3,15},... | collective-permute-start | bytes 294920 | tf_op jit(solution)/shard_map/ppermute | solution.py:358
  15.1 10.3 %collective-permute-start = (bf16[32,1536]{1,0:T(8,128)(2,1)S(1)}, bf16[32,1536]{1,0:T(8,128)(2,1)S(1)}, u32[]{:S(2)}, u32[]{:S(2)}) collective-permute-start(bf16[32,1536]{1,0:T(8,128)(2,1)S(1)} %get-tuple-element.21.refs_0_), channel_id=1, source_target_pairs={{0,8},{1,9},{4,12},{5,13},{8,0},{9,1},{12,4},{13,5},{2,10},{3,11},... | collective-permute-start | bytes 294920 | tf_op jit(solution)/shard_map/ppermute | solution.py:358
  31.7 1.2 %collective-permute-start.7 = (f32[16,128]{1,0:T(8,128)S(1)}, f32[16,128]{1,0:T(8,128)S(1)}, u32[]{:S(2)}, u32[]{:S(2)}) collective-permute-start(f32[16,128]{1,0:T(8,128)S(1)} %loss.1), channel_id=1, source_target_pairs={{0,1},{1,0},{2,3},{3,2},{4,5},{5,4},{6,7},{7,6},{8,9},{9,8},{10,11... | collective-permute-start | bytes 24584 | tf_op jit(solution)/shard_map/ppermute | solution.py:376
  32.9 9.3 %collective-permute-start.10 = (f32[16,128]{1,0:T(8,128)S(1)}, f32[16,128]{1,0:T(8,128)S(1)}, u32[]{:S(2)}, u32[]{:S(2)}) collective-permute-start(f32[16,128]{1,0:T(8,128)S(1)} %add.15.refs_0_), channel_id=1, source_target_pairs={{0,12},{4,8},{8,4},{12,0},{1,13},{5,9},{9,5},{13,1},{2,14},{6,10},... | collective-permute-start | bytes 24584 | tf_op jit(solution)/shard_map/ppermute | solution.py:379
  36.0 6.2 %collective-permute-start.9 = (f32[16,128]{1,0:T(8,128)S(1)}, f32[16,128]{1,0:T(8,128)S(1)}, u32[]{:S(2)}, u32[]{:S(2)}) collective-permute-start(f32[16,128]{1,0:T(8,128)S(1)} %add.15.refs_0_), channel_id=1, source_target_pairs={{0,8},{4,12},{8,0},{12,4},{1,9},{5,13},{9,1},{13,5},{2,10},{6,14},... | collective-permute-start | bytes 24584 | tf_op jit(solution)/shard_map/ppermute | solution.py:379
  36.0 6.2 %collective-permute-start.8 = (f32[16,128]{1,0:T(8,128)S(1)}, f32[16,128]{1,0:T(8,128)S(1)}, u32[]{:S(2)}, u32[]{:S(2)}) collective-permute-start(f32[16,128]{1,0:T(8,128)S(1)} %add.15.refs_0_), channel_id=1, source_target_pairs={{0,4},{4,0},{8,12},{12,8},{1,5},{5,1},{9,13},{13,9},{2,6},{6,2},{1... | collective-permute-start | bytes 24584 | tf_op jit(solution)/shard_map/ppermute | solution.py:379

commit v4 on v3

--- a/solution.py
+++ b/solution.py
@@ -14,6 +14,7 @@
 LANES = 128
 DEPTH = 128
 ZONE_TILE = 256
+SHORT = pl.CostEstimate(flops=1, bytes_accessed=1, transcendentals=0)
 VMEM = pl.BlockSpec(memory_space=pltpu.VMEM)
 SMEM = pl.BlockSpec(memory_space=pltpu.SMEM)
 F32 = jnp.float32
@@ -28,16 +29,17 @@
     return pltpu.with_memory_space_constraint(x, pltpu.VMEM)
 
 
-def call(kernel, name, outs, args, scratch=()):
+def call(kernel, name, outs, args, scratch=(), cost=None):
     return pl.pallas_call(
         kernel,
-        in_specs=[SMEM] + [VMEM] * (len(args) - 1),
+        in_specs=[VMEM] * len(args),
         out_specs=[VMEM] * len(outs),
         out_shape=[pltpu.MemorySpace.VMEM(shape, kind) for shape, kind in outs],
         scratch_shapes=list(scratch),
         compiler_params=params(),
+        cost_estimate=cost,
         name=name,
-    )(args[0], *[near(a) for a in args[1:]])
+    )(*[near(a) for a in args])
 
 
 def coeff_kernel(
@@ -138,6 +140,7 @@
             pltpu.SemaphoreType.DMA((4,)),
         ],
         compiler_params=params(),
+        cost_estimate=SHORT,
         name="coefficients",
     )(*[pltpu.with_memory_space_constraint(a, pltpu.HBM) for a in args])
 
@@ -153,32 +156,42 @@
     return jnp.where(lane < half, pair, rest.astype(BF16))
 
 
+def here():
+    core = lax.axis_index("hour")
+    return core, lax.axis_index("zone") * lax.axis_size("hour") + core
+
+
 def occupancy(hour, hours_total):
     return 1.0 + 2.0 * hour.astype(F32) / (hours_total - 1)
 
 
-def scan_kernel(kind, hours_total, chunks, sources, last, place_ref, *refs):
-    with_loss, with_slope = "loss" in kind, "slope" in kind
+def scan_kernel(kind, hours_total, chunks, extra, sources, priors, unroll, *refs):
+    with_loss, with_slope, with_turn = "loss" in kind, "slope" in kind, "turn" in kind
     f_refs, refs = refs[:chunks], refs[chunks:]
+    turn_refs, refs = [*refs[:extra], *f_refs], refs[extra:]
     rhs_ref, area_ref, refs = refs[0], refs[1], refs[2:]
-    if last:
-        prior_ref, refs = refs[0], refs[1:]
+    prior_refs, refs = refs[:priors], refs[priors:]
     if with_loss:
         out_ref, refs = refs[0], refs[1:]
     if with_slope:
-        slope_ref, ft_ref, refs = refs[0], refs[1], refs[2:]
+        slope_ref, refs = refs[0], refs[1:]
+    if with_turn:
+        ft_ref, refs = refs[0], refs[1:]
     if with_loss:
         acc_ref = refs[0]
         acc_ref[...] = jnp.zeros_like(acc_ref)
     hours, _, zones = rhs_ref.shape
-    core = place_ref[0]
+    core, me = here()
+
+    def rows_of(parts, at):
+        parts = [part[:, at] for part in parts]
+        return parts[0] if len(parts) == 1 else jnp.concatenate(parts, axis=0)
 
     def pair_step(j, carry):
         at = pl.ds(pl.multiple_of(j * LANES, LANES), LANES)
-        pair = [f_ref[:, at] for f_ref in f_refs]
-        pair = pair[0] if chunks == 1 else jnp.concatenate(pair, axis=0)
-        if with_slope:
-            ft_ref[at, :] = pair.T
+        pair = rows_of(f_refs, at)
+        if with_turn:
+            ft_ref[at, :] = rows_of(turn_refs, at).T
         gathered = None
         for k in range(2):
             h = 2 * j + k
@@ -209,16 +222,20 @@
             acc_ref[...] += gathered
         return carry
 
-    lax.fori_loop(0, hours // 2, pair_step, 0, unroll=2)
+    lax.fori_loop(0, hours // 2, pair_step, 0, unroll=unroll)
 
     if with_loss:
         row = jnp.sum(acc_ref[...].T, axis=0, keepdims=True)
-        if not last:
+        if not priors:
             out_ref[...] = jnp.broadcast_to(row, out_ref.shape)
         else:
-            me = place_ref[1]
-            per_half = sources // 2
-            chunk = row.shape[1] // per_half
+            known = [ref[0:1, :] for ref in prior_refs] + [row]
+            chunk = sum(part.shape[1] for part in known) // sources
+            pieces = [
+                part[:, first : first + chunk]
+                for part in known
+                for first in range(0, part.shape[1], chunk)
+            ]
             occ_sum = hours * 1.0 + (
                 2.0 * (core * hours * hours + hours * (hours - 1) // 2)
             ).astype(F32) / (hours_total - 1)
@@ -226,47 +243,45 @@
             message = jnp.zeros(out_ref.shape, F32) + weight
             index = lax.broadcasted_iota(jnp.int32, message.shape, 0)
             blank = jnp.zeros((1, LANES - chunk), F32)
-            for m in range(sources):
-                source = prior_ref[0:1, :] if m < per_half else row
-                first = (m % per_half) * chunk
-                piece = jnp.concatenate([source[:, first : first + chunk], blank], axis=1)
+            for m, piece in enumerate(pieces):
+                piece = jnp.concatenate([piece, blank], axis=1)
                 message = jnp.where(index == (me ^ m), piece, message)
             out_ref[...] = message
 
 
-def scan(kind, place, drivers_in, rhs, area, hours_total, sources, prior=None):
+def scan(kind, rows_in, rhs, area, hours_total, sources, extra=(), priors=(), unroll=4, cost=None):
     hours, _, zones = rhs.shape
-    rows = sum(f.shape[0] for f in drivers_in)
+    rows = sum(f.shape[0] for f in rows_in)
     outs = []
     scratch = []
     if "loss" in kind:
         sublanes = -(-(sources + 1) // 8) * 8
-        outs.append(((8, rows) if prior is None else (sublanes, LANES), F32))
+        outs.append(((sublanes, LANES) if priors else (8, rows), F32))
         scratch.append(pltpu.VMEM((rows, LANES), F32))
     if "slope" in kind:
         outs.append(((hours, rows, zones), BF16))
-        outs.append(((drivers_in[0].shape[1], rows), BF16))
+    if "turn" in kind:
+        outs.append(((rows_in[0].shape[1], rows + sum(f.shape[0] for f in extra)), BF16))
     return call(
         functools.partial(
-            scan_kernel, kind, hours_total, len(drivers_in), sources, prior is not None
+            scan_kernel, kind, hours_total, len(rows_in), len(extra), sources, len(priors), unroll
         ),
         kind,
         outs,
-        [place, *drivers_in, rhs, area] + ([] if prior is None else [prior]),
+        [*rows_in, *extra, rhs, area, *priors],
         scratch,
+        cost,
     )
 
 
 def gradient_kernel(
-    hours_total, gain, owners, sources, messages, place_ref, *refs
+    hours_total, gain, owners, sources, messages, *refs
 ):
     msg_refs, refs = refs[:messages], refs[messages:]
-    (
-        ft0_ref, ft1_ref, slope0_ref, slope1_ref, resp_ref, area_ref, plan_ref,
-        out_ref, acc_ref, score_ref, e_ref,
-    ) = refs
+    ft_refs, slope_refs, refs = refs[:2], refs[2:5], refs[5:]
+    resp_ref, area_ref, plan_ref, out_ref, acc_ref, score_ref, e_ref = refs
     hours, width, zones = resp_ref.shape
-    core, me = place_ref[0], place_ref[1]
+    core, me = here()
     chunk = e_ref.shape[1] // sources
     total = [msg_ref[...] for msg_ref in msg_refs]
     while len(total) > 1:
@@ -289,20 +304,20 @@
     def hour_step(h, carry):
         occ = occupancy(core * hours + h, hours_total)
         at = pl.ds(pl.multiple_of(h * width, width), width)
-        ft = jnp.concatenate([ft0_ref[at, :], ft1_ref[at, :]], axis=1).astype(F32)
+        ft = jnp.concatenate([ref[at, :] for ref in ft_refs], axis=1).astype(F32)
         ft = ft * (e_ref[...] * occ)
         high = ft.astype(BF16)
         low = (ft - high.astype(F32)).astype(BF16)
         both = jnp.concatenate([high, low], axis=0)
         for z in range(0, zones, ZONE_TILE):
             at = slice(z, z + ZONE_TILE)
-            kept = jnp.concatenate([slope0_ref[h, :, at], slope1_ref[h, :, at]], axis=0)
+            kept = jnp.concatenate([ref[h, :, at] for ref in slope_refs], axis=0)
             mixed = jnp.dot(both, kept, preferred_element_type=F32)
             mixed = mixed[:width] + mixed[width:]
             acc_ref[:, at] += resp_ref[h, :, at].astype(F32) * mixed
         return carry
 
-    lax.fori_loop(0, hours, hour_step, 0, unroll=2)
+    lax.fori_loop(0, hours, hour_step, 0, unroll=4)
 
     grad = acc_ref[...] * area_ref[...]
     blocks, pad, _ = out_ref.shape
@@ -344,43 +359,43 @@
     scen_parts = lax.axis_size("scen")
     hours_total = hours * hour_parts
     core = lax.axis_index("hour")
-    me = lax.axis_index(("zone", "hour"))
     sources = zone_parts * hour_parts
-    place = jnp.stack([core, me]).astype(jnp.int32)
 
     half = hours * width
     everyone = forcing.reshape(forcing.shape[0], hours_total * width)
     keep = lax.dynamic_slice_in_dim(everyone, core * half, half, axis=1)
     leave = lax.dynamic_slice_in_dim(everyone, (1 - core) * half, half, axis=1)
-    pairs = [[(i, i ^ m) for i in range(sources)] for m in range(sources)]
-    if sources == 8:
-        came = {
-            m: lax.ppermute(leave if m % 2 else keep, ("zone", "hour"), pairs[m])
-            for m in (4, 5, 6, 7, 1, 2, 3)
-        }
-        came[0] = keep
-        halves = ([came[m] for m in range(4)], [came[m] for m in range(4, 8)])
-    else:
-        other = lax.ppermute(leave, "hour", [(0, 1), (1, 0)])
-        both = jnp.where(core == 0, jnp.stack([keep, other]), jnp.stack([other, keep]))
-        gathered = lax.all_gather(both, "zone", axis=0, tiled=True)
-        ordered = jnp.take(gathered, me ^ jnp.arange(sources), axis=0).reshape(2, -1, half)
-        halves = ([ordered[0]], [ordered[1]])
+    came = lax.ppermute(leave, "hour", [(0, 1), (1, 0)])
+    mine = jnp.concatenate([keep, came], axis=0)
+
+    def swap(x, step):
+        return lax.ppermute(x, "zone", [(i, i ^ step) for i in range(zone_parts)])
 
     rhs, plan, area, near_response = coefficients(
         building_map, owner_ids, window_params, band_ids, floor_area, response
     )
     common = (rhs, area, hours_total, sources)
-    first, slope0, ft0 = scan("loss_slope", place, halves[0], *common)
-    (message,) = scan("loss", place, halves[1], *common, prior=first)
+    if zone_parts == 4:
+        far = swap(mine, 2)
+        beside = swap(mine, 1)
+        loss0, slope0 = scan("loss_slope", [mine], *common, cost=SHORT)
+        far, loss0 = lax.optimization_barrier((far, loss0))
+        last = [far, swap(far, 1)]
+    else:
+        me = lax.axis_index(("zone", "hour"))
+        both = jnp.where(core == 0, jnp.stack([keep, came]), jnp.stack([came, keep]))
+        gathered = lax.all_gather(both, "zone", axis=0, tiled=True)
+        ordered = jnp.take(gathered, me ^ jnp.arange(sources), axis=0).reshape(4, -1, half)
+        mine, beside, last = ordered[0], ordered[1], [ordered[2], ordered[3]]
+        loss0, slope0 = scan("loss_slope", [mine], *common)
+    loss1, slope1, ft0 = scan("loss_slope_turn", [beside], *common, extra=[mine])
+    (message,) = scan("loss", last, *common, priors=[loss0, loss1], unroll=6)
     message = message + lax.ppermute(message, "hour", [(0, 1), (1, 0)])
     if zone_parts == 4:
-        messages = [message] + [
-            lax.ppermute(message, "zone", [(i, i ^ k) for i in range(4)]) for k in (1, 2, 3)
-        ]
+        messages = [message] + [swap(message, k) for k in (1, 2, 3)]
     else:
         messages = [lax.psum(message, "zone")]
-    slope1, ft1 = scan("slope", place, halves[1], *common)
+    slope2, ft1 = scan("slope_turn", last, *common)
 
     designs = window_params.shape[0]
     devices = zone_parts * scen_parts * hour_parts
@@ -391,7 +406,7 @@
         functools.partial(gradient_kernel, hours_total, gain, owners, sources, len(messages)),
         "gradient",
         [((devices, pad, LANES), F32)],
-        [place, *messages, ft0, ft1, slope0, slope1, near_response, area, plan],
+        [*messages, ft0, ft1, slope0, slope1, slope2, near_response, area, plan],
         [
             pltpu.VMEM((width, zones), F32),
             pltpu.VMEM(message.shape, F32),

time: 60.6 us -> 56 us (0.924)
  Pallas kernels: 29.2 us -> 25.7 us
  waiting for transfers between devices: 2.55 us -> 5.8 us
  starting transfers between devices: 14.4 us -> 11.3 us
  blocking collectives: 12.1 us -> 11 us
    pallas_call x4 -> x5, Pallas kernels: 24.9 us -> 21.5 us  [call(): pl.pallas_call(kernel, in_specs=[VMEM] * len(args), out_specs=[VMEM] * le...]
    ppermute x10 -> x7, waiting for transfers between devices: 1.49 us -> 4.64 us  [the longest x6 3.7 us: swap(): return lax.ppermute(x, 'zone', [(i, i ^ step) for i in range(zone_parts)])]
    ppermute x10 -> x7, starting transfers between devices: 14.2 us -> 11.2 us  [the longest x6 10.7 us: swap(): return lax.ppermute(x, 'zone', [(i, i ^ step) for i in range(zone_parts)])]
    all_to_all x1, blocking collectives: 12.1 us -> 11 us  [on_device(): lax.all_to_all(parts, ('zone', 'scen', 'hour'), split_axis=0, concat_axis...]
  transfers between devices with their start and end apart: 11 -> 8, of which waited for: 2 -> 4; matrix products, arithmetic and copies ran while one was open for 0% -> 0% of each run, Pallas kernels for 28% -> 28%
where the time goes in v4:
time: 56 us; the launch traced here: 55.8 us
  Pallas kernels  25.7 us (46%)
  starting transfers between devices  11.3 us (20%)
  blocking collectives  11 us (20%)
  waiting for transfers between devices  5.8 us (10%)
  local copies, waits for them, and re-layouts  1.34 us (2%)
  between operations  0.73 us (1%)
    pallas_call x5, Pallas kernels, call(): pl.pallas_call(kernel, in_specs=[VMEM] * len(args), out_specs=[VMEM] * le...  21.5 us
    all_to_all x1, blocking collectives, on_device(): lax.all_to_all(parts, ('zone', 'scen', 'hour'), split_axis=0, concat_axis...  11 us
    ppermute x6, starting transfers between devices, swap(): return lax.ppermute(x, 'zone', [(i, i ^ step) for i in range(zone_parts)])  10.7 us
    ppermute x6, waiting for transfers between devices, swap(): return lax.ppermute(x, 'zone', [(i, i ^ step) for i in range(zone_parts)])  3.7 us
    pallas_call x1, Pallas kernels, coefficients(): pl.pallas_call(coeff_kernel, in_specs=[pl.BlockSpec(memory_space=pl.ANY)]...  3.28 us
    reshape x1, local copies, waits for them, and re-layouts, on_device(): everyone = forcing.reshape(forcing.shape[0], hours_total * width)  1.32 us
    ppermute x1, waiting for transfers between devices, on_device(): message = message + lax.ppermute(message, 'hour', [(0, 1), (1, 0)])  1.16 us
  transfers between devices with their start and end apart: 8, of which 4 were waited for; matrix products, arithmetic and copies ran while one was open for 0% of the time, Pallas kernels for 28%

profile of v4, /device:TPU:0, one launch (start us, length us, event | category | flops | bytes accessed | tf_op | source)
XLA Modules:
  0.0 55.8 jit_solution(16564312079155757949)
XLA Ops:
  0.6 1.3 %reshape.16 = bf16[32,3072]{1,0:T(8,128)(2,1)S(1)} reshape(bf16[32,48,64]{2,1,0:T(8,128)(2,1)} %param.7) | data formatting | bytes 393216 | tf_op jit(solution)/shard_map/reshape | solution.py:365
  2.0 0.5 collective-permute-start
  2.5 0.9 %collective-permute-done = bf16[32,1536]{1,0:T(8,128)(2,1)S(1)} collective-permute-done((bf16[32,1536]{1,0:T(8,128)(2,1)S(1)}, bf16[32,1536]{1,0:T(8,128)(2,1)S(1)}, u32[]{:S(2)}, u32[]{:S(2)}) %collective-permute-start) | collective-permute-done | bytes 98336 | tf_op jit(solution)/shard_map/ppermute | solution.py:368
  3.5 4.0 %collective-permute-start.1 = (bf16[64,1536]{1,0:T(8,128)(2,1)S(1)}, bf16[64,1536]{1,0:T(8,128)(2,1)S(1)}, u32[]{:S(2)}, u32[]{:S(2)}) collective-permute-start(bf16[64,1536]{1,0:T(8,128)(2,1)S(1)} %pad_maximum_fusion.refs_0_.refs_1_), channel_id=1, source_target_pairs={{0,8},{4,12},{8,0},{12,4},{1,9},{5,13},{9,1},{13,5},{2,10},{6,14},... | collective-permute-start | bytes 589832 | tf_op jit(solution)/shard_map/ppermute | solution.py:372
  7.5 3.3 %coefficients.1 = (bf16[24,128,1024]{2,1,0:T(8,128)(2,1)S(1)}, s32[1,1024]{1,0:T(1,128)S(1)}, f32[1,1024]{1,0:T(1,128)S(1)}, bf16[24,64,1024]{2,1,0:T(8,128)(2,1)S(1)}) custom-call(s32[8,128]{1,0:T(8,128)} %bitcast.3, s32[8,128]{1,0:T(8,128)} %bitcast.4, f32[64,64]{1,0:T(8,128)} %wp_hbm.1, s32[24,1024]{1,0:T(8,128)} %band_hbm.1, f32[1,1024]{1,0:T(1,128)} %bitcast.5, ...), custom_call_target="tpu_custom_call" | custom-call | flops 1 | bytes 1 | tf_op jit(solution)/shard_map/coefficients/pallas_call | solution.py:131
  10.8 1.6 %collective-permute-start.3 = (bf16[64,1536]{1,0:T(8,128)(2,1)S(1)}, bf16[64,1536]{1,0:T(8,128)(2,1)S(1)}, u32[]{:S(2)}, u32[]{:S(2)}) collective-permute-start(bf16[64,1536]{1,0:T(8,128)(2,1)S(1)} %pad_maximum_fusion.refs_0_.refs_1_), channel_id=1, source_target_pairs={{0,4},{4,0},{8,12},{12,8},{1,5},{5,1},{9,13},{13,9},{2,6},{6,2},{1... | collective-permute-start | bytes 589832 | tf_op jit(solution)/shard_map/ppermute | solution.py:372
  12.4 4.3 %loss_slope.1 = (f32[8,64]{1,0:T(8,128)S(1)}, bf16[24,64,1024]{2,1,0:T(8,128)(2,1)S(1)}) custom-call(bf16[64,1536]{1,0:T(8,128)(2,1)S(1)} %pad_maximum_fusion.refs_0_.refs_1_, bf16[24,128,1024]{2,1,0:T(8,128)(2,1)S(1)} %get-tuple-element.15.refs_1_.refs_2_, f32[1,1024]{1,0:T(1,128)S(1)} %get-tuple-element.16.refs_2_.refs_3_.refs_10_), custom_call_target="tpu_custom_call" | custom-call | flops 1 | bytes 1 | tf_op jit(solution)/shard_map/loss_slope/pallas_call | solution.py:33
  16.7 0.3 collective-permute-done.1.refs_0_
  17.0 0.7 %collective-permute-start.2 = (bf16[64,1536]{1,0:T(8,128)(2,1)S(1)}, bf16[64,1536]{1,0:T(8,128)(2,1)S(1)}, u32[]{:S(2)}, u32[]{:S(2)}) collective-permute-start(bf16[64,1536]{1,0:T(8,128)(2,1)S(1)} %collective-permute-done.1.refs_0_), channel_id=1, source_target_pairs={{0,4},{4,0},{8,12},{12,8},{1,5},{5,1},{9,13},{13,9},{2,6},{6,2},{1... | collective-permute-start | bytes 589832 | tf_op jit(solution)/shard_map/ppermute | solution.py:372
  17.7 3.4 %collective-permute-done.3.refs_0_ = bf16[64,1536]{1,0:T(8,128)(2,1)S(1)} collective-permute-done((bf16[64,1536]{1,0:T(8,128)(2,1)S(1)}, bf16[64,1536]{1,0:T(8,128)(2,1)S(1)}, u32[]{:S(2)}, u32[]{:S(2)}) %collective-permute-start.3) | collective-permute-done | bytes 196640 | tf_op jit(solution)/shard_map/ppermute | solution.py:372
  21.1 4.3 %loss_slope_turn.1 = (f32[8,64]{1,0:T(8,128)S(1)}, bf16[24,64,1024]{2,1,0:T(8,128)(2,1)S(1)}, bf16[1536,128]{1,0:T(8,128)(2,1)S(1)}) custom-call(bf16[64,1536]{1,0:T(8,128)(2,1)S(1)} %collective-permute-done.3.refs_0_, bf16[64,1536]{1,0:T(8,128)(2,1)S(1)} %pad_maximum_fusion.refs_0_.refs_1_, bf16[24,128,1024]{2,1,0:T(8,128)(2,1)S(1)} %get-tuple-element.15.refs_1_.refs_2_, ...), custom_call_target="tpu_custom_call" | custom-call | tf_op jit(solution)/shard_map/loss_slope_turn/pallas_call | solution.py:33
  25.4 0.0 collective-permute-done.2.refs_1_
  25.4 5.2 %loss.1 = f32[16,128]{1,0:T(8,128)S(1)} custom-call(bf16[64,1536]{1,0:T(8,128)(2,1)S(1)} %collective-permute-done.1.refs_0_, bf16[64,1536]{1,0:T(8,128)(2,1)S(1)} %collective-permute-done.2.refs_1_, bf16[24,128,1024]{2,1,0:T(8,128)(2,1)S(1)} %get-tuple-element.15.refs_1_.refs_2_, f32[1,1024]{1,0:T(1,128)S(1)} %get-tuple-element.16.refs_2_.refs_3_.refs_10_, ...), custom_call_target="tpu_custom_call" | custom-call | tf_op jit(solution)/shard_map/loss/pallas_call | solution.py:33
  30.6 0.0 collective-permute-start.4
  30.6 1.2 %collective-permute-done.4 = f32[16,128]{1,0:T(8,128)S(1)} collective-permute-done((f32[16,128]{1,0:T(8,128)S(1)}, f32[16,128]{1,0:T(8,128)S(1)}, u32[]{:S(2)}, u32[]{:S(2)}) %collective-permute-start.4) | collective-permute-done | bytes 8224 | tf_op jit(solution)/shard_map/ppermute | solution.py:393
  31.8 1.9 %collective-permute-start.7 = (f32[16,128]{1,0:T(8,128)S(1)}, f32[16,128]{1,0:T(8,128)S(1)}, u32[]{:S(2)}, u32[]{:S(2)}) collective-permute-start(f32[16,128]{1,0:T(8,128)S(1)} %add.11.refs_0_), channel_id=1, source_target_pairs={{0,12},{4,8},{8,4},{12,0},{1,13},{5,9},{9,5},{13,1},{2,14},{6,10},... | collective-permute-start | bytes 24584 | tf_op jit(solution)/shard_map/ppermute | solution.py:372
  33.7 0.0 collective-permute-start.6
  33.7 2.5 %collective-permute-start.5 = (f32[16,128]{1,0:T(8,128)S(1)}, f32[16,128]{1,0:T(8,128)S(1)}, u32[]{:S(2)}, u32[]{:S(2)}) collective-permute-start(f32[16,128]{1,0:T(8,128)S(1)} %add.11.refs_0_), channel_id=1, source_target_pairs={{0,4},{4,0},{8,12},{12,8},{1,5},{5,1},{9,13},{13,9},{2,6},{6,2},{1... | collective-permute-start | bytes 24584 | tf_op jit(solution)/shard_map/ppermute | solution.py:372
  36.2 3.9 %slope_turn.1 = (bf16[24,128,1024]{2,1,0:T(8,128)(2,1)S(1)}, bf16[1536,128]{1,0:T(8,128)(2,1)S(1)}) custom-call(bf16[64,1536]{1,0:T(8,128)(2,1)S(1)} %collective-permute-done.1.refs_0_, bf16[64,1536]{1,0:T(8,128)(2,1)S(1)} %collective-permute-done.2.refs_1_, bf16[24,128,1024]{2,1,0:T(8,128)(2,1)S(1)} %get-tuple-element.15.refs_1_.refs_2_, ...), custom_call_target="tpu_custom_call" | custom-call | tf_op jit(solution)/shard_map/slope_turn/pallas_call | solution.py:33
  40.1 0.0 collective-permute-done.7.refs_3_
  40.1 0.0 collective-permute-done.6.refs_2_
  40.2 0.0 collective-permute-done.5.refs_1_
  40.2 3.8 %gradient.1 = f32[16,8,128]{2,1,0:T(8,128)S(1)} custom-call(f32[16,128]{1,0:T(8,128)S(1)} %add.11.refs_0_, f32[16,128]{1,0:T(8,128)S(1)} %collective-permute-done.5.refs_1_, f32[16,128]{1,0:T(8,128)S(1)} %collective-permute-done.6.refs_2_, f32[16,128]{1,0:T(8,128)S(1)} %collective-permute-done.7.refs_3_, bf16[1536,128]{1,0:T(8,128)(2,1)S(1)} %get-tuple-element.21.refs_4_, ...), custom_call_target="tpu_custom_call" | custom-call | tf_op jit(solution)/shard_map/gradient/pallas_call | solution.py:33
  43.9 11.0 %all_to_all.5.parts_ref = f32[16,8,128]{2,1,0:T(8,128)S(1)} all-to-all(f32[16,8,128]{2,1,0:T(8,128)S(1)} %gradient.1), channel_id=1, replica_groups=mesh['groups'=2,'zone'=4,'scen'=2,'hour'=2] {'zone','scen','hour'}, dimensions={0} | all-to-all | bytes 131072 | tf_op jit(solution)/shard_map/all_to_all | solution.py:416
  54.9 0.9 %finish.1 = (f32[4,64]{1,0:T(4,128)}, f32[1]{0:T(128)}) custom-call(f32[16,8,128]{2,1,0:T(8,128)S(1)} %all_to_all.5.parts_ref), custom_call_target="tpu_custom_call" | custom-call | tf_op jit(solution)/shard_map/finish/pallas_call | solution.py:419
  (3 shorter events, 0.0 us)
Async XLA Ops:
  2.0 1.5 %collective-permute-start = (bf16[32,1536]{1,0:T(8,128)(2,1)S(1)}, bf16[32,1536]{1,0:T(8,128)(2,1)S(1)}, u32[]{:S(2)}, u32[]{:S(2)}) collective-permute-start(bf16[32,1536]{1,0:T(8,128)(2,1)S(1)} %get-tuple-element.29), channel_id=1, source_target_pairs={{0,1},{1,0},{2,3},{3,2},{4,5},{5,4},{6,7},{7,6},{8,9},{9,8},{10,11... | collective-permute-start | bytes 294920 | tf_op jit(solution)/shard_map/ppermute | solution.py:368
  3.5 13.5 %collective-permute-start.1 = (bf16[64,1536]{1,0:T(8,128)(2,1)S(1)}, bf16[64,1536]{1,0:T(8,128)(2,1)S(1)}, u32[]{:S(2)}, u32[]{:S(2)}) collective-permute-start(bf16[64,1536]{1,0:T(8,128)(2,1)S(1)} %pad_maximum_fusion.refs_0_.refs_1_), channel_id=1, source_target_pairs={{0,8},{4,12},{8,0},{12,4},{1,9},{5,13},{9,1},{13,5},{2,10},{6,14},... | collective-permute-start | bytes 589832 | tf_op jit(solution)/shard_map/ppermute | solution.py:372
  10.8 10.3 %collective-permute-start.3 = (bf16[64,1536]{1,0:T(8,128)(2,1)S(1)}, bf16[64,1536]{1,0:T(8,128)(2,1)S(1)}, u32[]{:S(2)}, u32[]{:S(2)}) collective-permute-start(bf16[64,1536]{1,0:T(8,128)(2,1)S(1)} %pad_maximum_fusion.refs_0_.refs_1_), channel_id=1, source_target_pairs={{0,4},{4,0},{8,12},{12,8},{1,5},{5,1},{9,13},{13,9},{2,6},{6,2},{1... | collective-permute-start | bytes 589832 | tf_op jit(solution)/shard_map/ppermute | solution.py:372
  17.0 8.4 %collective-permute-start.2 = (bf16[64,1536]{1,0:T(8,128)(2,1)S(1)}, bf16[64,1536]{1,0:T(8,128)(2,1)S(1)}, u32[]{:S(2)}, u32[]{:S(2)}) collective-permute-start(bf16[64,1536]{1,0:T(8,128)(2,1)S(1)} %collective-permute-done.1.refs_0_), channel_id=1, source_target_pairs={{0,4},{4,0},{8,12},{12,8},{1,5},{5,1},{9,13},{13,9},{2,6},{6,2},{1... | collective-permute-start | bytes 589832 | tf_op jit(solution)/shard_map/ppermute | solution.py:372
  30.6 1.2 %collective-permute-start.4 = (f32[16,128]{1,0:T(8,128)S(1)}, f32[16,128]{1,0:T(8,128)S(1)}, u32[]{:S(2)}, u32[]{:S(2)}) collective-permute-start(f32[16,128]{1,0:T(8,128)S(1)} %loss.1), channel_id=1, source_target_pairs={{0,1},{1,0},{2,3},{3,2},{4,5},{5,4},{6,7},{7,6},{8,9},{9,8},{10,11... | collective-permute-start | bytes 24584 | tf_op jit(solution)/shard_map/ppermute | solution.py:393
  31.8 8.3 %collective-permute-start.7 = (f32[16,128]{1,0:T(8,128)S(1)}, f32[16,128]{1,0:T(8,128)S(1)}, u32[]{:S(2)}, u32[]{:S(2)}) collective-permute-start(f32[16,128]{1,0:T(8,128)S(1)} %add.11.refs_0_), channel_id=1, source_target_pairs={{0,12},{4,8},{8,4},{12,0},{1,13},{5,9},{9,5},{13,1},{2,14},{6,10},... | collective-permute-start | bytes 24584 | tf_op jit(solution)/shard_map/ppermute | solution.py:372
  33.7 6.4 %collective-permute-start.6 = (f32[16,128]{1,0:T(8,128)S(1)}, f32[16,128]{1,0:T(8,128)S(1)}, u32[]{:S(2)}, u32[]{:S(2)}) collective-permute-start(f32[16,128]{1,0:T(8,128)S(1)} %add.11.refs_0_), channel_id=1, source_target_pairs={{0,8},{4,12},{8,0},{12,4},{1,9},{5,13},{9,1},{13,5},{2,10},{6,14},... | collective-permute-start | bytes 24584 | tf_op jit(solution)/shard_map/ppermute | solution.py:372
  33.7 6.4 %collective-permute-start.5 = (f32[16,128]{1,0:T(8,128)S(1)}, f32[16,128]{1,0:T(8,128)S(1)}, u32[]{:S(2)}, u32[]{:S(2)}) collective-permute-start(f32[16,128]{1,0:T(8,128)S(1)} %add.11.refs_0_), channel_id=1, source_target_pairs={{0,4},{4,0},{8,12},{12,8},{1,5},{5,1},{9,13},{13,9},{2,6},{6,2},{1... | collective-permute-start | bytes 24584 | tf_op jit(solution)/shard_map/ppermute | solution.py:372

commit v5 on v4

--- a/solution.py
+++ b/solution.py
@@ -99,17 +99,21 @@
     extra = lax.broadcasted_iota(jnp.int32, (16, zones), 0)
     blank = jnp.zeros((DEPTH - width - 16, zones), BF16)
 
-    def hour_step(h, carry):
-        rhs_ref[h, :width, :] = (resp_ref[h].astype(F32) * zp_ref[...]).astype(BF16)
-        middle = 0.25 * (band_ref[pl.ds(h, 1), :].astype(F32) - 3.5)
-        tail = jnp.where(extra == 0, -middle, jnp.where(extra == 1, 1.0, 0.0))
-        rhs_ref[h, width : width + 16, :] = tail.astype(BF16)
-        rhs_ref[h, width + 16 :, :] = blank
+    def pair_step(j, carry):
+        for k in range(2):
+            h = 2 * j + k
+            at = k * DEPTH
+            coeff = resp_ref[h].astype(F32) * zp_ref[...]
+            rhs_ref[j, at : at + width, :] = coeff.astype(BF16)
+            middle = 0.25 * (band_ref[pl.ds(h, 1), :].astype(F32) - 3.5)
+            tail = jnp.where(extra == 0, -middle, jnp.where(extra == 1, 1.0, 0.0))
+            rhs_ref[j, at + width : at + width + 16, :] = tail.astype(BF16)
+            rhs_ref[j, at + width + 16 : at + DEPTH, :] = blank
         return carry
 
     for i in range(pieces):
         large[i].wait()
-        lax.fori_loop(i * span, (i + 1) * span, hour_step, 0)
+        lax.fori_loop(i * span // 2, (i + 1) * span // 2, pair_step, 0)
 
 
 def coefficients(building_map, owner_ids, window_params, band_ids, floor_area, response):
@@ -123,7 +127,7 @@
         response,
     ]
     outs = [
-        ((hours, DEPTH, zones), BF16),
+        ((hours // 2, 2 * DEPTH, zones), BF16),
         ((1, zones), jnp.int32),
         ((1, zones), F32),
         (response.shape, BF16),
@@ -180,7 +184,8 @@
     if with_loss:
         acc_ref = refs[0]
         acc_ref[...] = jnp.zeros_like(acc_ref)
-    hours, _, zones = rhs_ref.shape
+    pairs, _, zones = rhs_ref.shape
+    hours = 2 * pairs
     core, me = here()
 
     def rows_of(parts, at):
@@ -192,37 +197,42 @@
         pair = rows_of(f_refs, at)
         if with_turn:
             ft_ref[at, :] = rows_of(turn_refs, at).T
-        gathered = None
-        for k in range(2):
-            h = 2 * j + k
+        rows = pair.shape[0]
+        fill = (1.0,) if with_loss else (0.5, 0.25)
+        if not with_loss:
+            pair = (pair.astype(F32) * 0.5).astype(BF16)
+        none = jnp.zeros(pair.shape, BF16)
+        lhs = jnp.concatenate(
+            [
+                jnp.concatenate([drivers(pair, False, fill), none], axis=1),
+                jnp.concatenate([none, drivers(pair, True, fill)], axis=1),
+            ],
+            axis=0,
+        )
+        summed = None
+        for z in range(0, zones, ZONE_TILE):
+            v = jnp.dot(lhs, rhs_ref[j, :, z : z + ZONE_TILE], preferred_element_type=F32)
             if with_loss:
-                lhs = drivers(pair, k == 1, (1.0,))
-                occ = occupancy(core * hours + h, hours_total)
-            else:
-                lhs = drivers((pair.astype(F32) * 0.5).astype(BF16), k == 1, (0.5, 0.25))
-            summed = None
-            for z in range(0, zones, ZONE_TILE):
-                v = jnp.dot(lhs, rhs_ref[h, :, z : z + ZONE_TILE], preferred_element_type=F32)
-                if with_loss:
-                    a = jnp.abs(v) * MINUS_LOG2_E
-                    q = jnp.exp2(a)
-                    pen = jnp.log2((q + EDGE) * q + 1.0) - a
-                    pen = pen * area_ref[:, z : z + ZONE_TILE]
-                    for c in range(0, ZONE_TILE, LANES):
-                        piece = pen[:, c : c + LANES]
-                        summed = piece if summed is None else summed + piece
-                if with_slope:
-                    x = v * 0.5 + 0.25 if with_loss else v
-                    slope = jnp.tanh(x) + jnp.tanh(x - 0.5)
-                    slope_ref[h, :, z : z + ZONE_TILE] = slope.astype(BF16)
-            if with_loss:
-                summed = summed * occ
-                gathered = summed if gathered is None else gathered + summed
+                a = jnp.abs(v) * MINUS_LOG2_E
+                q = jnp.exp2(a)
+                pen = jnp.log2((q + EDGE) * q + 1.0) - a
+                pen = pen * area_ref[:, z : z + ZONE_TILE]
+                for c in range(0, ZONE_TILE, LANES):
+                    piece = pen[:, c : c + LANES]
+                    summed = piece if summed is None else summed + piece
+            if with_slope:
+                x = v * 0.5 + 0.25 if with_loss else v
+                slope = (jnp.tanh(x) + jnp.tanh(x - 0.5)).astype(BF16)
+                slope_ref[2 * j, :, z : z + ZONE_TILE] = slope[:rows]
+                slope_ref[2 * j + 1, :, z : z + ZONE_TILE] = slope[rows:]
         if with_loss:
-            acc_ref[...] += gathered
+            first = core * hours + 2 * j
+            acc_ref[...] += summed[:rows] * occupancy(first, hours_total) + summed[
+                rows:
+            ] * occupancy(first + 1, hours_total)
         return carry
 
-    lax.fori_loop(0, hours // 2, pair_step, 0, unroll=unroll)
+    lax.fori_loop(0, pairs, pair_step, 0, unroll=unroll)
 
     if with_loss:
         row = jnp.sum(acc_ref[...].T, axis=0, keepdims=True)
@@ -250,7 +260,7 @@
 
 
 def scan(kind, rows_in, rhs, area, hours_total, sources, extra=(), priors=(), unroll=4, cost=None):
-    hours, _, zones = rhs.shape
+    hours, zones = 2 * rhs.shape[0], rhs.shape[2]
     rows = sum(f.shape[0] for f in rows_in)
     outs = []
     scratch = []
@@ -296,9 +306,11 @@
     e = jnp.where(valid, jnp.exp(jnp.where(valid, score - peak, 0.0)), 0.0)
     exp_total = jnp.sum(e)
     score_ref[...] = e
-    for m in range(sources):
+    quarter = sources // 4
+    order = [q * quarter + m for q in (1, 2, 0, 3) for m in range(quarter)]
+    for spot, m in enumerate(order):
         piece = score_ref[pl.ds(me ^ m, 1), :]
-        e_ref[:, m * chunk : (m + 1) * chunk] = piece[:, :chunk]
+        e_ref[:, spot * chunk : (spot + 1) * chunk] = piece[:, :chunk]
     acc_ref[...] = jnp.zeros_like(acc_ref)
 
     def hour_step(h, carry):
@@ -366,36 +378,46 @@
     keep = lax.dynamic_slice_in_dim(everyone, core * half, half, axis=1)
     leave = lax.dynamic_slice_in_dim(everyone, (1 - core) * half, half, axis=1)
     came = lax.ppermute(leave, "hour", [(0, 1), (1, 0)])
-    mine = jnp.concatenate([keep, came], axis=0)
+
+    def across(x, m):
+        return lax.ppermute(x, ("zone", "hour"), [(i, i ^ m) for i in range(sources)])
 
     def swap(x, step):
         return lax.ppermute(x, "zone", [(i, i ^ step) for i in range(zone_parts)])
 
+    came, building_map = lax.optimization_barrier((came, building_map))
     rhs, plan, area, near_response = coefficients(
         building_map, owner_ids, window_params, band_ids, floor_area, response
     )
-    common = (rhs, area, hours_total, sources)
     if zone_parts == 4:
-        far = swap(mine, 2)
-        beside = swap(mine, 1)
-        loss0, slope0 = scan("loss_slope", [mine], *common, cost=SHORT)
-        far, loss0 = lax.optimization_barrier((far, loss0))
-        last = [far, swap(far, 1)]
+        far0, far1 = across(keep, 4), across(leave, 5)
+        near0, near1 = across(keep, 2), across(leave, 3)
+        mine = [keep, came]
     else:
         me = lax.axis_index(("zone", "hour"))
         both = jnp.where(core == 0, jnp.stack([keep, came]), jnp.stack([came, keep]))
         gathered = lax.all_gather(both, "zone", axis=0, tiled=True)
         ordered = jnp.take(gathered, me ^ jnp.arange(sources), axis=0).reshape(4, -1, half)
-        mine, beside, last = ordered[0], ordered[1], [ordered[2], ordered[3]]
-        loss0, slope0 = scan("loss_slope", [mine], *common)
-    loss1, slope1, ft0 = scan("loss_slope_turn", [beside], *common, extra=[mine])
-    (message,) = scan("loss", last, *common, priors=[loss0, loss1], unroll=6)
+        mine, beside, far, last = [ordered[0]], ordered[1], ordered[2], ordered[3]
+    common = (rhs, area, hours_total, sources)
+    loss0, slope0 = scan("loss_slope", mine, *common, cost=SHORT)
+    if zone_parts == 4:
+        near0, near1, far0, far1, loss0 = lax.optimization_barrier(
+            (near0, near1, far0, far1, loss0)
+        )
+        beside = jnp.concatenate([near0, near1], axis=0)
+        far = jnp.concatenate([far0, far1], axis=0)
+        last = swap(far, 1)
+    loss1, slope1, ft1 = scan("loss_slope_turn", [beside, far], *common)
+    (message,) = scan("loss", [last], *common, priors=[loss0, loss1])
     message = message + lax.ppermute(message, "hour", [(0, 1), (1, 0)])
+    slope2, ft2 = scan("slope_turn", [last], *common, extra=mine)
     if zone_parts == 4:
-        messages = [message] + [swap(message, k) for k in (1, 2, 3)]
+        others = [swap(message, k) for k in (1, 2, 3)]
+        *others, slope2 = lax.optimization_barrier((*others, slope2))
+        messages = [message, *others]
     else:
         messages = [lax.psum(message, "zone")]
-    slope2, ft1 = scan("slope_turn", last, *common)
 
     designs = window_params.shape[0]
     devices = zone_parts * scen_parts * hour_parts
@@ -406,11 +428,11 @@
         functools.partial(gradient_kernel, hours_total, gain, owners, sources, len(messages)),
         "gradient",
         [((devices, pad, LANES), F32)],
-        [*messages, ft0, ft1, slope0, slope1, slope2, near_response, area, plan],
+        [*messages, ft1, ft2, slope1, slope0, slope2, near_response, area, plan],
         [
             pltpu.VMEM((width, zones), F32),
             pltpu.VMEM(message.shape, F32),
-            pltpu.VMEM((1, ft0.shape[1] + ft1.shape[1]), F32),
+            pltpu.VMEM((1, ft1.shape[1] + ft2.shape[1]), F32),
         ],
     )
     parts = lax.all_to_all(

time: 56 us -> 54.5 us (0.973)
    ppermute x6 -> x4, starting transfers between devices: 10.7 us -> 4.92 us  [swap(): return lax.ppermute(x, 'zone', [(i, i ^ step) for i in range(zone_parts)])]
    ppermute x0 -> x4, starting transfers between devices: none -> 5.48 us  [across(): lax.ppermute(x, ('zone', 'hour'), [(i, i ^ m) for i in range(sources)])]
    ppermute x0 -> x4, waiting for transfers between devices: none -> 2.44 us  [across(): lax.ppermute(x, ('zone', 'hour'), [(i, i ^ m) for i in range(sources)])]
    ppermute x6 -> x4, waiting for transfers between devices: 3.7 us -> 1.66 us  [swap(): return lax.ppermute(x, 'zone', [(i, i ^ step) for i in range(zone_parts)])]
    ppermute x1, waiting for transfers between devices: 0.94 us -> 0.01 us  [on_device(): came = lax.ppermute(leave, 'hour', [(0, 1), (1, 0)])]
  transfers between devices with their start and end apart: 8 -> 10, of which waited for: 4 -> 3; matrix products, arithmetic and copies ran while one was open for 0% -> 0% of each run, Pallas kernels for 28% -> 33%
where the time goes in v5:
time: 54.5 us; the launch traced here: 54.2 us
  Pallas kernels  25.4 us (47%)
  starting transfers between devices  10.9 us (20%)
  blocking collectives  10.5 us (19%)
  waiting for transfers between devices  5.26 us (10%)
  local copies, waits for them, and re-layouts  1.35 us (2%)
  between operations  0.76 us (1%)
    pallas_call x5, Pallas kernels, call(): pl.pallas_call(kernel, in_specs=[VMEM] * len(args), out_specs=[VMEM] * le...  21.2 us
    all_to_all x1, blocking collectives, on_device(): lax.all_to_all(parts, ('zone', 'scen', 'hour'), split_axis=0, concat_axis...  10.5 us
    ppermute x4, starting transfers between devices, across(): lax.ppermute(x, ('zone', 'hour'), [(i, i ^ m) for i in range(sources)])  5.48 us
    ppermute x4, starting transfers between devices, swap(): return lax.ppermute(x, 'zone', [(i, i ^ step) for i in range(zone_parts)])  4.92 us
    pallas_call x1, Pallas kernels, coefficients(): pl.pallas_call(coeff_kernel, in_specs=[pl.BlockSpec(memory_space=pl.ANY)]...  3.22 us
    ppermute x4, waiting for transfers between devices, across(): lax.ppermute(x, ('zone', 'hour'), [(i, i ^ m) for i in range(sources)])  2.44 us
    ppermute x4, waiting for transfers between devices, swap(): return lax.ppermute(x, 'zone', [(i, i ^ step) for i in range(zone_parts)])  1.66 us
    reshape x1, local copies, waits for them, and re-layouts, on_device(): everyone = forcing.reshape(forcing.shape[0], hours_total * width)  1.32 us
  transfers between devices with their start and end apart: 10, of which 3 were waited for; matrix products, arithmetic and copies ran while one was open for 0% of the time, Pallas kernels for 33%

profile of v5, /device:TPU:0, one launch (start us, length us, event | category | flops | bytes accessed | tf_op | source)
XLA Modules:
  0.0 54.2 jit_solution(6670060761855599342)
XLA Ops:
  0.6 1.3 %reshape.16 = bf16[32,3072]{1,0:T(8,128)(2,1)S(1)} reshape(bf16[32,48,64]{2,1,0:T(8,128)(2,1)} %param.7) | data formatting | bytes 393216 | tf_op jit(solution)/shard_map/reshape | solution.py:377
  2.0 0.5 collective-permute-start.4
  2.5 2.6 %collective-permute-start = (bf16[32,1536]{1,0:T(8,128)(2,1)S(1)}, bf16[32,1536]{1,0:T(8,128)(2,1)S(1)}, u32[]{:S(2)}, u32[]{:S(2)}) collective-permute-start(bf16[32,1536]{1,0:T(8,128)(2,1)S(1)} %get-tuple-element.47.refs_0_.refs_1_), channel_id=1, source_target_pairs={{0,4},{1,5},{4,0},{5,1},{8,12},{9,13},{12,8},{13,9},{2,6},{3,7},{6... | collective-permute-start | bytes 294920 | tf_op jit(solution)/shard_map/ppermute | solution.py:383
  5.1 0.1 collective-permute-start.1
  5.2 2.8 %collective-permute-start.2 = (bf16[32,1536]{1,0:T(8,128)(2,1)S(1)}, bf16[32,1536]{1,0:T(8,128)(2,1)S(1)}, u32[]{:S(2)}, u32[]{:S(2)}) collective-permute-start(bf16[32,1536]{1,0:T(8,128)(2,1)S(1)} %get-tuple-element.47.refs_0_.refs_1_), channel_id=1, source_target_pairs={{0,8},{1,9},{4,12},{5,13},{8,0},{9,1},{12,4},{13,5},{2,10},{3,11},... | collective-permute-start | bytes 294920 | tf_op jit(solution)/shard_map/ppermute | solution.py:383
  8.0 0.0 collective-permute-start.3
  8.0 0.0 collective-permute-done.4.refs_1_.refs_2_
  8.0 3.2 %coefficients.1 = (bf16[12,256,1024]{2,1,0:T(8,128)(2,1)S(1)}, s32[1,1024]{1,0:T(1,128)S(1)}, f32[1,1024]{1,0:T(1,128)S(1)}, bf16[24,64,1024]{2,1,0:T(8,128)(2,1)S(1)}) custom-call(s32[8,128]{1,0:T(8,128)} %bitcast.3, s32[8,128]{1,0:T(8,128)} %bitcast.4, f32[64,64]{1,0:T(8,128)} %wp_hbm.1, s32[24,1024]{1,0:T(8,128)} %band_hbm.1, f32[1,1024]{1,0:T(1,128)} %bitcast.5, ...), custom_call_target="tpu_custom_call" | custom-call | flops 1 | bytes 1 | tf_op jit(solution)/shard_map/coefficients/pallas_call | solution.py:135
  11.2 4.3 %loss_slope.1 = (f32[8,64]{1,0:T(8,128)S(1)}, bf16[24,64,1024]{2,1,0:T(8,128)(2,1)S(1)}) custom-call(bf16[32,1536]{1,0:T(8,128)(2,1)S(1)} %get-tuple-element.47.refs_0_.refs_1_, bf16[32,1536]{1,0:T(8,128)(2,1)S(1)} %collective-permute-done.4.refs_1_.refs_2_, bf16[12,256,1024]{2,1,0:T(8,128)(2,1)S(1)} %get-tuple-element.26.refs_2_.refs_1_.refs_3_, ...), custom_call_target="tpu_custom_call" | custom-call | flops 1 | bytes 1 | tf_op jit(solution)/shard_map/loss_slope/pallas_call | solution.py:33
  15.5 0.0 collective-permute-done
  15.5 0.0 collective-permute-done.1
  15.5 0.0 collective-permute-done.2
  15.5 2.4 %collective-permute-done.3 = bf16[32,1536]{1,0:T(8,128)(2,1)S(1)} collective-permute-done((bf16[32,1536]{1,0:T(8,128)(2,1)S(1)}, bf16[32,1536]{1,0:T(8,128)(2,1)S(1)}, u32[]{:S(2)}, u32[]{:S(2)}) %collective-permute-start.3) | collective-permute-done | bytes 98336 | tf_op jit(solution)/shard_map/ppermute | solution.py:383
  18.0 0.5 collective-permute-start.5
  18.5 7.9 %loss_slope_turn.1 = (f32[8,128]{1,0:T(8,128)S(1)}, bf16[24,128,1024]{2,1,0:T(8,128)(2,1)S(1)}, bf16[1536,128]{1,0:T(8,128)(2,1)S(1)}) custom-call(bf16[64,1536]{1,0:T(8,128)(2,1)S(1)} %pad_maximum_fusion.refs_0_, bf16[64,1536]{1,0:T(8,128)(2,1)S(1)} %constant_dynamic-update-slice_fusion.refs_1_, ...), custom_call_target="tpu_custom_call" | custom-call | tf_op jit(solution)/shard_map/loss_slope_turn/pallas_call | solution.py:33
  26.4 0.0 collective-permute-done.5.refs_0_
  26.4 3.1 %loss.1 = f32[16,128]{1,0:T(8,128)S(1)} custom-call(bf16[64,1536]{1,0:T(8,128)(2,1)S(1)} %collective-permute-done.5.refs_0_, bf16[12,256,1024]{2,1,0:T(8,128)(2,1)S(1)} %get-tuple-element.26.refs_2_.refs_1_.refs_3_, f32[1,1024]{1,0:T(1,128)S(1)} %get-tuple-element.27.refs_3_.refs_2_.refs_4_.refs_10_, f32[8,64]{1,0:T(8,128)S(1)} %get-tuple-element.31.refs_3_, ...), custom_call_target="tpu_custom_call" | custom-call | tf_op jit(solution)/shard_map/loss/pallas_call | solution.py:33
  29.5 0.0 collective-permute-start.6
  29.6 1.2 %collective-permute-done.6 = f32[16,128]{1,0:T(8,128)S(1)} collective-permute-done((f32[16,128]{1,0:T(8,128)S(1)}, f32[16,128]{1,0:T(8,128)S(1)}, u32[]{:S(2)}, u32[]{:S(2)}) %collective-permute-start.6) | collective-permute-done | bytes 8224 | tf_op jit(solution)/shard_map/ppermute | solution.py:413
  30.7 1.6 %collective-permute-start.7 = (f32[16,128]{1,0:T(8,128)S(1)}, f32[16,128]{1,0:T(8,128)S(1)}, u32[]{:S(2)}, u32[]{:S(2)}) collective-permute-start(f32[16,128]{1,0:T(8,128)S(1)} %add.11.refs_0_), channel_id=1, source_target_pairs={{0,4},{4,0},{8,12},{12,8},{1,5},{5,1},{9,13},{13,9},{2,6},{6,2},{1... | collective-permute-start | bytes 24584 | tf_op jit(solution)/shard_map/ppermute | solution.py:386
  32.3 1.3 %collective-permute-start.8 = (f32[16,128]{1,0:T(8,128)S(1)}, f32[16,128]{1,0:T(8,128)S(1)}, u32[]{:S(2)}, u32[]{:S(2)}) collective-permute-start(f32[16,128]{1,0:T(8,128)S(1)} %add.11.refs_0_), channel_id=1, source_target_pairs={{0,8},{4,12},{8,0},{12,4},{1,9},{5,13},{9,1},{13,5},{2,10},{6,14},... | collective-permute-start | bytes 24584 | tf_op jit(solution)/shard_map/ppermute | solution.py:386
  33.6 1.5 %collective-permute-start.9 = (f32[16,128]{1,0:T(8,128)S(1)}, f32[16,128]{1,0:T(8,128)S(1)}, u32[]{:S(2)}, u32[]{:S(2)}) collective-permute-start(f32[16,128]{1,0:T(8,128)S(1)} %add.11.refs_0_), channel_id=1, source_target_pairs={{0,12},{4,8},{8,4},{12,0},{1,13},{5,9},{9,5},{13,1},{2,14},{6,10},... | collective-permute-start | bytes 24584 | tf_op jit(solution)/shard_map/ppermute | solution.py:386
  35.1 2.3 %slope_turn.1 = (bf16[24,64,1024]{2,1,0:T(8,128)(2,1)S(1)}, bf16[1536,128]{1,0:T(8,128)(2,1)S(1)}) custom-call(bf16[64,1536]{1,0:T(8,128)(2,1)S(1)} %collective-permute-done.5.refs_0_, bf16[32,1536]{1,0:T(8,128)(2,1)S(1)} %get-tuple-element.47.refs_0_.refs_1_, bf16[32,1536]{1,0:T(8,128)(2,1)S(1)} %collective-permute-done.4.refs_1_.refs_2_, ...), custom_call_target="tpu_custom_call" | custom-call | tf_op jit(solution)/shard_map/slope_turn/pallas_call | solution.py:33
  37.4 0.0 collective-permute-done.7.refs_1_
  37.4 0.0 collective-permute-done.8.refs_2_
  37.4 1.7 %collective-permute-done.9.refs_3_ = f32[16,128]{1,0:T(8,128)S(1)} collective-permute-done((f32[16,128]{1,0:T(8,128)S(1)}, f32[16,128]{1,0:T(8,128)S(1)}, u32[]{:S(2)}, u32[]{:S(2)}) %collective-permute-start.9) | collective-permute-done | bytes 8224 | tf_op jit(solution)/shard_map/ppermute | solution.py:386
  39.1 3.7 %gradient.1 = f32[16,8,128]{2,1,0:T(8,128)S(1)} custom-call(f32[16,128]{1,0:T(8,128)S(1)} %add.11.refs_0_, f32[16,128]{1,0:T(8,128)S(1)} %collective-permute-done.7.refs_1_, f32[16,128]{1,0:T(8,128)S(1)} %collective-permute-done.8.refs_2_, f32[16,128]{1,0:T(8,128)S(1)} %collective-permute-done.9.refs_3_, bf16[1536,128]{1,0:T(8,128)(2,1)S(1)} %get-tuple-element.39.refs_4_, ...), custom_call_target="tpu_custom_call" | custom-call | tf_op jit(solution)/shard_map/gradient/pallas_call | solution.py:33
  42.8 10.5 %all_to_all.5.parts_ref = f32[16,8,128]{2,1,0:T(8,128)S(1)} all-to-all(f32[16,8,128]{2,1,0:T(8,128)S(1)} %gradient.1), channel_id=1, replica_groups=mesh['groups'=2,'zone'=4,'scen'=2,'hour'=2] {'zone','scen','hour'}, dimensions={0} | all-to-all | bytes 131072 | tf_op jit(solution)/shard_map/all_to_all | solution.py:438
  53.3 0.9 %finish.1 = (f32[4,64]{1,0:T(4,128)}, f32[1]{0:T(128)}) custom-call(f32[16,8,128]{2,1,0:T(8,128)S(1)} %all_to_all.5.parts_ref), custom_call_target="tpu_custom_call" | custom-call | tf_op jit(solution)/shard_map/finish/pallas_call | solution.py:441
  (5 shorter events, 0.1 us)
Async XLA Ops:
  2.0 6.0 %collective-permute-start.4 = (bf16[32,1536]{1,0:T(8,128)(2,1)S(1)}, bf16[32,1536]{1,0:T(8,128)(2,1)S(1)}, u32[]{:S(2)}, u32[]{:S(2)}) collective-permute-start(bf16[32,1536]{1,0:T(8,128)(2,1)S(1)} %get-tuple-element.46), channel_id=1, source_target_pairs={{0,1},{1,0},{2,3},{3,2},{4,5},{5,4},{6,7},{7,6},{8,9},{9,8},{10,11... | collective-permute-start | bytes 294920 | tf_op jit(solution)/shard_map/ppermute | solution.py:380
  2.5 13.0 %collective-permute-start = (bf16[32,1536]{1,0:T(8,128)(2,1)S(1)}, bf16[32,1536]{1,0:T(8,128)(2,1)S(1)}, u32[]{:S(2)}, u32[]{:S(2)}) collective-permute-start(bf16[32,1536]{1,0:T(8,128)(2,1)S(1)} %get-tuple-element.47.refs_0_.refs_1_), channel_id=1, source_target_pairs={{0,4},{1,5},{4,0},{5,1},{8,12},{9,13},{12,8},{13,9},{2,6},{3,7},{6... | collective-permute-start | bytes 294920 | tf_op jit(solution)/shard_map/ppermute | solution.py:383
  5.1 10.4 %collective-permute-start.1 = (bf16[32,1536]{1,0:T(8,128)(2,1)S(1)}, bf16[32,1536]{1,0:T(8,128)(2,1)S(1)}, u32[]{:S(2)}, u32[]{:S(2)}) collective-permute-start(bf16[32,1536]{1,0:T(8,128)(2,1)S(1)} %get-tuple-element.46), channel_id=1, source_target_pairs={{0,5},{1,4},{4,1},{5,0},{8,13},{9,12},{12,9},{13,8},{2,7},{3,6},{6... | collective-permute-start | bytes 294920 | tf_op jit(solution)/shard_map/ppermute | solution.py:383
  5.2 10.3 %collective-permute-start.2 = (bf16[32,1536]{1,0:T(8,128)(2,1)S(1)}, bf16[32,1536]{1,0:T(8,128)(2,1)S(1)}, u32[]{:S(2)}, u32[]{:S(2)}) collective-permute-start(bf16[32,1536]{1,0:T(8,128)(2,1)S(1)} %get-tuple-element.47.refs_0_.refs_1_), channel_id=1, source_target_pairs={{0,8},{1,9},{4,12},{5,13},{8,0},{9,1},{12,4},{13,5},{2,10},{3,11},... | collective-permute-start | bytes 294920 | tf_op jit(solution)/shard_map/ppermute | solution.py:383
  8.0 10.0 %collective-permute-start.3 = (bf16[32,1536]{1,0:T(8,128)(2,1)S(1)}, bf16[32,1536]{1,0:T(8,128)(2,1)S(1)}, u32[]{:S(2)}, u32[]{:S(2)}) collective-permute-start(bf16[32,1536]{1,0:T(8,128)(2,1)S(1)} %get-tuple-element.46), channel_id=1, source_target_pairs={{0,9},{1,8},{4,13},{5,12},{8,1},{9,0},{12,5},{13,4},{2,11},{3,10},... | collective-permute-start | bytes 294920 | tf_op jit(solution)/shard_map/ppermute | solution.py:383
  18.0 8.4 %collective-permute-start.5 = (bf16[64,1536]{1,0:T(8,128)(2,1)S(1)}, bf16[64,1536]{1,0:T(8,128)(2,1)S(1)}, u32[]{:S(2)}, u32[]{:S(2)}) collective-permute-start(bf16[64,1536]{1,0:T(8,128)(2,1)S(1)} %constant_dynamic-update-slice_fusion.refs_1_), channel_id=1, source_target_pairs={{0,4},{4,0},{8,12},{12,8},{1,5},{5,1},{9,13},{13,9},{2,6},{6,2},{1... | collective-permute-start | bytes 589832 | tf_op jit(solution)/shard_map/ppermute | solution.py:386
  29.5 1.2 %collective-permute-start.6 = (f32[16,128]{1,0:T(8,128)S(1)}, f32[16,128]{1,0:T(8,128)S(1)}, u32[]{:S(2)}, u32[]{:S(2)}) collective-permute-start(f32[16,128]{1,0:T(8,128)S(1)} %loss.1), channel_id=1, source_target_pairs={{0,1},{1,0},{2,3},{3,2},{4,5},{5,4},{6,7},{7,6},{8,9},{9,8},{10,11... | collective-permute-start | bytes 24584 | tf_op jit(solution)/shard_map/ppermute | solution.py:413
  30.7 6.7 %collective-permute-start.7 = (f32[16,128]{1,0:T(8,128)S(1)}, f32[16,128]{1,0:T(8,128)S(1)}, u32[]{:S(2)}, u32[]{:S(2)}) collective-permute-start(f32[16,128]{1,0:T(8,128)S(1)} %add.11.refs_0_), channel_id=1, source_target_pairs={{0,4},{4,0},{8,12},{12,8},{1,5},{5,1},{9,13},{13,9},{2,6},{6,2},{1... | collective-permute-start | bytes 24584 | tf_op jit(solution)/shard_map/ppermute | solution.py:386
  32.3 5.1 %collective-permute-start.8 = (f32[16,128]{1,0:T(8,128)S(1)}, f32[16,128]{1,0:T(8,128)S(1)}, u32[]{:S(2)}, u32[]{:S(2)}) collective-permute-start(f32[16,128]{1,0:T(8,128)S(1)} %add.11.refs_0_), channel_id=1, source_target_pairs={{0,8},{4,12},{8,0},{12,4},{1,9},{5,13},{9,1},{13,5},{2,10},{6,14},... | collective-permute-start | bytes 24584 | tf_op jit(solution)/shard_map/ppermute | solution.py:386
  33.6 5.4 %collective-permute-start.9 = (f32[16,128]{1,0:T(8,128)S(1)}, f32[16,128]{1,0:T(8,128)S(1)}, u32[]{:S(2)}, u32[]{:S(2)}) collective-permute-start(f32[16,128]{1,0:T(8,128)S(1)} %add.11.refs_0_), channel_id=1, source_target_pairs={{0,12},{4,8},{8,4},{12,0},{1,13},{5,9},{9,5},{13,1},{2,14},{6,10},... | collective-permute-start | bytes 24584 | tf_op jit(solution)/shard_map/ppermute | solution.py:386

commit v6 on v5

--- a/solution.py
+++ b/solution.py
@@ -113,7 +113,7 @@
 
     for i in range(pieces):
         large[i].wait()
-        lax.fori_loop(i * span // 2, (i + 1) * span // 2, pair_step, 0)
+        lax.fori_loop(i * span // 2, (i + 1) * span // 2, pair_step, 0, unroll=span // 2)
 
 
 def coefficients(building_map, owner_ids, window_params, band_ids, floor_area, response):
@@ -198,9 +198,8 @@
         if with_turn:
             ft_ref[at, :] = rows_of(turn_refs, at).T
         rows = pair.shape[0]
-        fill = (1.0,) if with_loss else (0.5, 0.25)
-        if not with_loss:
-            pair = (pair.astype(F32) * 0.5).astype(BF16)
+        fill = (0.5,) if with_loss else (0.5, 0.25)
+        pair = (pair.astype(F32) * 0.5).astype(BF16)
         none = jnp.zeros(pair.shape, BF16)
         lhs = jnp.concatenate(
             [
@@ -213,7 +212,7 @@
         for z in range(0, zones, ZONE_TILE):
             v = jnp.dot(lhs, rhs_ref[j, :, z : z + ZONE_TILE], preferred_element_type=F32)
             if with_loss:
-                a = jnp.abs(v) * MINUS_LOG2_E
+                a = jnp.abs(v) * (2.0 * MINUS_LOG2_E)
                 q = jnp.exp2(a)
                 pen = jnp.log2((q + EDGE) * q + 1.0) - a
                 pen = pen * area_ref[:, z : z + ZONE_TILE]
@@ -221,8 +220,11 @@
                     piece = pen[:, c : c + LANES]
                     summed = piece if summed is None else summed + piece
             if with_slope:
-                x = v * 0.5 + 0.25 if with_loss else v
-                slope = (jnp.tanh(x) + jnp.tanh(x - 0.5)).astype(BF16)
+                if with_loss:
+                    slope = jnp.tanh(v + 0.25) + jnp.tanh(v - 0.25)
+                else:
+                    slope = jnp.tanh(v) + jnp.tanh(v - 0.5)
+                slope = slope.astype(BF16)
                 slope_ref[2 * j, :, z : z + ZONE_TILE] = slope[:rows]
                 slope_ref[2 * j + 1, :, z : z + ZONE_TILE] = slope[rows:]
         if with_loss:
@@ -259,7 +261,7 @@
             out_ref[...] = message
 
 
-def scan(kind, rows_in, rhs, area, hours_total, sources, extra=(), priors=(), unroll=4, cost=None):
+def scan(kind, rows_in, rhs, area, hours_total, sources, extra=(), priors=(), unroll=6, cost=None):
     hours, zones = 2 * rhs.shape[0], rhs.shape[2]
     rows = sum(f.shape[0] for f in rows_in)
     outs = []
@@ -329,7 +331,7 @@
             acc_ref[:, at] += resp_ref[h, :, at].astype(F32) * mixed
         return carry
 
-    lax.fori_loop(0, hours, hour_step, 0, unroll=4)
+    lax.fori_loop(0, hours, hour_step, 0, unroll=hours // 2)
 
     grad = acc_ref[...] * area_ref[...]
     blocks, pad, _ = out_ref.shape
@@ -379,9 +381,6 @@
     leave = lax.dynamic_slice_in_dim(everyone, (1 - core) * half, half, axis=1)
     came = lax.ppermute(leave, "hour", [(0, 1), (1, 0)])
 
-    def across(x, m):
-        return lax.ppermute(x, ("zone", "hour"), [(i, i ^ m) for i in range(sources)])
-
     def swap(x, step):
         return lax.ppermute(x, "zone", [(i, i ^ step) for i in range(zone_parts)])
 
@@ -390,9 +389,9 @@
         building_map, owner_ids, window_params, band_ids, floor_area, response
     )
     if zone_parts == 4:
-        far0, far1 = across(keep, 4), across(leave, 5)
-        near0, near1 = across(keep, 2), across(leave, 3)
-        mine = [keep, came]
+        mine = jnp.concatenate([keep, came], axis=0)
+        far, beside = swap(mine, 2), swap(mine, 1)
+        mine = [mine]
     else:
         me = lax.axis_index(("zone", "hour"))
         both = jnp.where(core == 0, jnp.stack([keep, came]), jnp.stack([came, keep]))
@@ -402,11 +401,7 @@
     common = (rhs, area, hours_total, sources)
     loss0, slope0 = scan("loss_slope", mine, *common, cost=SHORT)
     if zone_parts == 4:
-        near0, near1, far0, far1, loss0 = lax.optimization_barrier(
-            (near0, near1, far0, far1, loss0)
-        )
-        beside = jnp.concatenate([near0, near1], axis=0)
-        far = jnp.concatenate([far0, far1], axis=0)
+        beside, far, loss0 = lax.optimization_barrier((beside, far, loss0))
         last = swap(far, 1)
     loss1, slope1, ft1 = scan("loss_slope_turn", [beside, far], *common)
     (message,) = scan("loss", [last], *common, priors=[loss0, loss1])

time: 54.5 us -> 53.7 us (0.985)
  Pallas kernels: 25.4 us -> 24 us
    ppermute x4 -> x6, starting transfers between devices: 4.92 us -> 10.4 us  [swap(): return lax.ppermute(x, 'zone', [(i, i ^ step) for i in range(zone_parts)])]
    ppermute x4 -> x0, starting transfers between devices: 5.48 us -> none  [across(): lax.ppermute(x, ('zone', 'hour'), [(i, i ^ m) for i in range(sources)])]
    ppermute x4 -> x0, waiting for transfers between devices: 2.44 us -> none  [across(): lax.ppermute(x, ('zone', 'hour'), [(i, i ^ m) for i in range(sources)])]
    ppermute x4 -> x6, waiting for transfers between devices: 1.66 us -> 3.52 us  [swap(): return lax.ppermute(x, 'zone', [(i, i ^ step) for i in range(zone_parts)])]
    pallas_call x5, Pallas kernels: 21.2 us -> 19.8 us  [call(): pl.pallas_call(kernel, in_specs=[VMEM] * len(args), out_specs=[VMEM] * le...]
    ppermute x1, waiting for transfers between devices: 0.01 us -> 0.94 us  [on_device(): came = lax.ppermute(leave, 'hour', [(0, 1), (1, 0)])]
  transfers between devices with their start and end apart: 10 -> 8, of which waited for: 3 -> 4; matrix products, arithmetic and copies ran while one was open for 0% -> 0% of each run, Pallas kernels for 33% -> 32%
where the time goes in v6:
time: 53.7 us; the launch traced here: 53.5 us
  Pallas kernels  24 us (45%)
  starting transfers between devices  11 us (20%)
  blocking collectives  10.8 us (20%)
  waiting for transfers between devices  5.63 us (10%)
  local copies, waits for them, and re-layouts  1.34 us (2%)
  between operations  0.73 us (1%)
    pallas_call x5, Pallas kernels, call(): pl.pallas_call(kernel, in_specs=[VMEM] * len(args), out_specs=[VMEM] * le...  19.8 us
    all_to_all x1, blocking collectives, on_device(): lax.all_to_all(parts, ('zone', 'scen', 'hour'), split_axis=0, concat_axis...  10.8 us
    ppermute x6, starting transfers between devices, swap(): return lax.ppermute(x, 'zone', [(i, i ^ step) for i in range(zone_parts)])  10.4 us
    ppermute x6, waiting for transfers between devices, swap(): return lax.ppermute(x, 'zone', [(i, i ^ step) for i in range(zone_parts)])  3.52 us
    pallas_call x1, Pallas kernels, coefficients(): pl.pallas_call(coeff_kernel, in_specs=[pl.BlockSpec(memory_space=pl.ANY)]...  3.22 us
    reshape x1, local copies, waits for them, and re-layouts, on_device(): everyone = forcing.reshape(forcing.shape[0], hours_total * width)  1.32 us
    ppermute x1, waiting for transfers between devices, on_device(): message = message + lax.ppermute(message, 'hour', [(0, 1), (1, 0)])  1.16 us
  transfers between devices with their start and end apart: 8, of which 4 were waited for; matrix products, arithmetic and copies ran while one was open for 0% of the time, Pallas kernels for 32%

profile of v6, /device:TPU:0, one launch (start us, length us, event | category | flops | bytes accessed | tf_op | source)
XLA Modules:
  0.0 53.5 jit_solution(8067496500188348868)
XLA Ops:
  0.6 1.3 %reshape.16 = bf16[32,3072]{1,0:T(8,128)(2,1)S(1)} reshape(bf16[32,48,64]{2,1,0:T(8,128)(2,1)} %param.7) | data formatting | bytes 393216 | tf_op jit(solution)/shard_map/reshape | solution.py:379
  2.0 0.5 collective-permute-start
  2.5 0.9 %collective-permute-done = bf16[32,1536]{1,0:T(8,128)(2,1)S(1)} collective-permute-done((bf16[32,1536]{1,0:T(8,128)(2,1)S(1)}, bf16[32,1536]{1,0:T(8,128)(2,1)S(1)}, u32[]{:S(2)}, u32[]{:S(2)}) %collective-permute-start) | collective-permute-done | bytes 98336 | tf_op jit(solution)/shard_map/ppermute | solution.py:382
  3.5 3.0 %collective-permute-start.1 = (bf16[64,1536]{1,0:T(8,128)(2,1)S(1)}, bf16[64,1536]{1,0:T(8,128)(2,1)S(1)}, u32[]{:S(2)}, u32[]{:S(2)}) collective-permute-start(bf16[64,1536]{1,0:T(8,128)(2,1)S(1)} %pad_maximum_fusion.refs_0_.refs_1_), channel_id=1, source_target_pairs={{0,4},{4,0},{8,12},{12,8},{1,5},{5,1},{9,13},{13,9},{2,6},{6,2},{1... | collective-permute-start | bytes 589832 | tf_op jit(solution)/shard_map/ppermute | solution.py:385
  6.5 2.6 %collective-permute-start.2 = (bf16[64,1536]{1,0:T(8,128)(2,1)S(1)}, bf16[64,1536]{1,0:T(8,128)(2,1)S(1)}, u32[]{:S(2)}, u32[]{:S(2)}) collective-permute-start(bf16[64,1536]{1,0:T(8,128)(2,1)S(1)} %pad_maximum_fusion.refs_0_.refs_1_), channel_id=1, source_target_pairs={{0,8},{4,12},{8,0},{12,4},{1,9},{5,13},{9,1},{13,5},{2,10},{6,14},... | collective-permute-start | bytes 589832 | tf_op jit(solution)/shard_map/ppermute | solution.py:385
  9.0 3.2 %coefficients.1 = (bf16[12,256,1024]{2,1,0:T(8,128)(2,1)S(1)}, s32[1,1024]{1,0:T(1,128)S(1)}, f32[1,1024]{1,0:T(1,128)S(1)}, bf16[24,64,1024]{2,1,0:T(8,128)(2,1)S(1)}) custom-call(s32[8,128]{1,0:T(8,128)} %bitcast.3, s32[8,128]{1,0:T(8,128)} %bitcast.4, f32[64,64]{1,0:T(8,128)} %wp_hbm.1, s32[24,1024]{1,0:T(8,128)} %band_hbm.1, f32[1,1024]{1,0:T(1,128)} %bitcast.5, ...), custom_call_target="tpu_custom_call" | custom-call | flops 1 | bytes 1 | tf_op jit(solution)/shard_map/coefficients/pallas_call | solution.py:135
  12.3 4.0 %loss_slope.1 = (f32[8,64]{1,0:T(8,128)S(1)}, bf16[24,64,1024]{2,1,0:T(8,128)(2,1)S(1)}) custom-call(bf16[64,1536]{1,0:T(8,128)(2,1)S(1)} %pad_maximum_fusion.refs_0_.refs_1_, bf16[12,256,1024]{2,1,0:T(8,128)(2,1)S(1)} %get-tuple-element.24.refs_1_.refs_2_, f32[1,1024]{1,0:T(1,128)S(1)} %get-tuple-element.25.refs_2_.refs_3_.refs_10_), custom_call_target="tpu_custom_call" | custom-call | flops 1 | bytes 1 | tf_op jit(solution)/shard_map/loss_slope/pallas_call | solution.py:33
  16.3 0.0 collective-permute-done.1.refs_0_
  16.3 2.0 %collective-permute-done.2.refs_1_ = bf16[64,1536]{1,0:T(8,128)(2,1)S(1)} collective-permute-done((bf16[64,1536]{1,0:T(8,128)(2,1)S(1)}, bf16[64,1536]{1,0:T(8,128)(2,1)S(1)}, u32[]{:S(2)}, u32[]{:S(2)}) %collective-permute-start.2) | collective-permute-done | bytes 196640 | tf_op jit(solution)/shard_map/ppermute | solution.py:385
  18.3 0.4 collective-permute-start.3
  18.7 7.6 %loss_slope_turn.1 = (f32[8,128]{1,0:T(8,128)S(1)}, bf16[24,128,1024]{2,1,0:T(8,128)(2,1)S(1)}, bf16[1536,128]{1,0:T(8,128)(2,1)S(1)}) custom-call(bf16[64,1536]{1,0:T(8,128)(2,1)S(1)} %collective-permute-done.1.refs_0_, bf16[64,1536]{1,0:T(8,128)(2,1)S(1)} %collective-permute-done.2.refs_1_, bf16[12,256,1024]{2,1,0:T(8,128)(2,1)S(1)} %get-tuple-element.24.refs_1_.refs_2_, ...), custom_call_target="tpu_custom_call" | custom-call | tf_op jit(solution)/shard_map/loss_slope_turn/pallas_call | solution.py:33
  26.3 0.0 collective-permute-done.3.refs_0_
  26.3 3.0 %loss.1 = f32[16,128]{1,0:T(8,128)S(1)} custom-call(bf16[64,1536]{1,0:T(8,128)(2,1)S(1)} %collective-permute-done.3.refs_0_, bf16[12,256,1024]{2,1,0:T(8,128)(2,1)S(1)} %get-tuple-element.24.refs_1_.refs_2_, f32[1,1024]{1,0:T(1,128)S(1)} %get-tuple-element.25.refs_2_.refs_3_.refs_10_, f32[8,64]{1,0:T(8,128)S(1)} %get-tuple-element.28.refs_3_, ...), custom_call_target="tpu_custom_call" | custom-call | tf_op jit(solution)/shard_map/loss/pallas_call | solution.py:33
  29.3 0.0 collective-permute-start.4
  29.4 1.2 %collective-permute-done.4 = f32[16,128]{1,0:T(8,128)S(1)} collective-permute-done((f32[16,128]{1,0:T(8,128)S(1)}, f32[16,128]{1,0:T(8,128)S(1)}, u32[]{:S(2)}, u32[]{:S(2)}) %collective-permute-start.4) | collective-permute-done | bytes 8224 | tf_op jit(solution)/shard_map/ppermute | solution.py:408
  30.5 1.6 %collective-permute-start.5 = (f32[16,128]{1,0:T(8,128)S(1)}, f32[16,128]{1,0:T(8,128)S(1)}, u32[]{:S(2)}, u32[]{:S(2)}) collective-permute-start(f32[16,128]{1,0:T(8,128)S(1)} %add.11.refs_0_), channel_id=1, source_target_pairs={{0,4},{4,0},{8,12},{12,8},{1,5},{5,1},{9,13},{13,9},{2,6},{6,2},{1... | collective-permute-start | bytes 24584 | tf_op jit(solution)/shard_map/ppermute | solution.py:385
  32.1 1.0 %collective-permute-start.6 = (f32[16,128]{1,0:T(8,128)S(1)}, f32[16,128]{1,0:T(8,128)S(1)}, u32[]{:S(2)}, u32[]{:S(2)}) collective-permute-start(f32[16,128]{1,0:T(8,128)S(1)} %add.11.refs_0_), channel_id=1, source_target_pairs={{0,8},{4,12},{8,0},{12,4},{1,9},{5,13},{9,1},{13,5},{2,10},{6,14},... | collective-permute-start | bytes 24584 | tf_op jit(solution)/shard_map/ppermute | solution.py:385
  33.1 1.8 %collective-permute-start.7 = (f32[16,128]{1,0:T(8,128)S(1)}, f32[16,128]{1,0:T(8,128)S(1)}, u32[]{:S(2)}, u32[]{:S(2)}) collective-permute-start(f32[16,128]{1,0:T(8,128)S(1)} %add.11.refs_0_), channel_id=1, source_target_pairs={{0,12},{4,8},{8,4},{12,0},{1,13},{5,9},{9,5},{13,1},{2,14},{6,10},... | collective-permute-start | bytes 24584 | tf_op jit(solution)/shard_map/ppermute | solution.py:385
  34.9 2.1 %slope_turn.1 = (bf16[24,64,1024]{2,1,0:T(8,128)(2,1)S(1)}, bf16[1536,128]{1,0:T(8,128)(2,1)S(1)}) custom-call(bf16[64,1536]{1,0:T(8,128)(2,1)S(1)} %collective-permute-done.3.refs_0_, bf16[64,1536]{1,0:T(8,128)(2,1)S(1)} %pad_maximum_fusion.refs_0_.refs_1_, bf16[12,256,1024]{2,1,0:T(8,128)(2,1)S(1)} %get-tuple-element.24.refs_1_.refs_2_, ...), custom_call_target="tpu_custom_call" | custom-call | tf_op jit(solution)/shard_map/slope_turn/pallas_call | solution.py:33
  37.0 0.0 collective-permute-done.5.refs_1_
  37.0 0.0 collective-permute-done.6.refs_2_
  37.1 1.5 %collective-permute-done.7.refs_3_ = f32[16,128]{1,0:T(8,128)S(1)} collective-permute-done((f32[16,128]{1,0:T(8,128)S(1)}, f32[16,128]{1,0:T(8,128)S(1)}, u32[]{:S(2)}, u32[]{:S(2)}) %collective-permute-start.7) | collective-permute-done | bytes 8224 | tf_op jit(solution)/shard_map/ppermute | solution.py:385
  38.6 3.1 %gradient.1 = f32[16,8,128]{2,1,0:T(8,128)S(1)} custom-call(f32[16,128]{1,0:T(8,128)S(1)} %add.11.refs_0_, f32[16,128]{1,0:T(8,128)S(1)} %collective-permute-done.5.refs_1_, f32[16,128]{1,0:T(8,128)S(1)} %collective-permute-done.6.refs_2_, f32[16,128]{1,0:T(8,128)S(1)} %collective-permute-done.7.refs_3_, bf16[1536,128]{1,0:T(8,128)(2,1)S(1)} %get-tuple-element.35.refs_4_, ...), custom_call_target="tpu_custom_call" | custom-call | tf_op jit(solution)/shard_map/gradient/pallas_call | solution.py:33
  41.7 10.8 %all_to_all.5.parts_ref = f32[16,8,128]{2,1,0:T(8,128)S(1)} all-to-all(f32[16,8,128]{2,1,0:T(8,128)S(1)} %gradient.1), channel_id=1, replica_groups=mesh['groups'=2,'zone'=4,'scen'=2,'hour'=2] {'zone','scen','hour'}, dimensions={0} | all-to-all | bytes 131072 | tf_op jit(solution)/shard_map/all_to_all | solution.py:433
  52.5 0.9 %finish.1 = (f32[4,64]{1,0:T(4,128)}, f32[1]{0:T(128)}) custom-call(f32[16,8,128]{2,1,0:T(8,128)S(1)} %all_to_all.5.parts_ref), custom_call_target="tpu_custom_call" | custom-call | tf_op jit(solution)/shard_map/finish/pallas_call | solution.py:436
  (3 shorter events, 0.0 us)
Async XLA Ops:
  2.0 1.5 %collective-permute-start = (bf16[32,1536]{1,0:T(8,128)(2,1)S(1)}, bf16[32,1536]{1,0:T(8,128)(2,1)S(1)}, u32[]{:S(2)}, u32[]{:S(2)}) collective-permute-start(bf16[32,1536]{1,0:T(8,128)(2,1)S(1)} %get-tuple-element.43), channel_id=1, source_target_pairs={{0,1},{1,0},{2,3},{3,2},{4,5},{5,4},{6,7},{7,6},{8,9},{9,8},{10,11... | collective-permute-start | bytes 294920 | tf_op jit(solution)/shard_map/ppermute | solution.py:382
  3.5 12.8 %collective-permute-start.1 = (bf16[64,1536]{1,0:T(8,128)(2,1)S(1)}, bf16[64,1536]{1,0:T(8,128)(2,1)S(1)}, u32[]{:S(2)}, u32[]{:S(2)}) collective-permute-start(bf16[64,1536]{1,0:T(8,128)(2,1)S(1)} %pad_maximum_fusion.refs_0_.refs_1_), channel_id=1, source_target_pairs={{0,4},{4,0},{8,12},{12,8},{1,5},{5,1},{9,13},{13,9},{2,6},{6,2},{1... | collective-permute-start | bytes 589832 | tf_op jit(solution)/shard_map/ppermute | solution.py:385
  6.5 11.8 %collective-permute-start.2 = (bf16[64,1536]{1,0:T(8,128)(2,1)S(1)}, bf16[64,1536]{1,0:T(8,128)(2,1)S(1)}, u32[]{:S(2)}, u32[]{:S(2)}) collective-permute-start(bf16[64,1536]{1,0:T(8,128)(2,1)S(1)} %pad_maximum_fusion.refs_0_.refs_1_), channel_id=1, source_target_pairs={{0,8},{4,12},{8,0},{12,4},{1,9},{5,13},{9,1},{13,5},{2,10},{6,14},... | collective-permute-start | bytes 589832 | tf_op jit(solution)/shard_map/ppermute | solution.py:385
  18.3 8.0 %collective-permute-start.3 = (bf16[64,1536]{1,0:T(8,128)(2,1)S(1)}, bf16[64,1536]{1,0:T(8,128)(2,1)S(1)}, u32[]{:S(2)}, u32[]{:S(2)}) collective-permute-start(bf16[64,1536]{1,0:T(8,128)(2,1)S(1)} %collective-permute-done.2.refs_1_), channel_id=1, source_target_pairs={{0,4},{4,0},{8,12},{12,8},{1,5},{5,1},{9,13},{13,9},{2,6},{6,2},{1... | collective-permute-start | bytes 589832 | tf_op jit(solution)/shard_map/ppermute | solution.py:385
  29.3 1.2 %collective-permute-start.4 = (f32[16,128]{1,0:T(8,128)S(1)}, f32[16,128]{1,0:T(8,128)S(1)}, u32[]{:S(2)}, u32[]{:S(2)}) collective-permute-start(f32[16,128]{1,0:T(8,128)S(1)} %loss.1), channel_id=1, source_target_pairs={{0,1},{1,0},{2,3},{3,2},{4,5},{5,4},{6,7},{7,6},{8,9},{9,8},{10,11... | collective-permute-start | bytes 24584 | tf_op jit(solution)/shard_map/ppermute | solution.py:408
  30.5 6.5 %collective-permute-start.5 = (f32[16,128]{1,0:T(8,128)S(1)}, f32[16,128]{1,0:T(8,128)S(1)}, u32[]{:S(2)}, u32[]{:S(2)}) collective-permute-start(f32[16,128]{1,0:T(8,128)S(1)} %add.11.refs_0_), channel_id=1, source_target_pairs={{0,4},{4,0},{8,12},{12,8},{1,5},{5,1},{9,13},{13,9},{2,6},{6,2},{1... | collective-permute-start | bytes 24584 | tf_op jit(solution)/shard_map/ppermute | solution.py:385
  32.1 4.9 %collective-permute-start.6 = (f32[16,128]{1,0:T(8,128)S(1)}, f32[16,128]{1,0:T(8,128)S(1)}, u32[]{:S(2)}, u32[]{:S(2)}) collective-permute-start(f32[16,128]{1,0:T(8,128)S(1)} %add.11.refs_0_), channel_id=1, source_target_pairs={{0,8},{4,12},{8,0},{12,4},{1,9},{5,13},{9,1},{13,5},{2,10},{6,14},... | collective-permute-start | bytes 24584 | tf_op jit(solution)/shard_map/ppermute | solution.py:385
  33.1 5.4 %collective-permute-start.7 = (f32[16,128]{1,0:T(8,128)S(1)}, f32[16,128]{1,0:T(8,128)S(1)}, u32[]{:S(2)}, u32[]{:S(2)}) collective-permute-start(f32[16,128]{1,0:T(8,128)S(1)} %add.11.refs_0_), channel_id=1, source_target_pairs={{0,12},{4,8},{8,4},{12,0},{1,13},{5,9},{9,5},{13,1},{2,14},{6,10},... | collective-permute-start | bytes 24584 | tf_op jit(solution)/shard_map/ppermute | solution.py:385

commit v7 on v6

--- a/solution.py
+++ b/solution.py
@@ -290,7 +290,7 @@
     hours_total, gain, owners, sources, messages, *refs
 ):
     msg_refs, refs = refs[:messages], refs[messages:]
-    ft_refs, slope_refs, refs = refs[:2], refs[2:5], refs[5:]
+    ft_refs, slope_refs, refs = refs[:2], refs[2:6], refs[6:]
     resp_ref, area_ref, plan_ref, out_ref, acc_ref, score_ref, e_ref = refs
     hours, width, zones = resp_ref.shape
     core, me = here()
@@ -309,7 +309,7 @@
     exp_total = jnp.sum(e)
     score_ref[...] = e
     quarter = sources // 4
-    order = [q * quarter + m for q in (1, 2, 0, 3) for m in range(quarter)]
+    order = [q * quarter + m for q in (0, 2, 1, 3) for m in range(quarter)]
     for spot, m in enumerate(order):
         piece = score_ref[pl.ds(me ^ m, 1), :]
         e_ref[:, spot * chunk : (spot + 1) * chunk] = piece[:, :chunk]
@@ -390,26 +390,28 @@
     )
     if zone_parts == 4:
         mine = jnp.concatenate([keep, came], axis=0)
-        far, beside = swap(mine, 2), swap(mine, 1)
-        mine = [mine]
+        far0, far1, beside = swap(keep, 2), swap(came, 2), swap(mine, 1)
     else:
         me = lax.axis_index(("zone", "hour"))
         both = jnp.where(core == 0, jnp.stack([keep, came]), jnp.stack([came, keep]))
         gathered = lax.all_gather(both, "zone", axis=0, tiled=True)
         ordered = jnp.take(gathered, me ^ jnp.arange(sources), axis=0).reshape(4, -1, half)
-        mine, beside, far, last = [ordered[0]], ordered[1], ordered[2], ordered[3]
+        mine, beside, far, last = ordered
     common = (rhs, area, hours_total, sources)
-    loss0, slope0 = scan("loss_slope", mine, *common, cost=SHORT)
+    loss0, slope0 = scan("loss_slope", [mine], *common, cost=SHORT)
     if zone_parts == 4:
-        beside, far, loss0 = lax.optimization_barrier((beside, far, loss0))
+        far0, far1, loss0 = lax.optimization_barrier((far0, far1, loss0))
+        far = jnp.concatenate([far0, far1], axis=0)
         last = swap(far, 1)
-    loss1, slope1, ft1 = scan("loss_slope_turn", [beside, far], *common)
-    (message,) = scan("loss", [last], *common, priors=[loss0, loss1])
+    loss2, slope2, ft0 = scan("loss_slope_turn", [far], *common, extra=[mine])
+    beside, loss2 = lax.optimization_barrier((beside, loss2))
+    loss1, slope1 = scan("loss_slope", [beside], *common)
+    (message,) = scan("loss", [last], *common, priors=[loss0, loss1, loss2])
     message = message + lax.ppermute(message, "hour", [(0, 1), (1, 0)])
-    slope2, ft2 = scan("slope_turn", [last], *common, extra=mine)
+    slope3, ft1 = scan("slope_turn", [last], *common, extra=[beside])
     if zone_parts == 4:
         others = [swap(message, k) for k in (1, 2, 3)]
-        *others, slope2 = lax.optimization_barrier((*others, slope2))
+        *others, slope3 = lax.optimization_barrier((*others, slope3))
         messages = [message, *others]
     else:
         messages = [lax.psum(message, "zone")]
@@ -423,11 +425,11 @@
         functools.partial(gradient_kernel, hours_total, gain, owners, sources, len(messages)),
         "gradient",
         [((devices, pad, LANES), F32)],
-        [*messages, ft1, ft2, slope1, slope0, slope2, near_response, area, plan],
+        [*messages, ft0, ft1, slope0, slope2, slope1, slope3, near_response, area, plan],
         [
             pltpu.VMEM((width, zones), F32),
             pltpu.VMEM(message.shape, F32),
-            pltpu.VMEM((1, ft1.shape[1] + ft2.shape[1]), F32),
+            pltpu.VMEM((1, ft0.shape[1] + ft1.shape[1]), F32),
         ],
     )
     parts = lax.all_to_all(

time: 53.7 us -> 52.4 us (0.976)
  waiting for transfers between devices: 5.63 us -> 2.02 us
  starting transfers between devices: 11 us -> 12 us
  blocking collectives: 10.8 us -> 11.6 us
    ppermute x6 -> x7, waiting for transfers between devices: 3.52 us -> 0.85 us  [swap(): return lax.ppermute(x, 'zone', [(i, i ^ step) for i in range(zone_parts)])]
    ppermute x6 -> x7, starting transfers between devices: 10.4 us -> 11.4 us  [swap(): return lax.ppermute(x, 'zone', [(i, i ^ step) for i in range(zone_parts)])]
    ppermute x1, waiting for transfers between devices: 0.94 us -> 0.01 us  [on_device(): came = lax.ppermute(leave, 'hour', [(0, 1), (1, 0)])]
    all_to_all x1, blocking collectives: 10.8 us -> 11.6 us  [on_device(): lax.all_to_all(parts, ('zone', 'scen', 'hour'), split_axis=0, concat_axis...]
    pallas_call x5 -> x6, Pallas kernels: 19.8 us -> 20.4 us  [call(): pl.pallas_call(kernel, in_specs=[VMEM] * len(args), out_specs=[VMEM] * le...]
  transfers between devices with their start and end apart: 8 -> 9, of which waited for: 4 -> 2; matrix products, arithmetic and copies ran while one was open for 0% -> 0% of each run, Pallas kernels for 32% -> 33%
where the time goes in v7:
time: 52.4 us; the launch traced here: 52.2 us
  Pallas kernels  24.5 us (47%)
  starting transfers between devices  12 us (23%)
  blocking collectives  11.6 us (22%)
  waiting for transfers between devices  2.02 us (4%)
  local copies, waits for them, and re-layouts  1.35 us (3%)
  between operations  0.76 us (1%)
    pallas_call x6, Pallas kernels, call(): pl.pallas_call(kernel, in_specs=[VMEM] * len(args), out_specs=[VMEM] * le...  20.4 us
    all_to_all x1, blocking collectives, on_device(): lax.all_to_all(parts, ('zone', 'scen', 'hour'), split_axis=0, concat_axis...  11.6 us
    ppermute x7, starting transfers between devices, swap(): return lax.ppermute(x, 'zone', [(i, i ^ step) for i in range(zone_parts)])  11.4 us
    pallas_call x1, Pallas kernels, coefficients(): pl.pallas_call(coeff_kernel, in_specs=[pl.BlockSpec(memory_space=pl.ANY)]...  3.21 us
    reshape x1, local copies, waits for them, and re-layouts, on_device(): everyone = forcing.reshape(forcing.shape[0], hours_total * width)  1.32 us
    ppermute x1, waiting for transfers between devices, on_device(): message = message + lax.ppermute(message, 'hour', [(0, 1), (1, 0)])  1.16 us
  transfers between devices with their start and end apart: 9, of which 2 were waited for; matrix products, arithmetic and copies ran while one was open for 0% of the time, Pallas kernels for 33%

profile of v7, /device:TPU:0, one launch (start us, length us, event | category | flops | bytes accessed | tf_op | source)
XLA Modules:
  0.0 52.2 jit_solution(16862684812266162916)
XLA Ops:
  0.6 1.3 %reshape.16 = bf16[32,3072]{1,0:T(8,128)(2,1)S(1)} reshape(bf16[32,48,64]{2,1,0:T(8,128)(2,1)} %param.7) | data formatting | bytes 393216 | tf_op jit(solution)/shard_map/reshape | solution.py:379
  2.0 0.5 collective-permute-start.1
  2.5 3.7 %collective-permute-start = (bf16[32,1536]{1,0:T(8,128)(2,1)S(1)}, bf16[32,1536]{1,0:T(8,128)(2,1)S(1)}, u32[]{:S(2)}, u32[]{:S(2)}) collective-permute-start(bf16[32,1536]{1,0:T(8,128)(2,1)S(1)} %get-tuple-element.51), channel_id=1, source_target_pairs={{0,8},{4,12},{8,0},{12,4},{1,9},{5,13},{9,1},{13,5},{2,10},{6,14},... | collective-permute-start | bytes 294920 | tf_op jit(solution)/shard_map/ppermute | solution.py:385
  6.2 0.0 collective-permute-done.1
  6.2 1.2 %collective-permute-start.2 = (bf16[32,1536]{1,0:T(8,128)(2,1)S(1)}, bf16[32,1536]{1,0:T(8,128)(2,1)S(1)}, u32[]{:S(2)}, u32[]{:S(2)}) collective-permute-start(bf16[32,1536]{1,0:T(8,128)(2,1)S(1)} %collective-permute-done.1), channel_id=1, source_target_pairs={{0,8},{4,12},{8,0},{12,4},{1,9},{5,13},{9,1},{13,5},{2,10},{6,14},... | collective-permute-start | bytes 294920 | tf_op jit(solution)/shard_map/ppermute | solution.py:385
  7.4 1.6 %collective-permute-start.4 = (bf16[64,1536]{1,0:T(8,128)(2,1)S(1)}, bf16[64,1536]{1,0:T(8,128)(2,1)S(1)}, u32[]{:S(2)}, u32[]{:S(2)}) collective-permute-start(bf16[64,1536]{1,0:T(8,128)(2,1)S(1)} %pad_maximum_fusion.refs_0_.refs_1_), channel_id=1, source_target_pairs={{0,4},{4,0},{8,12},{12,8},{1,5},{5,1},{9,13},{13,9},{2,6},{6,2},{1... | collective-permute-start | bytes 589832 | tf_op jit(solution)/shard_map/ppermute | solution.py:385
  9.0 3.2 %coefficients.1 = (bf16[12,256,1024]{2,1,0:T(8,128)(2,1)S(1)}, s32[1,1024]{1,0:T(1,128)S(1)}, f32[1,1024]{1,0:T(1,128)S(1)}, bf16[24,64,1024]{2,1,0:T(8,128)(2,1)S(1)}) custom-call(s32[8,128]{1,0:T(8,128)} %bitcast.3, s32[8,128]{1,0:T(8,128)} %bitcast.4, f32[64,64]{1,0:T(8,128)} %wp_hbm.1, s32[24,1024]{1,0:T(8,128)} %band_hbm.1, f32[1,1024]{1,0:T(1,128)} %bitcast.5, ...), custom_call_target="tpu_custom_call" | custom-call | flops 1 | bytes 1 | tf_op jit(solution)/shard_map/coefficients/pallas_call | solution.py:135
  12.3 4.0 %loss_slope.2 = (f32[8,64]{1,0:T(8,128)S(1)}, bf16[24,64,1024]{2,1,0:T(8,128)(2,1)S(1)}) custom-call(bf16[64,1536]{1,0:T(8,128)(2,1)S(1)} %pad_maximum_fusion.refs_0_.refs_1_, bf16[12,256,1024]{2,1,0:T(8,128)(2,1)S(1)} %get-tuple-element.28.refs_1_.refs_2_, f32[1,1024]{1,0:T(1,128)S(1)} %get-tuple-element.29.refs_2_.refs_3_.refs_11_), custom_call_target="tpu_custom_call" | custom-call | flops 1 | bytes 1 | tf_op jit(solution)/shard_map/loss_slope/pallas_call | solution.py:33
  16.3 0.0 collective-permute-done
  16.3 0.0 collective-permute-done.2
  16.3 0.5 %collective-permute-start.3 = (bf16[64,1536]{1,0:T(8,128)(2,1)S(1)}, bf16[64,1536]{1,0:T(8,128)(2,1)S(1)}, u32[]{:S(2)}, u32[]{:S(2)}) collective-permute-start(bf16[64,1536]{1,0:T(8,128)(2,1)S(1)} %constant_dynamic-update-slice_fusion.refs_0_), channel_id=1, source_target_pairs={{0,4},{4,0},{8,12},{12,8},{1,5},{5,1},{9,13},{13,9},{2,6},{6,2},{1... | collective-permute-start | bytes 589832 | tf_op jit(solution)/shard_map/ppermute | solution.py:385
  16.9 4.1 %loss_slope_turn.1 = (f32[8,64]{1,0:T(8,128)S(1)}, bf16[24,64,1024]{2,1,0:T(8,128)(2,1)S(1)}, bf16[1536,128]{1,0:T(8,128)(2,1)S(1)}) custom-call(bf16[64,1536]{1,0:T(8,128)(2,1)S(1)} %constant_dynamic-update-slice_fusion.refs_0_, bf16[64,1536]{1,0:T(8,128)(2,1)S(1)} %pad_maximum_fusion.refs_0_.refs_1_, ...), custom_call_target="tpu_custom_call" | custom-call | tf_op jit(solution)/shard_map/loss_slope_turn/pallas_call | solution.py:33
  20.9 0.0 collective-permute-done.4.refs_0_.refs_1_
  20.9 4.0 %loss_slope.3 = (f32[8,64]{1,0:T(8,128)S(1)}, bf16[24,64,1024]{2,1,0:T(8,128)(2,1)S(1)}) custom-call(bf16[64,1536]{1,0:T(8,128)(2,1)S(1)} %collective-permute-done.4.refs_0_.refs_1_, bf16[12,256,1024]{2,1,0:T(8,128)(2,1)S(1)} %get-tuple-element.28.refs_1_.refs_2_, f32[1,1024]{1,0:T(1,128)S(1)} %get-tuple-element.29.refs_2_.refs_3_.refs_11_), custom_call_target="tpu_custom_call" | custom-call | tf_op jit(solution)/shard_map/loss_slope/pallas_call | solution.py:33
  24.9 0.0 collective-permute-done.3.refs_0_
  25.0 3.0 %loss.1 = f32[16,128]{1,0:T(8,128)S(1)} custom-call(bf16[64,1536]{1,0:T(8,128)(2,1)S(1)} %collective-permute-done.3.refs_0_, bf16[12,256,1024]{2,1,0:T(8,128)(2,1)S(1)} %get-tuple-element.28.refs_1_.refs_2_, f32[1,1024]{1,0:T(1,128)S(1)} %get-tuple-element.29.refs_2_.refs_3_.refs_11_, f32[8,64]{1,0:T(8,128)S(1)} %get-tuple-element.33.refs_3_, ...), custom_call_target="tpu_custom_call" | custom-call | tf_op jit(solution)/shard_map/loss/pallas_call | solution.py:33
  28.0 0.0 collective-permute-start.5
  28.0 1.2 %collective-permute-done.5 = f32[16,128]{1,0:T(8,128)S(1)} collective-permute-done((f32[16,128]{1,0:T(8,128)S(1)}, f32[16,128]{1,0:T(8,128)S(1)}, u32[]{:S(2)}, u32[]{:S(2)}) %collective-permute-start.5) | collective-permute-done | bytes 8224 | tf_op jit(solution)/shard_map/ppermute | solution.py:410
  29.2 2.8 %collective-permute-start.8 = (f32[16,128]{1,0:T(8,128)S(1)}, f32[16,128]{1,0:T(8,128)S(1)}, u32[]{:S(2)}, u32[]{:S(2)}) collective-permute-start(f32[16,128]{1,0:T(8,128)S(1)} %add.11.refs_0_), channel_id=1, source_target_pairs={{0,12},{4,8},{8,4},{12,0},{1,13},{5,9},{9,5},{13,1},{2,14},{6,10},... | collective-permute-start | bytes 24584 | tf_op jit(solution)/shard_map/ppermute | solution.py:385
  32.0 0.5 %collective-permute-start.7 = (f32[16,128]{1,0:T(8,128)S(1)}, f32[16,128]{1,0:T(8,128)S(1)}, u32[]{:S(2)}, u32[]{:S(2)}) collective-permute-start(f32[16,128]{1,0:T(8,128)S(1)} %add.11.refs_0_), channel_id=1, source_target_pairs={{0,8},{4,12},{8,0},{12,4},{1,9},{5,13},{9,1},{13,5},{2,10},{6,14},... | collective-permute-start | bytes 24584 | tf_op jit(solution)/shard_map/ppermute | solution.py:385
  32.5 1.1 %collective-permute-start.6 = (f32[16,128]{1,0:T(8,128)S(1)}, f32[16,128]{1,0:T(8,128)S(1)}, u32[]{:S(2)}, u32[]{:S(2)}) collective-permute-start(f32[16,128]{1,0:T(8,128)S(1)} %add.11.refs_0_), channel_id=1, source_target_pairs={{0,4},{4,0},{8,12},{12,8},{1,5},{5,1},{9,13},{13,9},{2,6},{6,2},{1... | collective-permute-start | bytes 24584 | tf_op jit(solution)/shard_map/ppermute | solution.py:385
  33.6 2.1 %slope_turn.1 = (bf16[24,64,1024]{2,1,0:T(8,128)(2,1)S(1)}, bf16[1536,128]{1,0:T(8,128)(2,1)S(1)}) custom-call(bf16[64,1536]{1,0:T(8,128)(2,1)S(1)} %collective-permute-done.3.refs_0_, bf16[64,1536]{1,0:T(8,128)(2,1)S(1)} %collective-permute-done.4.refs_0_.refs_1_, bf16[12,256,1024]{2,1,0:T(8,128)(2,1)S(1)} %get-tuple-element.28.refs_1_.refs_2_, ...), custom_call_target="tpu_custom_call" | custom-call | tf_op jit(solution)/shard_map/slope_turn/pallas_call | solution.py:33
  35.7 0.0 collective-permute-done.8.refs_3_
  35.7 0.8 %collective-permute-done.7.refs_2_ = f32[16,128]{1,0:T(8,128)S(1)} collective-permute-done((f32[16,128]{1,0:T(8,128)S(1)}, f32[16,128]{1,0:T(8,128)S(1)}, u32[]{:S(2)}, u32[]{:S(2)}) %collective-permute-start.7) | collective-permute-done | bytes 8224 | tf_op jit(solution)/shard_map/ppermute | solution.py:385
  36.5 0.0 collective-permute-done.6.refs_1_
  36.5 3.2 %gradient.1 = f32[16,8,128]{2,1,0:T(8,128)S(1)} custom-call(f32[16,128]{1,0:T(8,128)S(1)} %add.11.refs_0_, f32[16,128]{1,0:T(8,128)S(1)} %collective-permute-done.6.refs_1_, f32[16,128]{1,0:T(8,128)S(1)} %collective-permute-done.7.refs_2_, f32[16,128]{1,0:T(8,128)S(1)} %collective-permute-done.8.refs_3_, bf16[1536,128]{1,0:T(8,128)(2,1)S(1)} %get-tuple-element.42.refs_4_, ...), custom_call_target="tpu_custom_call" | custom-call | tf_op jit(solution)/shard_map/gradient/pallas_call | solution.py:33
  39.7 11.6 %all_to_all.5.parts_ref = f32[16,8,128]{2,1,0:T(8,128)S(1)} all-to-all(f32[16,8,128]{2,1,0:T(8,128)S(1)} %gradient.1), channel_id=1, replica_groups=mesh['groups'=2,'zone'=4,'scen'=2,'hour'=2] {'zone','scen','hour'}, dimensions={0} | all-to-all | bytes 131072 | tf_op jit(solution)/shard_map/all_to_all | solution.py:435
  51.3 0.9 %finish.1 = (f32[4,64]{1,0:T(4,128)}, f32[1]{0:T(128)}) custom-call(f32[16,8,128]{2,1,0:T(8,128)S(1)} %all_to_all.5.parts_ref), custom_call_target="tpu_custom_call" | custom-call | tf_op jit(solution)/shard_map/finish/pallas_call | solution.py:438
  (5 shorter events, 0.1 us)
Async XLA Ops:
  2.0 4.2 %collective-permute-start.1 = (bf16[32,1536]{1,0:T(8,128)(2,1)S(1)}, bf16[32,1536]{1,0:T(8,128)(2,1)S(1)}, u32[]{:S(2)}, u32[]{:S(2)}) collective-permute-start(bf16[32,1536]{1,0:T(8,128)(2,1)S(1)} %get-tuple-element.50), channel_id=1, source_target_pairs={{0,1},{1,0},{2,3},{3,2},{4,5},{5,4},{6,7},{7,6},{8,9},{9,8},{10,11... | collective-permute-start | bytes 294920 | tf_op jit(solution)/shard_map/ppermute | solution.py:382
  2.5 13.8 %collective-permute-start = (bf16[32,1536]{1,0:T(8,128)(2,1)S(1)}, bf16[32,1536]{1,0:T(8,128)(2,1)S(1)}, u32[]{:S(2)}, u32[]{:S(2)}) collective-permute-start(bf16[32,1536]{1,0:T(8,128)(2,1)S(1)} %get-tuple-element.51), channel_id=1, source_target_pairs={{0,8},{4,12},{8,0},{12,4},{1,9},{5,13},{9,1},{13,5},{2,10},{6,14},... | collective-permute-start | bytes 294920 | tf_op jit(solution)/shard_map/ppermute | solution.py:385
  6.2 10.1 %collective-permute-start.2 = (bf16[32,1536]{1,0:T(8,128)(2,1)S(1)}, bf16[32,1536]{1,0:T(8,128)(2,1)S(1)}, u32[]{:S(2)}, u32[]{:S(2)}) collective-permute-start(bf16[32,1536]{1,0:T(8,128)(2,1)S(1)} %collective-permute-done.1), channel_id=1, source_target_pairs={{0,8},{4,12},{8,0},{12,4},{1,9},{5,13},{9,1},{13,5},{2,10},{6,14},... | collective-permute-start | bytes 294920 | tf_op jit(solution)/shard_map/ppermute | solution.py:385
  7.4 13.5 %collective-permute-start.4 = (bf16[64,1536]{1,0:T(8,128)(2,1)S(1)}, bf16[64,1536]{1,0:T(8,128)(2,1)S(1)}, u32[]{:S(2)}, u32[]{:S(2)}) collective-permute-start(bf16[64,1536]{1,0:T(8,128)(2,1)S(1)} %pad_maximum_fusion.refs_0_.refs_1_), channel_id=1, source_target_pairs={{0,4},{4,0},{8,12},{12,8},{1,5},{5,1},{9,13},{13,9},{2,6},{6,2},{1... | collective-permute-start | bytes 589832 | tf_op jit(solution)/shard_map/ppermute | solution.py:385
  16.3 8.6 %collective-permute-start.3 = (bf16[64,1536]{1,0:T(8,128)(2,1)S(1)}, bf16[64,1536]{1,0:T(8,128)(2,1)S(1)}, u32[]{:S(2)}, u32[]{:S(2)}) collective-permute-start(bf16[64,1536]{1,0:T(8,128)(2,1)S(1)} %constant_dynamic-update-slice_fusion.refs_0_), channel_id=1, source_target_pairs={{0,4},{4,0},{8,12},{12,8},{1,5},{5,1},{9,13},{13,9},{2,6},{6,2},{1... | collective-permute-start | bytes 589832 | tf_op jit(solution)/shard_map/ppermute | solution.py:385
  28.0 1.2 %collective-permute-start.5 = (f32[16,128]{1,0:T(8,128)S(1)}, f32[16,128]{1,0:T(8,128)S(1)}, u32[]{:S(2)}, u32[]{:S(2)}) collective-permute-start(f32[16,128]{1,0:T(8,128)S(1)} %loss.1), channel_id=1, source_target_pairs={{0,1},{1,0},{2,3},{3,2},{4,5},{5,4},{6,7},{7,6},{8,9},{9,8},{10,11... | collective-permute-start | bytes 24584 | tf_op jit(solution)/shard_map/ppermute | solution.py:410
  29.2 6.5 %collective-permute-start.8 = (f32[16,128]{1,0:T(8,128)S(1)}, f32[16,128]{1,0:T(8,128)S(1)}, u32[]{:S(2)}, u32[]{:S(2)}) collective-permute-start(f32[16,128]{1,0:T(8,128)S(1)} %add.11.refs_0_), channel_id=1, source_target_pairs={{0,12},{4,8},{8,4},{12,0},{1,13},{5,9},{9,5},{13,1},{2,14},{6,10},... | collective-permute-start | bytes 24584 | tf_op jit(solution)/shard_map/ppermute | solution.py:385
  32.0 4.5 %collective-permute-start.7 = (f32[16,128]{1,0:T(8,128)S(1)}, f32[16,128]{1,0:T(8,128)S(1)}, u32[]{:S(2)}, u32[]{:S(2)}) collective-permute-start(f32[16,128]{1,0:T(8,128)S(1)} %add.11.refs_0_), channel_id=1, source_target_pairs={{0,8},{4,12},{8,0},{12,4},{1,9},{5,13},{9,1},{13,5},{2,10},{6,14},... | collective-permute-start | bytes 24584 | tf_op jit(solution)/shard_map/ppermute | solution.py:385
  32.5 4.0 %collective-permute-start.6 = (f32[16,128]{1,0:T(8,128)S(1)}, f32[16,128]{1,0:T(8,128)S(1)}, u32[]{:S(2)}, u32[]{:S(2)}) collective-permute-start(f32[16,128]{1,0:T(8,128)S(1)} %add.11.refs_0_), channel_id=1, source_target_pairs={{0,4},{4,0},{8,12},{12,8},{1,5},{5,1},{9,13},{13,9},{2,6},{6,2},{1... | collective-permute-start | bytes 24584 | tf_op jit(solution)/shard_map/ppermute | solution.py:385

commit v8 on v7

--- a/solution.py
+++ b/solution.py
@@ -42,9 +42,10 @@
     )(*[near(a) for a in args])
 
 
-def coeff_kernel(
-    map_hbm, owner_hbm, wp_hbm, band_hbm, area_hbm, resp_hbm, rhs_ref, plan_ref, area_ref, resp_ref,
-    map_ref, owner_ref, wp_ref, band_ref, zp_ref, sems, resp_sems,
+def open_kernel(
+    hours_total, mine_ref, map_hbm, owner_hbm, wp_hbm, band_hbm, area_hbm, resp_hbm,
+    rhs_ref, plan_ref, area_ref, resp_ref, loss_ref, slope_ref,
+    map_ref, owner_ref, wp_ref, band_ref, zp_ref, acc_ref, sems, resp_sems,
 ):
     hours, width, zones = resp_ref.shape
     pieces = resp_sems.shape[0]
@@ -80,7 +81,7 @@
         here = jnp.take_along_axis(table, lane, axis=1, mode="promise_in_bounds")
         return jnp.where(row == i, here, found)
 
-    plan = lax.fori_loop(0, owner_ref.shape[0], look, jnp.zeros_like(place))
+    plan = lax.fori_loop(0, owner_ref.shape[0], look, jnp.zeros_like(place), unroll=8)
     for r in range(plan.shape[0]):
         plan_ref[:, r * LANES : (r + 1) * LANES] = plan[r : r + 1, :]
     designs = wp_ref.shape[0]
@@ -88,35 +89,47 @@
         lax.broadcasted_iota(jnp.int32, (designs, zones), 0) == plan_ref[...]
     ).astype(F32).astype(BF16)
     rest = wp_ref[...]
-    total = jnp.zeros((width, zones), F32)
+    exact = []
     for _ in range(3):
-        part = rest.astype(BF16)
-        rest = rest - part.astype(F32)
-        total = total + lax.dot_general(
-            part, onehot, (((0,), (0,)), ((), ())), preferred_element_type=F32
-        )
-    zp_ref[...] = total
+        exact.append(rest.astype(BF16))
+        rest = rest - exact[-1].astype(F32)
+    zp_ref[...] = lax.dot_general(
+        jnp.concatenate(exact, axis=0),
+        jnp.concatenate([onehot] * 3, axis=0),
+        (((0,), (0,)), ((), ())),
+        preferred_element_type=F32,
+    )
     extra = lax.broadcasted_iota(jnp.int32, (16, zones), 0)
     blank = jnp.zeros((DEPTH - width - 16, zones), BF16)
+    core, _ = here()
+    acc_ref[...] = jnp.zeros_like(acc_ref)
 
     def pair_step(j, carry):
+        depth = []
         for k in range(2):
             h = 2 * j + k
-            at = k * DEPTH
-            coeff = resp_ref[h].astype(F32) * zp_ref[...]
-            rhs_ref[j, at : at + width, :] = coeff.astype(BF16)
+            coeff = (resp_ref[h].astype(F32) * zp_ref[...]).astype(BF16)
             middle = 0.25 * (band_ref[pl.ds(h, 1), :].astype(F32) - 3.5)
             tail = jnp.where(extra == 0, -middle, jnp.where(extra == 1, 1.0, 0.0))
-            rhs_ref[j, at + width : at + width + 16, :] = tail.astype(BF16)
-            rhs_ref[j, at + width + 16 : at + DEPTH, :] = blank
+            depth += [coeff, tail.astype(BF16), blank]
+        rhs = jnp.concatenate(depth, axis=0)
+        rhs_ref[j] = rhs
+        pair = mine_ref[:, pl.ds(pl.multiple_of(j * LANES, LANES), LANES)]
+        summed = pair_work("loss_slope", pair, lambda at: rhs[:, at], area_ref, slope_ref, j)
+        acc_ref[...] += hour_weighted(summed, core, hours, hours_total, j)
         return carry
 
     for i in range(pieces):
         large[i].wait()
         lax.fori_loop(i * span // 2, (i + 1) * span // 2, pair_step, 0, unroll=span // 2)
-
-
-def coefficients(building_map, owner_ids, window_params, band_ids, floor_area, response):
+    loss_ref[...] = jnp.broadcast_to(
+        jnp.sum(acc_ref[...].T, axis=0, keepdims=True), loss_ref.shape
+    )
+
+
+def opening(
+    mine, building_map, owner_ids, window_params, band_ids, floor_area, response, hours_total
+):
     hours, width, zones = response.shape
     args = [
         building_map.reshape(-1, LANES),
@@ -131,22 +144,25 @@
         ((1, zones), jnp.int32),
         ((1, zones), F32),
         (response.shape, BF16),
+        ((8, mine.shape[0]), F32),
+        ((hours, mine.shape[0], zones), BF16),
     ]
     return pl.pallas_call(
-        coeff_kernel,
-        in_specs=[pl.BlockSpec(memory_space=pl.ANY)] * len(args),
+        functools.partial(open_kernel, hours_total),
+        in_specs=[VMEM] + [pl.BlockSpec(memory_space=pl.ANY)] * len(args),
         out_specs=[VMEM] * len(outs),
         out_shape=[pltpu.MemorySpace.VMEM(shape, kind) for shape, kind in outs],
         scratch_shapes=[pltpu.VMEM(a.shape, a.dtype) for a in args[:4]]
         + [
             pltpu.VMEM((width, zones), F32),
+            pltpu.VMEM((mine.shape[0], LANES), F32),
             pltpu.SemaphoreType.DMA((5,)),
-            pltpu.SemaphoreType.DMA((4,)),
+            pltpu.SemaphoreType.DMA((2,)),
         ],
         compiler_params=params(),
         cost_estimate=SHORT,
-        name="coefficients",
-    )(*[pltpu.with_memory_space_constraint(a, pltpu.HBM) for a in args])
+        name="opening",
+    )(near(mine), *[pltpu.with_memory_space_constraint(a, pltpu.HBM) for a in args])
 
 
 def drivers(pair, second, fill):
@@ -169,7 +185,51 @@
     return 1.0 + 2.0 * hour.astype(F32) / (hours_total - 1)
 
 
-def scan_kernel(kind, hours_total, chunks, extra, sources, priors, unroll, *refs):
+def pair_work(kind, pair, rhs_at, area_ref, slope_ref, j):
+    with_loss, with_slope = "loss" in kind, "slope" in kind
+    zones = area_ref.shape[1]
+    rows = pair.shape[0]
+    fill = (0.5,) if with_loss else (0.5, 0.25)
+    pair = (pair.astype(F32) * 0.5).astype(BF16)
+    none = jnp.zeros(pair.shape, BF16)
+    lhs = jnp.concatenate(
+        [
+            jnp.concatenate([drivers(pair, False, fill), none], axis=1),
+            jnp.concatenate([none, drivers(pair, True, fill)], axis=1),
+        ],
+        axis=0,
+    )
+    summed = None
+    for z in range(0, zones, ZONE_TILE):
+        v = jnp.dot(lhs, rhs_at(slice(z, z + ZONE_TILE)), preferred_element_type=F32)
+        if with_loss:
+            a = jnp.abs(v) * (2.0 * MINUS_LOG2_E)
+            q = jnp.exp2(a)
+            pen = jnp.log2((q + EDGE) * q + 1.0) - a
+            pen = pen * area_ref[:, z : z + ZONE_TILE]
+            for c in range(0, ZONE_TILE, LANES):
+                piece = pen[:, c : c + LANES]
+                summed = piece if summed is None else summed + piece
+        if with_slope:
+            if with_loss:
+                slope = jnp.tanh(v + 0.25) + jnp.tanh(v - 0.25)
+            else:
+                slope = jnp.tanh(v) + jnp.tanh(v - 0.5)
+            slope = slope.astype(BF16)
+            slope_ref[2 * j, :, z : z + ZONE_TILE] = slope[:rows]
+            slope_ref[2 * j + 1, :, z : z + ZONE_TILE] = slope[rows:]
+    return summed
+
+
+def hour_weighted(summed, core, hours, hours_total, j):
+    rows = summed.shape[0] // 2
+    first = core * hours + 2 * j
+    return summed[:rows] * occupancy(first, hours_total) + summed[rows:] * occupancy(
+        first + 1, hours_total
+    )
+
+
+def scan_kernel(kind, hours_total, chunks, extra, order, priors, unroll, *refs):
     with_loss, with_slope, with_turn = "loss" in kind, "slope" in kind, "turn" in kind
     f_refs, refs = refs[:chunks], refs[chunks:]
     turn_refs, refs = [*refs[:extra], *f_refs], refs[extra:]
@@ -177,6 +237,7 @@
     prior_refs, refs = refs[:priors], refs[priors:]
     if with_loss:
         out_ref, refs = refs[0], refs[1:]
+    slope_ref = None
     if with_slope:
         slope_ref, refs = refs[0], refs[1:]
     if with_turn:
@@ -197,41 +258,9 @@
         pair = rows_of(f_refs, at)
         if with_turn:
             ft_ref[at, :] = rows_of(turn_refs, at).T
-        rows = pair.shape[0]
-        fill = (0.5,) if with_loss else (0.5, 0.25)
-        pair = (pair.astype(F32) * 0.5).astype(BF16)
-        none = jnp.zeros(pair.shape, BF16)
-        lhs = jnp.concatenate(
-            [
-                jnp.concatenate([drivers(pair, False, fill), none], axis=1),
-                jnp.concatenate([none, drivers(pair, True, fill)], axis=1),
-            ],
-            axis=0,
-        )
-        summed = None
-        for z in range(0, zones, ZONE_TILE):
-            v = jnp.dot(lhs, rhs_ref[j, :, z : z + ZONE_TILE], preferred_element_type=F32)
-            if with_loss:
-                a = jnp.abs(v) * (2.0 * MINUS_LOG2_E)
-                q = jnp.exp2(a)
-                pen = jnp.log2((q + EDGE) * q + 1.0) - a
-                pen = pen * area_ref[:, z : z + ZONE_TILE]
-                for c in range(0, ZONE_TILE, LANES):
-                    piece = pen[:, c : c + LANES]
-                    summed = piece if summed is None else summed + piece
-            if with_slope:
-                if with_loss:
-                    slope = jnp.tanh(v + 0.25) + jnp.tanh(v - 0.25)
-                else:
-                    slope = jnp.tanh(v) + jnp.tanh(v - 0.5)
-                slope = slope.astype(BF16)
-                slope_ref[2 * j, :, z : z + ZONE_TILE] = slope[:rows]
-                slope_ref[2 * j + 1, :, z : z + ZONE_TILE] = slope[rows:]
+        summed = pair_work(kind, pair, lambda at: rhs_ref[j, :, at], area_ref, slope_ref, j)
         if with_loss:
-            first = core * hours + 2 * j
-            acc_ref[...] += summed[:rows] * occupancy(first, hours_total) + summed[
-                rows:
-            ] * occupancy(first + 1, hours_total)
+            acc_ref[...] += hour_weighted(summed, core, hours, hours_total, j)
         return carry
 
     lax.fori_loop(0, pairs, pair_step, 0, unroll=unroll)
@@ -242,7 +271,7 @@
             out_ref[...] = jnp.broadcast_to(row, out_ref.shape)
         else:
             known = [ref[0:1, :] for ref in prior_refs] + [row]
-            chunk = sum(part.shape[1] for part in known) // sources
+            chunk = sum(part.shape[1] for part in known) // len(order)
             pieces = [
                 part[:, first : first + chunk]
                 for part in known
@@ -255,19 +284,19 @@
             message = jnp.zeros(out_ref.shape, F32) + weight
             index = lax.broadcasted_iota(jnp.int32, message.shape, 0)
             blank = jnp.zeros((1, LANES - chunk), F32)
-            for m, piece in enumerate(pieces):
+            for m, piece in zip(order, pieces):
                 piece = jnp.concatenate([piece, blank], axis=1)
                 message = jnp.where(index == (me ^ m), piece, message)
             out_ref[...] = message
 
 
-def scan(kind, rows_in, rhs, area, hours_total, sources, extra=(), priors=(), unroll=6, cost=None):
+def scan(kind, rows_in, rhs, area, hours_total, order, extra=(), priors=(), unroll=6, cost=None):
     hours, zones = 2 * rhs.shape[0], rhs.shape[2]
     rows = sum(f.shape[0] for f in rows_in)
     outs = []
     scratch = []
     if "loss" in kind:
-        sublanes = -(-(sources + 1) // 8) * 8
+        sublanes = -(-(len(order) + 1) // 8) * 8
         outs.append(((sublanes, LANES) if priors else (8, rows), F32))
         scratch.append(pltpu.VMEM((rows, LANES), F32))
     if "slope" in kind:
@@ -276,7 +305,7 @@
         outs.append(((rows_in[0].shape[1], rows + sum(f.shape[0] for f in extra)), BF16))
     return call(
         functools.partial(
-            scan_kernel, kind, hours_total, len(rows_in), len(extra), sources, len(priors), unroll
+            scan_kernel, kind, hours_total, len(rows_in), len(extra), order, len(priors), unroll
         ),
         kind,
         outs,
@@ -287,13 +316,14 @@
 
 
 def gradient_kernel(
-    hours_total, gain, owners, sources, messages, *refs
+    hours_total, gain, owners, order, messages, *refs
 ):
     msg_refs, refs = refs[:messages], refs[messages:]
     ft_refs, slope_refs, refs = refs[:2], refs[2:6], refs[6:]
     resp_ref, area_ref, plan_ref, out_ref, acc_ref, score_ref, e_ref = refs
     hours, width, zones = resp_ref.shape
     core, me = here()
+    sources = len(order)
     chunk = e_ref.shape[1] // sources
     total = [msg_ref[...] for msg_ref in msg_refs]
     while len(total) > 1:
@@ -308,8 +338,6 @@
     e = jnp.where(valid, jnp.exp(jnp.where(valid, score - peak, 0.0)), 0.0)
     exp_total = jnp.sum(e)
     score_ref[...] = e
-    quarter = sources // 4
-    order = [q * quarter + m for q in (0, 2, 1, 3) for m in range(quarter)]
     for spot, m in enumerate(order):
         piece = score_ref[pl.ds(me ^ m, 1), :]
         e_ref[:, spot * chunk : (spot + 1) * chunk] = piece[:, :chunk]
@@ -384,10 +412,13 @@
     def swap(x, step):
         return lax.ppermute(x, "zone", [(i, i ^ step) for i in range(zone_parts)])
 
-    came, building_map = lax.optimization_barrier((came, building_map))
-    rhs, plan, area, near_response = coefficients(
-        building_map, owner_ids, window_params, band_ids, floor_area, response
-    )
+    piece = sources // 8
+    parts = [range(i, i + piece) for i in range(0, sources, piece)]
+    own, near0, near1, far_a, far_b, final = (
+        [*parts[0], *parts[1]], parts[2], parts[3], parts[4], parts[5], [*parts[6], *parts[7]]
+    )
+    worked = (*own, *far_a, *near0, *near1, *far_b, *final)
+    kept = (*far_a, *near0, *near1, *far_b, *own, *final)
     if zone_parts == 4:
         mine = jnp.concatenate([keep, came], axis=0)
         far0, far1, beside = swap(keep, 2), swap(came, 2), swap(mine, 1)
@@ -397,18 +428,20 @@
         gathered = lax.all_gather(both, "zone", axis=0, tiled=True)
         ordered = jnp.take(gathered, me ^ jnp.arange(sources), axis=0).reshape(4, -1, half)
         mine, beside, far, last = ordered
-    common = (rhs, area, hours_total, sources)
-    loss0, slope0 = scan("loss_slope", [mine], *common, cost=SHORT)
+        far0, far1 = far[: far.shape[0] // 2], far[far.shape[0] // 2 :]
+    rhs, plan, area, near_response, loss0, slope0 = opening(
+        mine, building_map, owner_ids, window_params, band_ids, floor_area, response, hours_total
+    )
+    common = (rhs, area, hours_total, worked)
+    far0, loss0 = lax.optimization_barrier((far0, loss0))
+    loss1, slope1 = scan("loss_slope", [far0], *common, cost=SHORT)
     if zone_parts == 4:
-        far0, far1, loss0 = lax.optimization_barrier((far0, far1, loss0))
-        far = jnp.concatenate([far0, far1], axis=0)
-        last = swap(far, 1)
-    loss2, slope2, ft0 = scan("loss_slope_turn", [far], *common, extra=[mine])
-    beside, loss2 = lax.optimization_barrier((beside, loss2))
-    loss1, slope1 = scan("loss_slope", [beside], *common)
+        far0, far1, loss1 = lax.optimization_barrier((far0, far1, loss1))
+        last = swap(jnp.concatenate([far0, far1], axis=0), 1)
+    loss2, slope2, ft0 = scan("loss_slope_turn", [beside, far1], *common, extra=[far0])
     (message,) = scan("loss", [last], *common, priors=[loss0, loss1, loss2])
     message = message + lax.ppermute(message, "hour", [(0, 1), (1, 0)])
-    slope3, ft1 = scan("slope_turn", [last], *common, extra=[beside])
+    slope3, ft1 = scan("slope_turn", [last], *common, extra=[mine])
     if zone_parts == 4:
         others = [swap(message, k) for k in (1, 2, 3)]
         *others, slope3 = lax.optimization_barrier((*others, slope3))
@@ -422,10 +455,10 @@
     pad = -(-owners // 8) * 8
     gain = math.sqrt(width * zones * zone_parts * hours_total * designs)
     (parts,) = call(
-        functools.partial(gradient_kernel, hours_total, gain, owners, sources, len(messages)),
+        functools.partial(gradient_kernel, hours_total, gain, owners, kept, len(messages)),
         "gradient",
         [((devices, pad, LANES), F32)],
-        [*messages, ft0, ft1, slope0, slope2, slope1, slope3, near_response, area, plan],
+        [*messages, ft0, ft1, slope1, slope2, slope0, slope3, near_response, area, plan],
         [
             pltpu.VMEM((width, zones), F32),
             pltpu.VMEM(message.shape, F32),

time: 52.4 us -> 51.8 us (0.989)
  blocking collectives: 11.6 us -> 10.2 us
  waiting for transfers between devices: 2.02 us -> 3.42 us
  Pallas kernels: 24.5 us -> 23.7 us
    pallas_call x6 -> x5, Pallas kernels: 20.4 us -> 16.6 us  [call(): pl.pallas_call(kernel, in_specs=[VMEM] * len(args), out_specs=[VMEM] * le...]
    pallas_call x1, Pallas kernels: 3.21 us -> 6.15 us  [opening(): pl.pallas_call(functools.partial(open_kernel, hours_total), in_specs=[VME...]
    ppermute x7, waiting for transfers between devices: 0.85 us -> 2.26 us  [swap(): return lax.ppermute(x, 'zone', [(i, i ^ step) for i in range(zone_parts)])]
    all_to_all x1, blocking collectives: 11.6 us -> 10.2 us  [on_device(): lax.all_to_all(parts, ('zone', 'scen', 'hour'), split_axis=0, concat_axis...]
  transfers between devices with their start and end apart: 9 -> 9, of which waited for: 2 -> 3; matrix products, arithmetic and copies ran while one was open for 0% -> 0% of each run, Pallas kernels for 33% -> 32%
where the time goes in v8:
time: 51.8 us; the launch traced here: 51.6 us
  Pallas kernels  23.7 us (46%)
  starting transfers between devices  12 us (23%)
  blocking collectives  10.2 us (20%)
  waiting for transfers between devices  3.42 us (7%)
  local copies, waits for them, and re-layouts  1.34 us (3%)
  between operations  0.89 us (2%)
    pallas_call x5, Pallas kernels, call(): pl.pallas_call(kernel, in_specs=[VMEM] * len(args), out_specs=[VMEM] * le...  16.6 us
    ppermute x7, starting transfers between devices, swap(): return lax.ppermute(x, 'zone', [(i, i ^ step) for i in range(zone_parts)])  11.4 us
    all_to_all x1, blocking collectives, on_device(): lax.all_to_all(parts, ('zone', 'scen', 'hour'), split_axis=0, concat_axis...  10.2 us
    pallas_call x1, Pallas kernels, opening(): pl.pallas_call(functools.partial(open_kernel, hours_total), in_specs=[VME...  6.15 us
    ppermute x7, waiting for transfers between devices, swap(): return lax.ppermute(x, 'zone', [(i, i ^ step) for i in range(zone_parts)])  2.26 us
    reshape x1, local copies, waits for them, and re-layouts, on_device(): everyone = forcing.reshape(forcing.shape[0], hours_total * width)  1.32 us
    ppermute x1, waiting for transfers between devices, on_device(): message = message + lax.ppermute(message, 'hour', [(0, 1), (1, 0)])  1.16 us
  transfers between devices with their start and end apart: 9, of which 3 were waited for; matrix products, arithmetic and copies ran while one was open for 0% of the time, Pallas kernels for 32%

profile of v8, /device:TPU:0, one launch (start us, length us, event | category | flops | bytes accessed | tf_op | source)
XLA Modules:
  0.0 51.6 jit_solution(9424013969355599949)
XLA Ops:
  0.6 1.3 %reshape.16 = bf16[32,3072]{1,0:T(8,128)(2,1)S(1)} reshape(bf16[32,48,64]{2,1,0:T(8,128)(2,1)} %param.7) | data formatting | bytes 393216 | tf_op jit(solution)/shard_map/reshape | solution.py:407
  2.0 0.5 %collective-permute-start.1 = (bf16[32,1536]{1,0:T(8,128)(2,1)S(1)}, bf16[32,1536]{1,0:T(8,128)(2,1)S(1)}, u32[]{:S(2)}, u32[]{:S(2)}) collective-permute-start(bf16[32,1536]{1,0:T(8,128)(2,1)S(1)} %get-tuple-element.46), channel_id=1, source_target_pairs={{0,1},{1,0},{2,3},{3,2},{4,5},{5,4},{6,7},{7,6},{8,9},{9,8},{10,11... | collective-permute-start | bytes 294920 | tf_op jit(solution)/shard_map/ppermute | solution.py:410
  2.5 3.7 %collective-permute-start = (bf16[32,1536]{1,0:T(8,128)(2,1)S(1)}, bf16[32,1536]{1,0:T(8,128)(2,1)S(1)}, u32[]{:S(2)}, u32[]{:S(2)}) collective-permute-start(bf16[32,1536]{1,0:T(8,128)(2,1)S(1)} %get-tuple-element.47), channel_id=1, source_target_pairs={{0,8},{4,12},{8,0},{12,4},{1,9},{5,13},{9,1},{13,5},{2,10},{6,14},... | collective-permute-start | bytes 294920 | tf_op jit(solution)/shard_map/ppermute | solution.py:413
  6.2 0.0 collective-permute-done.1
  6.2 1.2 %collective-permute-start.2 = (bf16[32,1536]{1,0:T(8,128)(2,1)S(1)}, bf16[32,1536]{1,0:T(8,128)(2,1)S(1)}, u32[]{:S(2)}, u32[]{:S(2)}) collective-permute-start(bf16[32,1536]{1,0:T(8,128)(2,1)S(1)} %collective-permute-done.1), channel_id=1, source_target_pairs={{0,8},{4,12},{8,0},{12,4},{1,9},{5,13},{9,1},{13,5},{2,10},{6,14},... | collective-permute-start | bytes 294920 | tf_op jit(solution)/shard_map/ppermute | solution.py:413
  7.4 1.6 %collective-permute-start.4 = (bf16[64,1536]{1,0:T(8,128)(2,1)S(1)}, bf16[64,1536]{1,0:T(8,128)(2,1)S(1)}, u32[]{:S(2)}, u32[]{:S(2)}) collective-permute-start(bf16[64,1536]{1,0:T(8,128)(2,1)S(1)} %pad_maximum_fusion.mine_ref.refs_1_), channel_id=1, source_target_pairs={{0,4},{4,0},{8,12},{12,8},{1,5},{5,1},{9,13},{13,9},{2,6},{6,2},{1... | collective-permute-start | bytes 589832 | tf_op jit(solution)/shard_map/ppermute | solution.py:413
  9.0 6.2 %opening.1 = (bf16[12,256,1024]{2,1,0:T(8,128)(2,1)S(1)}, s32[1,1024]{1,0:T(1,128)S(1)}, f32[1,1024]{1,0:T(1,128)S(1)}, bf16[24,64,1024]{2,1,0:T(8,128)(2,1)S(1)...) custom-call(bf16[64,1536]{1,0:T(8,128)(2,1)S(1)} %pad_maximum_fusion.mine_ref.refs_1_, s32[8,128]{1,0:T(8,128)} %bitcast.3, ...), custom_call_target="tpu_custom_call" | custom-call | flops 1 | bytes 1 | tf_op jit(solution)/shard_map/opening/pallas_call | solution.py:150
  15.2 0.0 collective-permute-done.refs_0_.refs_2_
  15.2 2.7 %loss_slope.1 = (f32[8,32]{1,0:T(8,128)S(1)}, bf16[24,32,1024]{2,1,0:T(8,128)(2,1)S(1)}) custom-call(bf16[32,1536]{1,0:T(8,128)(2,1)S(1)} %collective-permute-done.refs_0_.refs_2_, bf16[12,256,1024]{2,1,0:T(8,128)(2,1)S(1)} %get-tuple-element.26.refs_1_.refs_3_.refs_2_, f32[1,1024]{1,0:T(1,128)S(1)} %get-tuple-element.27.refs_2_.refs_4_.refs_3_.refs_11_), custom_call_target="tpu_custom_call" | custom-call | flops 1 | bytes 1 | tf_op jit(solution)/shard_map/loss_slope/pallas_call | solution.py:33
  17.9 0.0 collective-permute-done.2.refs_1_
  17.9 0.5 collective-permute-start.3
  18.5 0.0 collective-permute-done.4.refs_0_
  18.5 5.8 %loss_slope_turn.1 = (f32[8,96]{1,0:T(8,128)S(1)}, bf16[24,96,1024]{2,1,0:T(8,128)(2,1)S(1)}, bf16[1536,128]{1,0:T(8,128)(2,1)S(1)}) custom-call(bf16[64,1536]{1,0:T(8,128)(2,1)S(1)} %collective-permute-done.4.refs_0_, bf16[32,1536]{1,0:T(8,128)(2,1)S(1)} %collective-permute-done.2.refs_1_, bf16[32,1536]{1,0:T(8,128)(2,1)S(1)} %collective-permute-done.refs_0_.refs_2_, ...), custom_call_target="tpu_custom_call" | custom-call | tf_op jit(solution)/shard_map/loss_slope_turn/pallas_call | solution.py:33
  24.3 0.1 collective-permute-done.3.refs_0_
  24.4 3.0 %loss.1 = f32[16,128]{1,0:T(8,128)S(1)} custom-call(bf16[64,1536]{1,0:T(8,128)(2,1)S(1)} %collective-permute-done.3.refs_0_, bf16[12,256,1024]{2,1,0:T(8,128)(2,1)S(1)} %get-tuple-element.26.refs_1_.refs_3_.refs_2_, f32[1,1024]{1,0:T(1,128)S(1)} %get-tuple-element.27.refs_2_.refs_4_.refs_3_.refs_11_, f32[8,64]{1,0:T(8,128)S(1)} %get-tuple-element.31.refs_3_, ...), custom_call_target="tpu_custom_call" | custom-call | tf_op jit(solution)/shard_map/loss/pallas_call | solution.py:33
  27.4 0.0 collective-permute-start.5
  27.5 1.2 %collective-permute-done.5 = f32[16,128]{1,0:T(8,128)S(1)} collective-permute-done((f32[16,128]{1,0:T(8,128)S(1)}, f32[16,128]{1,0:T(8,128)S(1)}, u32[]{:S(2)}, u32[]{:S(2)}) %collective-permute-start.5) | collective-permute-done | bytes 8224 | tf_op jit(solution)/shard_map/ppermute | solution.py:443
  28.6 1.5 %collective-permute-start.6 = (f32[16,128]{1,0:T(8,128)S(1)}, f32[16,128]{1,0:T(8,128)S(1)}, u32[]{:S(2)}, u32[]{:S(2)}) collective-permute-start(f32[16,128]{1,0:T(8,128)S(1)} %add.11.refs_0_), channel_id=1, source_target_pairs={{0,4},{4,0},{8,12},{12,8},{1,5},{5,1},{9,13},{13,9},{2,6},{6,2},{1... | collective-permute-start | bytes 24584 | tf_op jit(solution)/shard_map/ppermute | solution.py:413
  30.1 1.7 %collective-permute-start.7 = (f32[16,128]{1,0:T(8,128)S(1)}, f32[16,128]{1,0:T(8,128)S(1)}, u32[]{:S(2)}, u32[]{:S(2)}) collective-permute-start(f32[16,128]{1,0:T(8,128)S(1)} %add.11.refs_0_), channel_id=1, source_target_pairs={{0,8},{4,12},{8,0},{12,4},{1,9},{5,13},{9,1},{13,5},{2,10},{6,14},... | collective-permute-start | bytes 24584 | tf_op jit(solution)/shard_map/ppermute | solution.py:413
  31.8 1.2 %collective-permute-start.8 = (f32[16,128]{1,0:T(8,128)S(1)}, f32[16,128]{1,0:T(8,128)S(1)}, u32[]{:S(2)}, u32[]{:S(2)}) collective-permute-start(f32[16,128]{1,0:T(8,128)S(1)} %add.11.refs_0_), channel_id=1, source_target_pairs={{0,12},{4,8},{8,4},{12,0},{1,13},{5,9},{9,5},{13,1},{2,14},{6,10},... | collective-permute-start | bytes 24584 | tf_op jit(solution)/shard_map/ppermute | solution.py:413
  33.0 2.1 %slope_turn.1 = (bf16[24,64,1024]{2,1,0:T(8,128)(2,1)S(1)}, bf16[1536,128]{1,0:T(8,128)(2,1)S(1)}) custom-call(bf16[64,1536]{1,0:T(8,128)(2,1)S(1)} %collective-permute-done.3.refs_0_, bf16[64,1536]{1,0:T(8,128)(2,1)S(1)} %pad_maximum_fusion.mine_ref.refs_1_, bf16[12,256,1024]{2,1,0:T(8,128)(2,1)S(1)} %get-tuple-element.26.refs_1_.refs_3_.refs_2_, ...), custom_call_target="tpu_custom_call" | custom-call | tf_op jit(solution)/shard_map/slope_turn/pallas_call | solution.py:33
  35.1 0.0 collective-permute-done.6.refs_1_
  35.1 0.0 collective-permute-done.7.refs_2_
  35.1 2.1 %collective-permute-done.8.refs_3_ = f32[16,128]{1,0:T(8,128)S(1)} collective-permute-done((f32[16,128]{1,0:T(8,128)S(1)}, f32[16,128]{1,0:T(8,128)S(1)}, u32[]{:S(2)}, u32[]{:S(2)}) %collective-permute-start.8) | collective-permute-done | bytes 8224 | tf_op jit(solution)/shard_map/ppermute | solution.py:413
  37.2 3.0 %gradient.1 = f32[16,8,128]{2,1,0:T(8,128)S(1)} custom-call(f32[16,128]{1,0:T(8,128)S(1)} %add.11.refs_0_, f32[16,128]{1,0:T(8,128)S(1)} %collective-permute-done.6.refs_1_, f32[16,128]{1,0:T(8,128)S(1)} %collective-permute-done.7.refs_2_, f32[16,128]{1,0:T(8,128)S(1)} %collective-permute-done.8.refs_3_, bf16[1536,128]{1,0:T(8,128)(2,1)S(1)} %get-tuple-element.38.refs_4_, ...), custom_call_target="tpu_custom_call" | custom-call | tf_op jit(solution)/shard_map/gradient/pallas_call | solution.py:33
  40.3 10.2 %all_to_all.5.parts_ref = f32[16,8,128]{2,1,0:T(8,128)S(1)} all-to-all(f32[16,8,128]{2,1,0:T(8,128)S(1)} %gradient.1), channel_id=1, replica_groups=mesh['groups'=2,'zone'=4,'scen'=2,'hour'=2] {'zone','scen','hour'}, dimensions={0} | all-to-all | bytes 131072 | tf_op jit(solution)/shard_map/all_to_all | solution.py:468
  50.5 0.9 %finish.1 = (f32[4,64]{1,0:T(4,128)}, f32[1]{0:T(128)}) custom-call(f32[16,8,128]{2,1,0:T(8,128)S(1)} %all_to_all.5.parts_ref), custom_call_target="tpu_custom_call" | custom-call | tf_op jit(solution)/shard_map/finish/pallas_call | solution.py:471
  (4 shorter events, 0.1 us)
Async XLA Ops:
  2.0 4.2 %collective-permute-start.1 = (bf16[32,1536]{1,0:T(8,128)(2,1)S(1)}, bf16[32,1536]{1,0:T(8,128)(2,1)S(1)}, u32[]{:S(2)}, u32[]{:S(2)}) collective-permute-start(bf16[32,1536]{1,0:T(8,128)(2,1)S(1)} %get-tuple-element.46), channel_id=1, source_target_pairs={{0,1},{1,0},{2,3},{3,2},{4,5},{5,4},{6,7},{7,6},{8,9},{9,8},{10,11... | collective-permute-start | bytes 294920 | tf_op jit(solution)/shard_map/ppermute | solution.py:410
  2.5 12.7 %collective-permute-start = (bf16[32,1536]{1,0:T(8,128)(2,1)S(1)}, bf16[32,1536]{1,0:T(8,128)(2,1)S(1)}, u32[]{:S(2)}, u32[]{:S(2)}) collective-permute-start(bf16[32,1536]{1,0:T(8,128)(2,1)S(1)} %get-tuple-element.47), channel_id=1, source_target_pairs={{0,8},{4,12},{8,0},{12,4},{1,9},{5,13},{9,1},{13,5},{2,10},{6,14},... | collective-permute-start | bytes 294920 | tf_op jit(solution)/shard_map/ppermute | solution.py:413
  6.2 11.8 %collective-permute-start.2 = (bf16[32,1536]{1,0:T(8,128)(2,1)S(1)}, bf16[32,1536]{1,0:T(8,128)(2,1)S(1)}, u32[]{:S(2)}, u32[]{:S(2)}) collective-permute-start(bf16[32,1536]{1,0:T(8,128)(2,1)S(1)} %collective-permute-done.1), channel_id=1, source_target_pairs={{0,8},{4,12},{8,0},{12,4},{1,9},{5,13},{9,1},{13,5},{2,10},{6,14},... | collective-permute-start | bytes 294920 | tf_op jit(solution)/shard_map/ppermute | solution.py:413
  7.4 11.1 %collective-permute-start.4 = (bf16[64,1536]{1,0:T(8,128)(2,1)S(1)}, bf16[64,1536]{1,0:T(8,128)(2,1)S(1)}, u32[]{:S(2)}, u32[]{:S(2)}) collective-permute-start(bf16[64,1536]{1,0:T(8,128)(2,1)S(1)} %pad_maximum_fusion.mine_ref.refs_1_), channel_id=1, source_target_pairs={{0,4},{4,0},{8,12},{12,8},{1,5},{5,1},{9,13},{13,9},{2,6},{6,2},{1... | collective-permute-start | bytes 589832 | tf_op jit(solution)/shard_map/ppermute | solution.py:413
  17.9 6.5 %collective-permute-start.3 = (bf16[64,1536]{1,0:T(8,128)(2,1)S(1)}, bf16[64,1536]{1,0:T(8,128)(2,1)S(1)}, u32[]{:S(2)}, u32[]{:S(2)}) collective-permute-start(bf16[64,1536]{1,0:T(8,128)(2,1)S(1)} %pad_maximum_fusion.1), channel_id=1, source_target_pairs={{0,4},{4,0},{8,12},{12,8},{1,5},{5,1},{9,13},{13,9},{2,6},{6,2},{1... | collective-permute-start | bytes 589832 | tf_op jit(solution)/shard_map/ppermute | solution.py:413
  27.4 1.2 %collective-permute-start.5 = (f32[16,128]{1,0:T(8,128)S(1)}, f32[16,128]{1,0:T(8,128)S(1)}, u32[]{:S(2)}, u32[]{:S(2)}) collective-permute-start(f32[16,128]{1,0:T(8,128)S(1)} %loss.1), channel_id=1, source_target_pairs={{0,1},{1,0},{2,3},{3,2},{4,5},{5,4},{6,7},{7,6},{8,9},{9,8},{10,11... | collective-permute-start | bytes 24584 | tf_op jit(solution)/shard_map/ppermute | solution.py:443
  28.6 6.5 %collective-permute-start.6 = (f32[16,128]{1,0:T(8,128)S(1)}, f32[16,128]{1,0:T(8,128)S(1)}, u32[]{:S(2)}, u32[]{:S(2)}) collective-permute-start(f32[16,128]{1,0:T(8,128)S(1)} %add.11.refs_0_), channel_id=1, source_target_pairs={{0,4},{4,0},{8,12},{12,8},{1,5},{5,1},{9,13},{13,9},{2,6},{6,2},{1... | collective-permute-start | bytes 24584 | tf_op jit(solution)/shard_map/ppermute | solution.py:413
  30.1 5.0 %collective-permute-start.7 = (f32[16,128]{1,0:T(8,128)S(1)}, f32[16,128]{1,0:T(8,128)S(1)}, u32[]{:S(2)}, u32[]{:S(2)}) collective-permute-start(f32[16,128]{1,0:T(8,128)S(1)} %add.11.refs_0_), channel_id=1, source_target_pairs={{0,8},{4,12},{8,0},{12,4},{1,9},{5,13},{9,1},{13,5},{2,10},{6,14},... | collective-permute-start | bytes 24584 | tf_op jit(solution)/shard_map/ppermute | solution.py:413
  31.8 5.4 %collective-permute-start.8 = (f32[16,128]{1,0:T(8,128)S(1)}, f32[16,128]{1,0:T(8,128)S(1)}, u32[]{:S(2)}, u32[]{:S(2)}) collective-permute-start(f32[16,128]{1,0:T(8,128)S(1)} %add.11.refs_0_), channel_id=1, source_target_pairs={{0,12},{4,8},{8,4},{12,0},{1,13},{5,9},{9,5},{13,1},{2,14},{6,10},... | collective-permute-start | bytes 24584 | tf_op jit(solution)/shard_map/ppermute | solution.py:413

commit v9 on v8

--- a/solution.py
+++ b/solution.py
@@ -443,8 +443,9 @@
     message = message + lax.ppermute(message, "hour", [(0, 1), (1, 0)])
     slope3, ft1 = scan("slope_turn", [last], *common, extra=[mine])
     if zone_parts == 4:
-        others = [swap(message, k) for k in (1, 2, 3)]
+        others = [swap(message, k) for k in (3, 2, 1)]
         *others, slope3 = lax.optimization_barrier((*others, slope3))
+        others = others[::-1]
         messages = [message, *others]
     else:
         messages = [lax.psum(message, "zone")]

time: 51.8 us -> 51.2 us (0.988)
  waiting for transfers between devices: 3.42 us -> 1.97 us
  blocking collectives: 10.2 us -> 11 us
    ppermute x7, waiting for transfers between devices: 2.26 us -> 0.81 us  [swap(): return lax.ppermute(x, 'zone', [(i, i ^ step) for i in range(zone_parts)])]
    all_to_all x1, blocking collectives: 10.2 us -> 11 us  [on_device(): lax.all_to_all(parts, ('zone', 'scen', 'hour'), split_axis=0, concat_axis...]
  transfers between devices with their start and end apart: 9 -> 9, of which waited for: 3 -> 3; matrix products, arithmetic and copies ran while one was open for 0% -> 0% of each run, Pallas kernels for 32% -> 33%
where the time goes in v9:
time: 51.2 us; the launch traced here: 50.9 us
  Pallas kernels  23.7 us (46%)
  starting transfers between devices  12 us (23%)
  blocking collectives  11 us (21%)
  waiting for transfers between devices  1.97 us (4%)
  local copies, waits for them, and re-layouts  1.34 us (3%)
  between operations  0.89 us (2%)
    pallas_call x5, Pallas kernels, call(): pl.pallas_call(kernel, in_specs=[VMEM] * len(args), out_specs=[VMEM] * le...  16.6 us
    ppermute x7, starting transfers between devices, swap(): return lax.ppermute(x, 'zone', [(i, i ^ step) for i in range(zone_parts)])  11.4 us
    all_to_all x1, blocking collectives, on_device(): lax.all_to_all(parts, ('zone', 'scen', 'hour'), split_axis=0, concat_axis...  11 us
    pallas_call x1, Pallas kernels, opening(): pl.pallas_call(functools.partial(open_kernel, hours_total), in_specs=[VME...  6.15 us
    reshape x1, local copies, waits for them, and re-layouts, on_device(): everyone = forcing.reshape(forcing.shape[0], hours_total * width)  1.32 us
    ppermute x1, waiting for transfers between devices, on_device(): message = message + lax.ppermute(message, 'hour', [(0, 1), (1, 0)])  1.16 us
  transfers between devices with their start and end apart: 9, of which 3 were waited for; matrix products, arithmetic and copies ran while one was open for 0% of the time, Pallas kernels for 33%

profile of v9, /device:TPU:0, one launch (start us, length us, event | category | flops | bytes accessed | tf_op | source)
XLA Modules:
  0.0 50.9 jit_solution(4780846938950455316)
XLA Ops:
  0.6 1.3 %reshape.16 = bf16[32,3072]{1,0:T(8,128)(2,1)S(1)} reshape(bf16[32,48,64]{2,1,0:T(8,128)(2,1)} %param.7) | data formatting | bytes 393216 | tf_op jit(solution)/shard_map/reshape | solution.py:407
  2.0 0.5 %collective-permute-start.1 = (bf16[32,1536]{1,0:T(8,128)(2,1)S(1)}, bf16[32,1536]{1,0:T(8,128)(2,1)S(1)}, u32[]{:S(2)}, u32[]{:S(2)}) collective-permute-start(bf16[32,1536]{1,0:T(8,128)(2,1)S(1)} %get-tuple-element.46), channel_id=1, source_target_pairs={{0,1},{1,0},{2,3},{3,2},{4,5},{5,4},{6,7},{7,6},{8,9},{9,8},{10,11... | collective-permute-start | bytes 294920 | tf_op jit(solution)/shard_map/ppermute | solution.py:410
  2.5 3.7 %collective-permute-start = (bf16[32,1536]{1,0:T(8,128)(2,1)S(1)}, bf16[32,1536]{1,0:T(8,128)(2,1)S(1)}, u32[]{:S(2)}, u32[]{:S(2)}) collective-permute-start(bf16[32,1536]{1,0:T(8,128)(2,1)S(1)} %get-tuple-element.47), channel_id=1, source_target_pairs={{0,8},{4,12},{8,0},{12,4},{1,9},{5,13},{9,1},{13,5},{2,10},{6,14},... | collective-permute-start | bytes 294920 | tf_op jit(solution)/shard_map/ppermute | solution.py:413
  6.2 0.0 collective-permute-done.1
  6.2 1.2 %collective-permute-start.2 = (bf16[32,1536]{1,0:T(8,128)(2,1)S(1)}, bf16[32,1536]{1,0:T(8,128)(2,1)S(1)}, u32[]{:S(2)}, u32[]{:S(2)}) collective-permute-start(bf16[32,1536]{1,0:T(8,128)(2,1)S(1)} %collective-permute-done.1), channel_id=1, source_target_pairs={{0,8},{4,12},{8,0},{12,4},{1,9},{5,13},{9,1},{13,5},{2,10},{6,14},... | collective-permute-start | bytes 294920 | tf_op jit(solution)/shard_map/ppermute | solution.py:413
  7.4 1.6 %collective-permute-start.4 = (bf16[64,1536]{1,0:T(8,128)(2,1)S(1)}, bf16[64,1536]{1,0:T(8,128)(2,1)S(1)}, u32[]{:S(2)}, u32[]{:S(2)}) collective-permute-start(bf16[64,1536]{1,0:T(8,128)(2,1)S(1)} %pad_maximum_fusion.mine_ref.refs_1_), channel_id=1, source_target_pairs={{0,4},{4,0},{8,12},{12,8},{1,5},{5,1},{9,13},{13,9},{2,6},{6,2},{1... | collective-permute-start | bytes 589832 | tf_op jit(solution)/shard_map/ppermute | solution.py:413
  9.0 6.2 %opening.1 = (bf16[12,256,1024]{2,1,0:T(8,128)(2,1)S(1)}, s32[1,1024]{1,0:T(1,128)S(1)}, f32[1,1024]{1,0:T(1,128)S(1)}, bf16[24,64,1024]{2,1,0:T(8,128)(2,1)S(1)...) custom-call(bf16[64,1536]{1,0:T(8,128)(2,1)S(1)} %pad_maximum_fusion.mine_ref.refs_1_, s32[8,128]{1,0:T(8,128)} %bitcast.3, ...), custom_call_target="tpu_custom_call" | custom-call | flops 1 | bytes 1 | tf_op jit(solution)/shard_map/opening/pallas_call | solution.py:150
  15.2 0.0 collective-permute-done.refs_0_.refs_2_
  15.2 2.7 %loss_slope.1 = (f32[8,32]{1,0:T(8,128)S(1)}, bf16[24,32,1024]{2,1,0:T(8,128)(2,1)S(1)}) custom-call(bf16[32,1536]{1,0:T(8,128)(2,1)S(1)} %collective-permute-done.refs_0_.refs_2_, bf16[12,256,1024]{2,1,0:T(8,128)(2,1)S(1)} %get-tuple-element.26.refs_1_.refs_3_.refs_2_, f32[1,1024]{1,0:T(1,128)S(1)} %get-tuple-element.27.refs_2_.refs_4_.refs_3_.refs_11_), custom_call_target="tpu_custom_call" | custom-call | flops 1 | bytes 1 | tf_op jit(solution)/shard_map/loss_slope/pallas_call | solution.py:33
  17.9 0.0 collective-permute-done.2.refs_1_
  17.9 0.5 %collective-permute-start.3 = (bf16[64,1536]{1,0:T(8,128)(2,1)S(1)}, bf16[64,1536]{1,0:T(8,128)(2,1)S(1)}, u32[]{:S(2)}, u32[]{:S(2)}) collective-permute-start(bf16[64,1536]{1,0:T(8,128)(2,1)S(1)} %pad_maximum_fusion.1), channel_id=1, source_target_pairs={{0,4},{4,0},{8,12},{12,8},{1,5},{5,1},{9,13},{13,9},{2,6},{6,2},{1... | collective-permute-start | bytes 589832 | tf_op jit(solution)/shard_map/ppermute | solution.py:413
  18.5 0.0 collective-permute-done.4.refs_0_
  18.5 5.8 %loss_slope_turn.1 = (f32[8,96]{1,0:T(8,128)S(1)}, bf16[24,96,1024]{2,1,0:T(8,128)(2,1)S(1)}, bf16[1536,128]{1,0:T(8,128)(2,1)S(1)}) custom-call(bf16[64,1536]{1,0:T(8,128)(2,1)S(1)} %collective-permute-done.4.refs_0_, bf16[32,1536]{1,0:T(8,128)(2,1)S(1)} %collective-permute-done.2.refs_1_, bf16[32,1536]{1,0:T(8,128)(2,1)S(1)} %collective-permute-done.refs_0_.refs_2_, ...), custom_call_target="tpu_custom_call" | custom-call | tf_op jit(solution)/shard_map/loss_slope_turn/pallas_call | solution.py:33
  24.3 0.1 collective-permute-done.3.refs_0_
  24.4 3.0 %loss.1 = f32[16,128]{1,0:T(8,128)S(1)} custom-call(bf16[64,1536]{1,0:T(8,128)(2,1)S(1)} %collective-permute-done.3.refs_0_, bf16[12,256,1024]{2,1,0:T(8,128)(2,1)S(1)} %get-tuple-element.26.refs_1_.refs_3_.refs_2_, f32[1,1024]{1,0:T(1,128)S(1)} %get-tuple-element.27.refs_2_.refs_4_.refs_3_.refs_11_, f32[8,64]{1,0:T(8,128)S(1)} %get-tuple-element.31.refs_3_, ...), custom_call_target="tpu_custom_call" | custom-call | tf_op jit(solution)/shard_map/loss/pallas_call | solution.py:33
  27.4 0.0 collective-permute-start.5
  27.5 1.2 %collective-permute-done.5 = f32[16,128]{1,0:T(8,128)S(1)} collective-permute-done((f32[16,128]{1,0:T(8,128)S(1)}, f32[16,128]{1,0:T(8,128)S(1)}, u32[]{:S(2)}, u32[]{:S(2)}) %collective-permute-start.5) | collective-permute-done | bytes 8224 | tf_op jit(solution)/shard_map/ppermute | solution.py:443
  28.6 2.6 %collective-permute-start.6 = (f32[16,128]{1,0:T(8,128)S(1)}, f32[16,128]{1,0:T(8,128)S(1)}, u32[]{:S(2)}, u32[]{:S(2)}) collective-permute-start(f32[16,128]{1,0:T(8,128)S(1)} %add.11.refs_0_), channel_id=1, source_target_pairs={{0,12},{4,8},{8,4},{12,0},{1,13},{5,9},{9,5},{13,1},{2,14},{6,10},... | collective-permute-start | bytes 24584 | tf_op jit(solution)/shard_map/ppermute | solution.py:413
  31.2 0.3 collective-permute-start.7
  31.5 1.5 %collective-permute-start.8 = (f32[16,128]{1,0:T(8,128)S(1)}, f32[16,128]{1,0:T(8,128)S(1)}, u32[]{:S(2)}, u32[]{:S(2)}) collective-permute-start(f32[16,128]{1,0:T(8,128)S(1)} %add.11.refs_0_), channel_id=1, source_target_pairs={{0,4},{4,0},{8,12},{12,8},{1,5},{5,1},{9,13},{13,9},{2,6},{6,2},{1... | collective-permute-start | bytes 24584 | tf_op jit(solution)/shard_map/ppermute | solution.py:413
  33.0 2.1 %slope_turn.1 = (bf16[24,64,1024]{2,1,0:T(8,128)(2,1)S(1)}, bf16[1536,128]{1,0:T(8,128)(2,1)S(1)}) custom-call(bf16[64,1536]{1,0:T(8,128)(2,1)S(1)} %collective-permute-done.3.refs_0_, bf16[64,1536]{1,0:T(8,128)(2,1)S(1)} %pad_maximum_fusion.mine_ref.refs_1_, bf16[12,256,1024]{2,1,0:T(8,128)(2,1)S(1)} %get-tuple-element.26.refs_1_.refs_3_.refs_2_, ...), custom_call_target="tpu_custom_call" | custom-call | tf_op jit(solution)/shard_map/slope_turn/pallas_call | solution.py:33
  35.1 0.0 collective-permute-done.6.refs_3_
  35.1 0.6 %collective-permute-done.7.refs_2_ = f32[16,128]{1,0:T(8,128)S(1)} collective-permute-done((f32[16,128]{1,0:T(8,128)S(1)}, f32[16,128]{1,0:T(8,128)S(1)}, u32[]{:S(2)}, u32[]{:S(2)}) %collective-permute-start.7) | collective-permute-done | bytes 8224 | tf_op jit(solution)/shard_map/ppermute | solution.py:413
  35.8 0.0 collective-permute-done.8.refs_1_
  35.8 3.0 %gradient.1 = f32[16,8,128]{2,1,0:T(8,128)S(1)} custom-call(f32[16,128]{1,0:T(8,128)S(1)} %add.11.refs_0_, f32[16,128]{1,0:T(8,128)S(1)} %collective-permute-done.8.refs_1_, f32[16,128]{1,0:T(8,128)S(1)} %collective-permute-done.7.refs_2_, f32[16,128]{1,0:T(8,128)S(1)} %collective-permute-done.6.refs_3_, bf16[1536,128]{1,0:T(8,128)(2,1)S(1)} %get-tuple-element.38.refs_4_, ...), custom_call_target="tpu_custom_call" | custom-call | tf_op jit(solution)/shard_map/gradient/pallas_call | solution.py:33
  38.8 11.0 %all_to_all.5.parts_ref = f32[16,8,128]{2,1,0:T(8,128)S(1)} all-to-all(f32[16,8,128]{2,1,0:T(8,128)S(1)} %gradient.1), channel_id=1, replica_groups=mesh['groups'=2,'zone'=4,'scen'=2,'hour'=2] {'zone','scen','hour'}, dimensions={0} | all-to-all | bytes 131072 | tf_op jit(solution)/shard_map/all_to_all | solution.py:469
  49.8 0.9 %finish.1 = (f32[4,64]{1,0:T(4,128)}, f32[1]{0:T(128)}) custom-call(f32[16,8,128]{2,1,0:T(8,128)S(1)} %all_to_all.5.parts_ref), custom_call_target="tpu_custom_call" | custom-call | tf_op jit(solution)/shard_map/finish/pallas_call | solution.py:472
  (4 shorter events, 0.1 us)
Async XLA Ops:
  2.0 4.2 %collective-permute-start.1 = (bf16[32,1536]{1,0:T(8,128)(2,1)S(1)}, bf16[32,1536]{1,0:T(8,128)(2,1)S(1)}, u32[]{:S(2)}, u32[]{:S(2)}) collective-permute-start(bf16[32,1536]{1,0:T(8,128)(2,1)S(1)} %get-tuple-element.46), channel_id=1, source_target_pairs={{0,1},{1,0},{2,3},{3,2},{4,5},{5,4},{6,7},{7,6},{8,9},{9,8},{10,11... | collective-permute-start | bytes 294920 | tf_op jit(solution)/shard_map/ppermute | solution.py:410
  2.5 12.7 %collective-permute-start = (bf16[32,1536]{1,0:T(8,128)(2,1)S(1)}, bf16[32,1536]{1,0:T(8,128)(2,1)S(1)}, u32[]{:S(2)}, u32[]{:S(2)}) collective-permute-start(bf16[32,1536]{1,0:T(8,128)(2,1)S(1)} %get-tuple-element.47), channel_id=1, source_target_pairs={{0,8},{4,12},{8,0},{12,4},{1,9},{5,13},{9,1},{13,5},{2,10},{6,14},... | collective-permute-start | bytes 294920 | tf_op jit(solution)/shard_map/ppermute | solution.py:413
  6.2 11.8 %collective-permute-start.2 = (bf16[32,1536]{1,0:T(8,128)(2,1)S(1)}, bf16[32,1536]{1,0:T(8,128)(2,1)S(1)}, u32[]{:S(2)}, u32[]{:S(2)}) collective-permute-start(bf16[32,1536]{1,0:T(8,128)(2,1)S(1)} %collective-permute-done.1), channel_id=1, source_target_pairs={{0,8},{4,12},{8,0},{12,4},{1,9},{5,13},{9,1},{13,5},{2,10},{6,14},... | collective-permute-start | bytes 294920 | tf_op jit(solution)/shard_map/ppermute | solution.py:413
  7.4 11.1 %collective-permute-start.4 = (bf16[64,1536]{1,0:T(8,128)(2,1)S(1)}, bf16[64,1536]{1,0:T(8,128)(2,1)S(1)}, u32[]{:S(2)}, u32[]{:S(2)}) collective-permute-start(bf16[64,1536]{1,0:T(8,128)(2,1)S(1)} %pad_maximum_fusion.mine_ref.refs_1_), channel_id=1, source_target_pairs={{0,4},{4,0},{8,12},{12,8},{1,5},{5,1},{9,13},{13,9},{2,6},{6,2},{1... | collective-permute-start | bytes 589832 | tf_op jit(solution)/shard_map/ppermute | solution.py:413
  17.9 6.5 %collective-permute-start.3 = (bf16[64,1536]{1,0:T(8,128)(2,1)S(1)}, bf16[64,1536]{1,0:T(8,128)(2,1)S(1)}, u32[]{:S(2)}, u32[]{:S(2)}) collective-permute-start(bf16[64,1536]{1,0:T(8,128)(2,1)S(1)} %pad_maximum_fusion.1), channel_id=1, source_target_pairs={{0,4},{4,0},{8,12},{12,8},{1,5},{5,1},{9,13},{13,9},{2,6},{6,2},{1... | collective-permute-start | bytes 589832 | tf_op jit(solution)/shard_map/ppermute | solution.py:413
  27.4 1.2 %collective-permute-start.5 = (f32[16,128]{1,0:T(8,128)S(1)}, f32[16,128]{1,0:T(8,128)S(1)}, u32[]{:S(2)}, u32[]{:S(2)}) collective-permute-start(f32[16,128]{1,0:T(8,128)S(1)} %loss.1), channel_id=1, source_target_pairs={{0,1},{1,0},{2,3},{3,2},{4,5},{5,4},{6,7},{7,6},{8,9},{9,8},{10,11... | collective-permute-start | bytes 24584 | tf_op jit(solution)/shard_map/ppermute | solution.py:443
  28.6 6.5 %collective-permute-start.6 = (f32[16,128]{1,0:T(8,128)S(1)}, f32[16,128]{1,0:T(8,128)S(1)}, u32[]{:S(2)}, u32[]{:S(2)}) collective-permute-start(f32[16,128]{1,0:T(8,128)S(1)} %add.11.refs_0_), channel_id=1, source_target_pairs={{0,12},{4,8},{8,4},{12,0},{1,13},{5,9},{9,5},{13,1},{2,14},{6,10},... | collective-permute-start | bytes 24584 | tf_op jit(solution)/shard_map/ppermute | solution.py:413
  31.2 4.5 %collective-permute-start.7 = (f32[16,128]{1,0:T(8,128)S(1)}, f32[16,128]{1,0:T(8,128)S(1)}, u32[]{:S(2)}, u32[]{:S(2)}) collective-permute-start(f32[16,128]{1,0:T(8,128)S(1)} %add.11.refs_0_), channel_id=1, source_target_pairs={{0,8},{4,12},{8,0},{12,4},{1,9},{5,13},{9,1},{13,5},{2,10},{6,14},... | collective-permute-start | bytes 24584 | tf_op jit(solution)/shard_map/ppermute | solution.py:413
  31.5 4.2 %collective-permute-start.8 = (f32[16,128]{1,0:T(8,128)S(1)}, f32[16,128]{1,0:T(8,128)S(1)}, u32[]{:S(2)}, u32[]{:S(2)}) collective-permute-start(f32[16,128]{1,0:T(8,128)S(1)} %add.11.refs_0_), channel_id=1, source_target_pairs={{0,4},{4,0},{8,12},{12,8},{1,5},{5,1},{9,13},{13,9},{2,6},{6,2},{1... | collective-permute-start | bytes 24584 | tf_op jit(solution)/shard_map/ppermute | solution.py:413

commit v10 on v9

--- a/solution.py
+++ b/solution.py
@@ -290,7 +290,7 @@
             out_ref[...] = message
 
 
-def scan(kind, rows_in, rhs, area, hours_total, order, extra=(), priors=(), unroll=6, cost=None):
+def scan(kind, rows_in, rhs, area, hours_total, order, extra=(), priors=(), unroll=12, cost=None):
     hours, zones = 2 * rhs.shape[0], rhs.shape[2]
     rows = sum(f.shape[0] for f in rows_in)
     outs = []
@@ -316,7 +316,7 @@
 
 
 def gradient_kernel(
-    hours_total, gain, owners, order, messages, *refs
+    hours_total, gain, order, messages, *refs
 ):
     msg_refs, refs = refs[:messages], refs[messages:]
     ft_refs, slope_refs, refs = refs[:2], refs[2:6], refs[6:]
@@ -362,12 +362,10 @@
     lax.fori_loop(0, hours, hour_step, 0, unroll=hours // 2)
 
     grad = acc_ref[...] * area_ref[...]
-    blocks, pad, _ = out_ref.shape
-    index = lax.broadcasted_iota(jnp.int32, (blocks * pad, zones), 0)
-    within = index % pad
-    design = jnp.where(within < owners, (index // pad) * owners + within, -1)
-    onehot = (design == plan_ref[...]).astype(F32).astype(BF16)
-    sens = jnp.zeros((blocks * pad, width), F32)
+    blocks, owners, _ = out_ref.shape
+    index = lax.broadcasted_iota(jnp.int32, (blocks * owners, zones), 0)
+    onehot = (index == plan_ref[...]).astype(F32).astype(BF16)
+    sens = jnp.zeros((blocks * owners, width), F32)
     for _ in range(3):
         part = grad.astype(BF16)
         grad = grad - part.astype(F32)
@@ -375,8 +373,9 @@
             onehot, part, (((1,), (1,)), ((), ())), preferred_element_type=F32
         )
     sens = sens * (0.5 * gain / weight)
-    out_ref[:, :, :width] = sens.reshape(blocks, pad, width)
-    lane = lax.broadcasted_iota(jnp.int32, (blocks, pad, LANES - width), 2)
+    for k in range(blocks):
+        out_ref[k, :, :width] = sens[k * owners : (k + 1) * owners]
+    lane = lax.broadcasted_iota(jnp.int32, (blocks, owners, LANES - width), 2)
     out_ref[:, :, width:] = jnp.where(lane == 0, peak, exp_total)
 
 
@@ -389,7 +388,7 @@
     scale = jnp.exp(peaks - peak)
     total = jnp.sum((scale * totals)[:, 0:1, :]) * (scen_parts / devices)
     summed = jnp.sum(parts[:, :, :width] * scale, axis=0) / total
-    sens_ref[...] = summed[: sens_ref.shape[0]]
+    sens_ref[...] = summed
     log_total = jnp.max(jnp.log(jnp.full((8, LANES), total, F32)))
     objective_ref[0] = (peak + log_total) / SHARPNESS - 0.5
 
@@ -453,12 +452,11 @@
     designs = window_params.shape[0]
     devices = zone_parts * scen_parts * hour_parts
     owners = designs // devices
-    pad = -(-owners // 8) * 8
     gain = math.sqrt(width * zones * zone_parts * hours_total * designs)
     (parts,) = call(
-        functools.partial(gradient_kernel, hours_total, gain, owners, kept, len(messages)),
+        functools.partial(gradient_kernel, hours_total, gain, kept, len(messages)),
         "gradient",
-        [((devices, pad, LANES), F32)],
+        [((devices, owners, LANES), F32)],
         [*messages, ft0, ft1, slope1, slope2, slope0, slope3, near_response, area, plan],
         [
             pltpu.VMEM((width, zones), F32),

time: 51.2 us -> 50.4 us (0.984)
  Pallas kernels: 23.7 us -> 23 us
    pallas_call x5, Pallas kernels: 16.6 us -> 15.9 us  [call(): pl.pallas_call(kernel, in_specs=[VMEM] * len(args), out_specs=[VMEM] * le...]
  transfers between devices with their start and end apart: 9 -> 9, of which waited for: 3 -> 3; matrix products, arithmetic and copies ran while one was open for 0% -> 0% of each run, Pallas kernels for 33% -> 32%
where the time goes in v10:
time: 50.4 us; the launch traced here: 50.2 us
  Pallas kernels  23 us (46%)
  starting transfers between devices  12 us (24%)
  blocking collectives  10.8 us (21%)
  waiting for transfers between devices  2.23 us (4%)
  local copies, waits for them, and re-layouts  1.34 us (3%)
  between operations  0.88 us (2%)
    pallas_call x5, Pallas kernels, call(): pl.pallas_call(kernel, in_specs=[VMEM] * len(args), out_specs=[VMEM] * le...  15.9 us
    ppermute x7, starting transfers between devices, swap(): return lax.ppermute(x, 'zone', [(i, i ^ step) for i in range(zone_parts)])  11.4 us
    all_to_all x1, blocking collectives, on_device(): lax.all_to_all(parts, ('zone', 'scen', 'hour'), split_axis=0, concat_axis...  10.8 us
    pallas_call x1, Pallas kernels, opening(): pl.pallas_call(functools.partial(open_kernel, hours_total), in_specs=[VME...  6.15 us
    reshape x1, local copies, waits for them, and re-layouts, on_device(): everyone = forcing.reshape(forcing.shape[0], hours_total * width)  1.32 us
    ppermute x1, waiting for transfers between devices, on_device(): message = message + lax.ppermute(message, 'hour', [(0, 1), (1, 0)])  1.16 us
    ppermute x7, waiting for transfers between devices, swap(): return lax.ppermute(x, 'zone', [(i, i ^ step) for i in range(zone_parts)])  1.07 us
  transfers between devices with their start and end apart: 9, of which 3 were waited for; matrix products, arithmetic and copies ran while one was open for 0% of the time, Pallas kernels for 32%

profile of v10, /device:TPU:0, one launch (start us, length us, event | category | flops | bytes accessed | tf_op | source)
XLA Modules:
  0.0 50.2 jit_solution(14811772900829071327)
XLA Ops:
  0.6 1.3 %reshape.16 = bf16[32,3072]{1,0:T(8,128)(2,1)S(1)} reshape(bf16[32,48,64]{2,1,0:T(8,128)(2,1)} %param.7) | data formatting | bytes 393216 | tf_op jit(solution)/shard_map/reshape | solution.py:406
  2.0 0.5 %collective-permute-start.1 = (bf16[32,1536]{1,0:T(8,128)(2,1)S(1)}, bf16[32,1536]{1,0:T(8,128)(2,1)S(1)}, u32[]{:S(2)}, u32[]{:S(2)}) collective-permute-start(bf16[32,1536]{1,0:T(8,128)(2,1)S(1)} %get-tuple-element.46), channel_id=1, source_target_pairs={{0,1},{1,0},{2,3},{3,2},{4,5},{5,4},{6,7},{7,6},{8,9},{9,8},{10,11... | collective-permute-start | bytes 294920 | tf_op jit(solution)/shard_map/ppermute | solution.py:409
  2.5 3.7 %collective-permute-start = (bf16[32,1536]{1,0:T(8,128)(2,1)S(1)}, bf16[32,1536]{1,0:T(8,128)(2,1)S(1)}, u32[]{:S(2)}, u32[]{:S(2)}) collective-permute-start(bf16[32,1536]{1,0:T(8,128)(2,1)S(1)} %get-tuple-element.47), channel_id=1, source_target_pairs={{0,8},{4,12},{8,0},{12,4},{1,9},{5,13},{9,1},{13,5},{2,10},{6,14},... | collective-permute-start | bytes 294920 | tf_op jit(solution)/shard_map/ppermute | solution.py:412
  6.2 0.0 collective-permute-done.1
  6.2 1.2 %collective-permute-start.2 = (bf16[32,1536]{1,0:T(8,128)(2,1)S(1)}, bf16[32,1536]{1,0:T(8,128)(2,1)S(1)}, u32[]{:S(2)}, u32[]{:S(2)}) collective-permute-start(bf16[32,1536]{1,0:T(8,128)(2,1)S(1)} %collective-permute-done.1), channel_id=1, source_target_pairs={{0,8},{4,12},{8,0},{12,4},{1,9},{5,13},{9,1},{13,5},{2,10},{6,14},... | collective-permute-start | bytes 294920 | tf_op jit(solution)/shard_map/ppermute | solution.py:412
  7.4 1.6 %collective-permute-start.4 = (bf16[64,1536]{1,0:T(8,128)(2,1)S(1)}, bf16[64,1536]{1,0:T(8,128)(2,1)S(1)}, u32[]{:S(2)}, u32[]{:S(2)}) collective-permute-start(bf16[64,1536]{1,0:T(8,128)(2,1)S(1)} %pad_maximum_fusion.mine_ref.refs_1_), channel_id=1, source_target_pairs={{0,4},{4,0},{8,12},{12,8},{1,5},{5,1},{9,13},{13,9},{2,6},{6,2},{1... | collective-permute-start | bytes 589832 | tf_op jit(solution)/shard_map/ppermute | solution.py:412
  9.0 6.2 %opening.1 = (bf16[12,256,1024]{2,1,0:T(8,128)(2,1)S(1)}, s32[1,1024]{1,0:T(1,128)S(1)}, f32[1,1024]{1,0:T(1,128)S(1)}, bf16[24,64,1024]{2,1,0:T(8,128)(2,1)S(1)...) custom-call(bf16[64,1536]{1,0:T(8,128)(2,1)S(1)} %pad_maximum_fusion.mine_ref.refs_1_, s32[8,128]{1,0:T(8,128)} %bitcast.3, ...), custom_call_target="tpu_custom_call" | custom-call | flops 1 | bytes 1 | tf_op jit(solution)/shard_map/opening/pallas_call | solution.py:150
  15.2 0.0 collective-permute-done.refs_0_.refs_2_
  15.2 2.4 %loss_slope.1 = (f32[8,32]{1,0:T(8,128)S(1)}, bf16[24,32,1024]{2,1,0:T(8,128)(2,1)S(1)}) custom-call(bf16[32,1536]{1,0:T(8,128)(2,1)S(1)} %collective-permute-done.refs_0_.refs_2_, bf16[12,256,1024]{2,1,0:T(8,128)(2,1)S(1)} %get-tuple-element.26.refs_1_.refs_3_.refs_2_, f32[1,1024]{1,0:T(1,128)S(1)} %get-tuple-element.27.refs_2_.refs_4_.refs_3_.refs_11_), custom_call_target="tpu_custom_call" | custom-call | flops 1 | bytes 1 | tf_op jit(solution)/shard_map/loss_slope/pallas_call | solution.py:33
  17.6 0.0 collective-permute-done.2.refs_1_
  17.6 0.5 %collective-permute-start.3 = (bf16[64,1536]{1,0:T(8,128)(2,1)S(1)}, bf16[64,1536]{1,0:T(8,128)(2,1)S(1)}, u32[]{:S(2)}, u32[]{:S(2)}) collective-permute-start(bf16[64,1536]{1,0:T(8,128)(2,1)S(1)} %pad_maximum_fusion.1), channel_id=1, source_target_pairs={{0,4},{4,0},{8,12},{12,8},{1,5},{5,1},{9,13},{13,9},{2,6},{6,2},{1... | collective-permute-start | bytes 589832 | tf_op jit(solution)/shard_map/ppermute | solution.py:412
  18.2 0.0 collective-permute-done.4.refs_0_
  18.2 5.8 %loss_slope_turn.1 = (f32[8,96]{1,0:T(8,128)S(1)}, bf16[24,96,1024]{2,1,0:T(8,128)(2,1)S(1)}, bf16[1536,128]{1,0:T(8,128)(2,1)S(1)}) custom-call(bf16[64,1536]{1,0:T(8,128)(2,1)S(1)} %collective-permute-done.4.refs_0_, bf16[32,1536]{1,0:T(8,128)(2,1)S(1)} %collective-permute-done.2.refs_1_, bf16[32,1536]{1,0:T(8,128)(2,1)S(1)} %collective-permute-done.refs_0_.refs_2_, ...), custom_call_target="tpu_custom_call" | custom-call | tf_op jit(solution)/shard_map/loss_slope_turn/pallas_call | solution.py:33
  23.9 0.2 collective-permute-done.3.refs_0_
  24.1 2.8 %loss.1 = f32[16,128]{1,0:T(8,128)S(1)} custom-call(bf16[64,1536]{1,0:T(8,128)(2,1)S(1)} %collective-permute-done.3.refs_0_, bf16[12,256,1024]{2,1,0:T(8,128)(2,1)S(1)} %get-tuple-element.26.refs_1_.refs_3_.refs_2_, f32[1,1024]{1,0:T(1,128)S(1)} %get-tuple-element.27.refs_2_.refs_4_.refs_3_.refs_11_, f32[8,64]{1,0:T(8,128)S(1)} %get-tuple-element.31.refs_3_, ...), custom_call_target="tpu_custom_call" | custom-call | tf_op jit(solution)/shard_map/loss/pallas_call | solution.py:33
  26.9 0.0 collective-permute-start.5
  26.9 1.2 %collective-permute-done.5 = f32[16,128]{1,0:T(8,128)S(1)} collective-permute-done((f32[16,128]{1,0:T(8,128)S(1)}, f32[16,128]{1,0:T(8,128)S(1)}, u32[]{:S(2)}, u32[]{:S(2)}) %collective-permute-start.5) | collective-permute-done | bytes 8224 | tf_op jit(solution)/shard_map/ppermute | solution.py:442
  28.1 2.7 %collective-permute-start.6 = (f32[16,128]{1,0:T(8,128)S(1)}, f32[16,128]{1,0:T(8,128)S(1)}, u32[]{:S(2)}, u32[]{:S(2)}) collective-permute-start(f32[16,128]{1,0:T(8,128)S(1)} %add.11.refs_0_), channel_id=1, source_target_pairs={{0,12},{4,8},{8,4},{12,0},{1,13},{5,9},{9,5},{13,1},{2,14},{6,10},... | collective-permute-start | bytes 24584 | tf_op jit(solution)/shard_map/ppermute | solution.py:412
  30.8 0.2 collective-permute-start.7
  31.0 1.5 %collective-permute-start.8 = (f32[16,128]{1,0:T(8,128)S(1)}, f32[16,128]{1,0:T(8,128)S(1)}, u32[]{:S(2)}, u32[]{:S(2)}) collective-permute-start(f32[16,128]{1,0:T(8,128)S(1)} %add.11.refs_0_), channel_id=1, source_target_pairs={{0,4},{4,0},{8,12},{12,8},{1,5},{5,1},{9,13},{13,9},{2,6},{6,2},{1... | collective-permute-start | bytes 24584 | tf_op jit(solution)/shard_map/ppermute | solution.py:412
  32.5 1.9 %slope_turn.1 = (bf16[24,64,1024]{2,1,0:T(8,128)(2,1)S(1)}, bf16[1536,128]{1,0:T(8,128)(2,1)S(1)}) custom-call(bf16[64,1536]{1,0:T(8,128)(2,1)S(1)} %collective-permute-done.3.refs_0_, bf16[64,1536]{1,0:T(8,128)(2,1)S(1)} %pad_maximum_fusion.mine_ref.refs_1_, bf16[12,256,1024]{2,1,0:T(8,128)(2,1)S(1)} %get-tuple-element.26.refs_1_.refs_3_.refs_2_, ...), custom_call_target="tpu_custom_call" | custom-call | tf_op jit(solution)/shard_map/slope_turn/pallas_call | solution.py:33
  34.4 0.0 collective-permute-done.6.refs_3_
  34.4 0.9 %collective-permute-done.7.refs_2_ = f32[16,128]{1,0:T(8,128)S(1)} collective-permute-done((f32[16,128]{1,0:T(8,128)S(1)}, f32[16,128]{1,0:T(8,128)S(1)}, u32[]{:S(2)}, u32[]{:S(2)}) %collective-permute-start.7) | collective-permute-done | bytes 8224 | tf_op jit(solution)/shard_map/ppermute | solution.py:412
  35.3 0.0 collective-permute-done.8.refs_1_
  35.3 3.0 %gradient.1 = f32[16,4,128]{2,1,0:T(4,128)S(1)} custom-call(f32[16,128]{1,0:T(8,128)S(1)} %add.11.refs_0_, f32[16,128]{1,0:T(8,128)S(1)} %collective-permute-done.8.refs_1_, f32[16,128]{1,0:T(8,128)S(1)} %collective-permute-done.7.refs_2_, f32[16,128]{1,0:T(8,128)S(1)} %collective-permute-done.6.refs_3_, bf16[1536,128]{1,0:T(8,128)(2,1)S(1)} %get-tuple-element.38.refs_4_, ...), custom_call_target="tpu_custom_call" | custom-call | tf_op jit(solution)/shard_map/gradient/pallas_call | solution.py:33
  38.3 10.8 %all_to_all.5.parts_ref = f32[16,4,128]{2,1,0:T(4,128)S(1)} all-to-all(f32[16,4,128]{2,1,0:T(4,128)S(1)} %gradient.1), channel_id=1, replica_groups=mesh['groups'=2,'zone'=4,'scen'=2,'hour'=2] {'zone','scen','hour'}, dimensions={0} | all-to-all | bytes 65536 | tf_op jit(solution)/shard_map/all_to_all | solution.py:467
  49.1 0.9 %finish.1 = (f32[4,64]{1,0:T(4,128)}, f32[1]{0:T(128)}) custom-call(f32[16,4,128]{2,1,0:T(4,128)S(1)} %all_to_all.5.parts_ref), custom_call_target="tpu_custom_call" | custom-call | tf_op jit(solution)/shard_map/finish/pallas_call | solution.py:470
  (4 shorter events, 0.1 us)
Async XLA Ops:
  2.0 4.2 %collective-permute-start.1 = (bf16[32,1536]{1,0:T(8,128)(2,1)S(1)}, bf16[32,1536]{1,0:T(8,128)(2,1)S(1)}, u32[]{:S(2)}, u32[]{:S(2)}) collective-permute-start(bf16[32,1536]{1,0:T(8,128)(2,1)S(1)} %get-tuple-element.46), channel_id=1, source_target_pairs={{0,1},{1,0},{2,3},{3,2},{4,5},{5,4},{6,7},{7,6},{8,9},{9,8},{10,11... | collective-permute-start | bytes 294920 | tf_op jit(solution)/shard_map/ppermute | solution.py:409
  2.5 12.7 %collective-permute-start = (bf16[32,1536]{1,0:T(8,128)(2,1)S(1)}, bf16[32,1536]{1,0:T(8,128)(2,1)S(1)}, u32[]{:S(2)}, u32[]{:S(2)}) collective-permute-start(bf16[32,1536]{1,0:T(8,128)(2,1)S(1)} %get-tuple-element.47), channel_id=1, source_target_pairs={{0,8},{4,12},{8,0},{12,4},{1,9},{5,13},{9,1},{13,5},{2,10},{6,14},... | collective-permute-start | bytes 294920 | tf_op jit(solution)/shard_map/ppermute | solution.py:412
  6.2 11.4 %collective-permute-start.2 = (bf16[32,1536]{1,0:T(8,128)(2,1)S(1)}, bf16[32,1536]{1,0:T(8,128)(2,1)S(1)}, u32[]{:S(2)}, u32[]{:S(2)}) collective-permute-start(bf16[32,1536]{1,0:T(8,128)(2,1)S(1)} %collective-permute-done.1), channel_id=1, source_target_pairs={{0,8},{4,12},{8,0},{12,4},{1,9},{5,13},{9,1},{13,5},{2,10},{6,14},... | collective-permute-start | bytes 294920 | tf_op jit(solution)/shard_map/ppermute | solution.py:412
  7.4 10.8 %collective-permute-start.4 = (bf16[64,1536]{1,0:T(8,128)(2,1)S(1)}, bf16[64,1536]{1,0:T(8,128)(2,1)S(1)}, u32[]{:S(2)}, u32[]{:S(2)}) collective-permute-start(bf16[64,1536]{1,0:T(8,128)(2,1)S(1)} %pad_maximum_fusion.mine_ref.refs_1_), channel_id=1, source_target_pairs={{0,4},{4,0},{8,12},{12,8},{1,5},{5,1},{9,13},{13,9},{2,6},{6,2},{1... | collective-permute-start | bytes 589832 | tf_op jit(solution)/shard_map/ppermute | solution.py:412
  17.6 6.5 %collective-permute-start.3 = (bf16[64,1536]{1,0:T(8,128)(2,1)S(1)}, bf16[64,1536]{1,0:T(8,128)(2,1)S(1)}, u32[]{:S(2)}, u32[]{:S(2)}) collective-permute-start(bf16[64,1536]{1,0:T(8,128)(2,1)S(1)} %pad_maximum_fusion.1), channel_id=1, source_target_pairs={{0,4},{4,0},{8,12},{12,8},{1,5},{5,1},{9,13},{13,9},{2,6},{6,2},{1... | collective-permute-start | bytes 589832 | tf_op jit(solution)/shard_map/ppermute | solution.py:412
  26.9 1.2 %collective-permute-start.5 = (f32[16,128]{1,0:T(8,128)S(1)}, f32[16,128]{1,0:T(8,128)S(1)}, u32[]{:S(2)}, u32[]{:S(2)}) collective-permute-start(f32[16,128]{1,0:T(8,128)S(1)} %loss.1), channel_id=1, source_target_pairs={{0,1},{1,0},{2,3},{3,2},{4,5},{5,4},{6,7},{7,6},{8,9},{9,8},{10,11... | collective-permute-start | bytes 24584 | tf_op jit(solution)/shard_map/ppermute | solution.py:442
  28.1 6.3 %collective-permute-start.6 = (f32[16,128]{1,0:T(8,128)S(1)}, f32[16,128]{1,0:T(8,128)S(1)}, u32[]{:S(2)}, u32[]{:S(2)}) collective-permute-start(f32[16,128]{1,0:T(8,128)S(1)} %add.11.refs_0_), channel_id=1, source_target_pairs={{0,12},{4,8},{8,4},{12,0},{1,13},{5,9},{9,5},{13,1},{2,14},{6,10},... | collective-permute-start | bytes 24584 | tf_op jit(solution)/shard_map/ppermute | solution.py:412
  30.8 4.5 %collective-permute-start.7 = (f32[16,128]{1,0:T(8,128)S(1)}, f32[16,128]{1,0:T(8,128)S(1)}, u32[]{:S(2)}, u32[]{:S(2)}) collective-permute-start(f32[16,128]{1,0:T(8,128)S(1)} %add.11.refs_0_), channel_id=1, source_target_pairs={{0,8},{4,12},{8,0},{12,4},{1,9},{5,13},{9,1},{13,5},{2,10},{6,14},... | collective-permute-start | bytes 24584 | tf_op jit(solution)/shard_map/ppermute | solution.py:412
  31.0 4.3 %collective-permute-start.8 = (f32[16,128]{1,0:T(8,128)S(1)}, f32[16,128]{1,0:T(8,128)S(1)}, u32[]{:S(2)}, u32[]{:S(2)}) collective-permute-start(f32[16,128]{1,0:T(8,128)S(1)} %add.11.refs_0_), channel_id=1, source_target_pairs={{0,4},{4,0},{8,12},{12,8},{1,5},{5,1},{9,13},{13,9},{2,6},{6,2},{1... | collective-permute-start | bytes 24584 | tf_op jit(solution)/shard_map/ppermute | solution.py:412

commit v11 on v10

--- a/solution.py
+++ b/solution.py
@@ -283,7 +283,7 @@
             weight = jnp.sum(area_ref[...]) * occ_sum
             message = jnp.zeros(out_ref.shape, F32) + weight
             index = lax.broadcasted_iota(jnp.int32, message.shape, 0)
-            blank = jnp.zeros((1, LANES - chunk), F32)
+            blank = jnp.zeros((1, LANES - chunk), F32) + weight
             for m, piece in zip(order, pieces):
                 piece = jnp.concatenate([piece, blank], axis=1)
                 message = jnp.where(index == (me ^ m), piece, message)
@@ -296,7 +296,7 @@
     outs = []
     scratch = []
     if "loss" in kind:
-        sublanes = -(-(len(order) + 1) // 8) * 8
+        sublanes = -(-len(order) // 8) * 8
         outs.append(((sublanes, LANES) if priors else (8, rows), F32))
         scratch.append(pltpu.VMEM((rows, LANES), F32))
     if "slope" in kind:
@@ -329,7 +329,7 @@
     while len(total) > 1:
         total = [first + second for first, second in zip(total[::2], total[1::2])]
     total = total[0]
-    weight = jnp.max(total[sources : sources + 1, :])
+    weight = jnp.max(total[0:1, chunk : chunk + 1])
     score = total * (SHARPNESS * math.log(2.0) / weight)
     rows = lax.broadcasted_iota(jnp.int32, score.shape, 0)
     lanes = lax.broadcasted_iota(jnp.int32, score.shape, 1)

time: 50.4 us -> 50.3 us (level)
  no operation moved by 1% of the time
where the time goes in v11:
time: 50.3 us; the launch traced here: 50.1 us
  Pallas kernels  22.9 us (46%)
  starting transfers between devices  12 us (24%)
  blocking collectives  10.8 us (21%)
  waiting for transfers between devices  2.18 us (4%)
  local copies, waits for them, and re-layouts  1.34 us (3%)
  between operations  0.88 us (2%)
    pallas_call x5, Pallas kernels, call(): pl.pallas_call(kernel, in_specs=[VMEM] * len(args), out_specs=[VMEM] * le...  15.8 us
    ppermute x7, starting transfers between devices, swap(): return lax.ppermute(x, 'zone', [(i, i ^ step) for i in range(zone_parts)])  11.4 us
    all_to_all x1, blocking collectives, on_device(): lax.all_to_all(parts, ('zone', 'scen', 'hour'), split_axis=0, concat_axis...  10.8 us
    pallas_call x1, Pallas kernels, opening(): pl.pallas_call(functools.partial(open_kernel, hours_total), in_specs=[VME...  6.15 us
    reshape x1, local copies, waits for them, and re-layouts, on_device(): everyone = forcing.reshape(forcing.shape[0], hours_total * width)  1.32 us
    ppermute x1, waiting for transfers between devices, on_device(): message = message + lax.ppermute(message, 'hour', [(0, 1), (1, 0)])  1.15 us
    ppermute x7, waiting for transfers between devices, swap(): return lax.ppermute(x, 'zone', [(i, i ^ step) for i in range(zone_parts)])  1.02 us
  transfers between devices with their start and end apart: 9, of which 3 were waited for; matrix products, arithmetic and copies ran while one was open for 0% of the time, Pallas kernels for 32%

profile of v11, /device:TPU:0, one launch (start us, length us, event | category | flops | bytes accessed | tf_op | source)
XLA Modules:
  0.0 50.1 jit_solution(12630144015736652059)
XLA Ops:
  0.6 1.3 %reshape.16 = bf16[32,3072]{1,0:T(8,128)(2,1)S(1)} reshape(bf16[32,48,64]{2,1,0:T(8,128)(2,1)} %param.7) | data formatting | bytes 393216 | tf_op jit(solution)/shard_map/reshape | solution.py:406
  2.0 0.5 %collective-permute-start.1 = (bf16[32,1536]{1,0:T(8,128)(2,1)S(1)}, bf16[32,1536]{1,0:T(8,128)(2,1)S(1)}, u32[]{:S(2)}, u32[]{:S(2)}) collective-permute-start(bf16[32,1536]{1,0:T(8,128)(2,1)S(1)} %get-tuple-element.46), channel_id=1, source_target_pairs={{0,1},{1,0},{2,3},{3,2},{4,5},{5,4},{6,7},{7,6},{8,9},{9,8},{10,11... | collective-permute-start | bytes 294920 | tf_op jit(solution)/shard_map/ppermute | solution.py:409
  2.5 3.7 %collective-permute-start = (bf16[32,1536]{1,0:T(8,128)(2,1)S(1)}, bf16[32,1536]{1,0:T(8,128)(2,1)S(1)}, u32[]{:S(2)}, u32[]{:S(2)}) collective-permute-start(bf16[32,1536]{1,0:T(8,128)(2,1)S(1)} %get-tuple-element.47), channel_id=1, source_target_pairs={{0,8},{4,12},{8,0},{12,4},{1,9},{5,13},{9,1},{13,5},{2,10},{6,14},... | collective-permute-start | bytes 294920 | tf_op jit(solution)/shard_map/ppermute | solution.py:412
  6.2 0.0 collective-permute-done.1
  6.2 1.2 %collective-permute-start.2 = (bf16[32,1536]{1,0:T(8,128)(2,1)S(1)}, bf16[32,1536]{1,0:T(8,128)(2,1)S(1)}, u32[]{:S(2)}, u32[]{:S(2)}) collective-permute-start(bf16[32,1536]{1,0:T(8,128)(2,1)S(1)} %collective-permute-done.1), channel_id=1, source_target_pairs={{0,8},{4,12},{8,0},{12,4},{1,9},{5,13},{9,1},{13,5},{2,10},{6,14},... | collective-permute-start | bytes 294920 | tf_op jit(solution)/shard_map/ppermute | solution.py:412
  7.4 1.6 %collective-permute-start.4 = (bf16[64,1536]{1,0:T(8,128)(2,1)S(1)}, bf16[64,1536]{1,0:T(8,128)(2,1)S(1)}, u32[]{:S(2)}, u32[]{:S(2)}) collective-permute-start(bf16[64,1536]{1,0:T(8,128)(2,1)S(1)} %pad_maximum_fusion.mine_ref.refs_1_), channel_id=1, source_target_pairs={{0,4},{4,0},{8,12},{12,8},{1,5},{5,1},{9,13},{13,9},{2,6},{6,2},{1... | collective-permute-start | bytes 589832 | tf_op jit(solution)/shard_map/ppermute | solution.py:412
  9.0 6.2 %opening.1 = (bf16[12,256,1024]{2,1,0:T(8,128)(2,1)S(1)}, s32[1,1024]{1,0:T(1,128)S(1)}, f32[1,1024]{1,0:T(1,128)S(1)}, bf16[24,64,1024]{2,1,0:T(8,128)(2,1)S(1)...) custom-call(bf16[64,1536]{1,0:T(8,128)(2,1)S(1)} %pad_maximum_fusion.mine_ref.refs_1_, s32[8,128]{1,0:T(8,128)} %bitcast.3, ...), custom_call_target="tpu_custom_call" | custom-call | flops 1 | bytes 1 | tf_op jit(solution)/shard_map/opening/pallas_call | solution.py:150
  15.2 0.0 collective-permute-done.refs_0_.refs_2_
  15.2 2.4 %loss_slope.1 = (f32[8,32]{1,0:T(8,128)S(1)}, bf16[24,32,1024]{2,1,0:T(8,128)(2,1)S(1)}) custom-call(bf16[32,1536]{1,0:T(8,128)(2,1)S(1)} %collective-permute-done.refs_0_.refs_2_, bf16[12,256,1024]{2,1,0:T(8,128)(2,1)S(1)} %get-tuple-element.26.refs_1_.refs_3_.refs_2_, f32[1,1024]{1,0:T(1,128)S(1)} %get-tuple-element.27.refs_2_.refs_4_.refs_3_.refs_11_), custom_call_target="tpu_custom_call" | custom-call | flops 1 | bytes 1 | tf_op jit(solution)/shard_map/loss_slope/pallas_call | solution.py:33
  17.6 0.0 collective-permute-done.2.refs_1_
  17.6 0.5 %collective-permute-start.3 = (bf16[64,1536]{1,0:T(8,128)(2,1)S(1)}, bf16[64,1536]{1,0:T(8,128)(2,1)S(1)}, u32[]{:S(2)}, u32[]{:S(2)}) collective-permute-start(bf16[64,1536]{1,0:T(8,128)(2,1)S(1)} %pad_maximum_fusion.1), channel_id=1, source_target_pairs={{0,4},{4,0},{8,12},{12,8},{1,5},{5,1},{9,13},{13,9},{2,6},{6,2},{1... | collective-permute-start | bytes 589832 | tf_op jit(solution)/shard_map/ppermute | solution.py:412
  18.2 0.0 collective-permute-done.4.refs_0_
  18.2 5.8 %loss_slope_turn.1 = (f32[8,96]{1,0:T(8,128)S(1)}, bf16[24,96,1024]{2,1,0:T(8,128)(2,1)S(1)}, bf16[1536,128]{1,0:T(8,128)(2,1)S(1)}) custom-call(bf16[64,1536]{1,0:T(8,128)(2,1)S(1)} %collective-permute-done.4.refs_0_, bf16[32,1536]{1,0:T(8,128)(2,1)S(1)} %collective-permute-done.2.refs_1_, bf16[32,1536]{1,0:T(8,128)(2,1)S(1)} %collective-permute-done.refs_0_.refs_2_, ...), custom_call_target="tpu_custom_call" | custom-call | tf_op jit(solution)/shard_map/loss_slope_turn/pallas_call | solution.py:33
  23.9 0.2 collective-permute-done.3.refs_0_
  24.1 2.8 %loss.1 = f32[8,128]{1,0:T(8,128)S(1)} custom-call(bf16[64,1536]{1,0:T(8,128)(2,1)S(1)} %collective-permute-done.3.refs_0_, bf16[12,256,1024]{2,1,0:T(8,128)(2,1)S(1)} %get-tuple-element.26.refs_1_.refs_3_.refs_2_, f32[1,1024]{1,0:T(1,128)S(1)} %get-tuple-element.27.refs_2_.refs_4_.refs_3_.refs_11_, f32[8,64]{1,0:T(8,128)S(1)} %get-tuple-element.31.refs_3_, ...), custom_call_target="tpu_custom_call" | custom-call | tf_op jit(solution)/shard_map/loss/pallas_call | solution.py:33
  26.9 0.0 collective-permute-start.5
  26.9 1.2 %collective-permute-done.5 = f32[8,128]{1,0:T(8,128)S(1)} collective-permute-done((f32[8,128]{1,0:T(8,128)S(1)}, f32[8,128]{1,0:T(8,128)S(1)}, u32[]{:S(2)}, u32[]{:S(2)}) %collective-permute-start.5) | collective-permute-done | bytes 4128 | tf_op jit(solution)/shard_map/ppermute | solution.py:442
  28.1 2.7 %collective-permute-start.6 = (f32[8,128]{1,0:T(8,128)S(1)}, f32[8,128]{1,0:T(8,128)S(1)}, u32[]{:S(2)}, u32[]{:S(2)}) collective-permute-start(f32[8,128]{1,0:T(8,128)S(1)} %add.11.refs_0_), channel_id=1, source_target_pairs={{0,12},{4,8},{8,4},{12,0},{1,13},{5,9},{9,5},{13,1},{2,14},{6,10},... | collective-permute-start | bytes 12296 | tf_op jit(solution)/shard_map/ppermute | solution.py:412
  30.8 0.2 collective-permute-start.7
  31.0 1.5 %collective-permute-start.8 = (f32[8,128]{1,0:T(8,128)S(1)}, f32[8,128]{1,0:T(8,128)S(1)}, u32[]{:S(2)}, u32[]{:S(2)}) collective-permute-start(f32[8,128]{1,0:T(8,128)S(1)} %add.11.refs_0_), channel_id=1, source_target_pairs={{0,4},{4,0},{8,12},{12,8},{1,5},{5,1},{9,13},{13,9},{2,6},{6,2},{1... | collective-permute-start | bytes 12296 | tf_op jit(solution)/shard_map/ppermute | solution.py:412
  32.5 1.9 %slope_turn.1 = (bf16[24,64,1024]{2,1,0:T(8,128)(2,1)S(1)}, bf16[1536,128]{1,0:T(8,128)(2,1)S(1)}) custom-call(bf16[64,1536]{1,0:T(8,128)(2,1)S(1)} %collective-permute-done.3.refs_0_, bf16[64,1536]{1,0:T(8,128)(2,1)S(1)} %pad_maximum_fusion.mine_ref.refs_1_, bf16[12,256,1024]{2,1,0:T(8,128)(2,1)S(1)} %get-tuple-element.26.refs_1_.refs_3_.refs_2_, ...), custom_call_target="tpu_custom_call" | custom-call | tf_op jit(solution)/shard_map/slope_turn/pallas_call | solution.py:33
  34.4 0.0 collective-permute-done.6.refs_3_
  34.4 0.8 %collective-permute-done.7.refs_2_ = f32[8,128]{1,0:T(8,128)S(1)} collective-permute-done((f32[8,128]{1,0:T(8,128)S(1)}, f32[8,128]{1,0:T(8,128)S(1)}, u32[]{:S(2)}, u32[]{:S(2)}) %collective-permute-start.7) | collective-permute-done | bytes 4128 | tf_op jit(solution)/shard_map/ppermute | solution.py:412
  35.3 0.0 collective-permute-done.8.refs_1_
  35.3 2.9 %gradient.1 = f32[16,4,128]{2,1,0:T(4,128)S(1)} custom-call(f32[8,128]{1,0:T(8,128)S(1)} %add.11.refs_0_, f32[8,128]{1,0:T(8,128)S(1)} %collective-permute-done.8.refs_1_, f32[8,128]{1,0:T(8,128)S(1)} %collective-permute-done.7.refs_2_, f32[8,128]{1,0:T(8,128)S(1)} %collective-permute-done.6.refs_3_, bf16[1536,128]{1,0:T(8,128)(2,1)S(1)} %get-tuple-element.38.refs_4_, ...), custom_call_target="tpu_custom_call" | custom-call | tf_op jit(solution)/shard_map/gradient/pallas_call | solution.py:33
  38.2 10.8 %all_to_all.5.parts_ref = f32[16,4,128]{2,1,0:T(4,128)S(1)} all-to-all(f32[16,4,128]{2,1,0:T(4,128)S(1)} %gradient.1), channel_id=1, replica_groups=mesh['groups'=2,'zone'=4,'scen'=2,'hour'=2] {'zone','scen','hour'}, dimensions={0} | all-to-all | bytes 65536 | tf_op jit(solution)/shard_map/all_to_all | solution.py:467
  49.0 0.9 %finish.1 = (f32[4,64]{1,0:T(4,128)}, f32[1]{0:T(128)}) custom-call(f32[16,4,128]{2,1,0:T(4,128)S(1)} %all_to_all.5.parts_ref), custom_call_target="tpu_custom_call" | custom-call | tf_op jit(solution)/shard_map/finish/pallas_call | solution.py:470
  (4 shorter events, 0.1 us)
Async XLA Ops:
  2.0 4.2 %collective-permute-start.1 = (bf16[32,1536]{1,0:T(8,128)(2,1)S(1)}, bf16[32,1536]{1,0:T(8,128)(2,1)S(1)}, u32[]{:S(2)}, u32[]{:S(2)}) collective-permute-start(bf16[32,1536]{1,0:T(8,128)(2,1)S(1)} %get-tuple-element.46), channel_id=1, source_target_pairs={{0,1},{1,0},{2,3},{3,2},{4,5},{5,4},{6,7},{7,6},{8,9},{9,8},{10,11... | collective-permute-start | bytes 294920 | tf_op jit(solution)/shard_map/ppermute | solution.py:409
  2.5 12.7 %collective-permute-start = (bf16[32,1536]{1,0:T(8,128)(2,1)S(1)}, bf16[32,1536]{1,0:T(8,128)(2,1)S(1)}, u32[]{:S(2)}, u32[]{:S(2)}) collective-permute-start(bf16[32,1536]{1,0:T(8,128)(2,1)S(1)} %get-tuple-element.47), channel_id=1, source_target_pairs={{0,8},{4,12},{8,0},{12,4},{1,9},{5,13},{9,1},{13,5},{2,10},{6,14},... | collective-permute-start | bytes 294920 | tf_op jit(solution)/shard_map/ppermute | solution.py:412
  6.2 11.4 %collective-permute-start.2 = (bf16[32,1536]{1,0:T(8,128)(2,1)S(1)}, bf16[32,1536]{1,0:T(8,128)(2,1)S(1)}, u32[]{:S(2)}, u32[]{:S(2)}) collective-permute-start(bf16[32,1536]{1,0:T(8,128)(2,1)S(1)} %collective-permute-done.1), channel_id=1, source_target_pairs={{0,8},{4,12},{8,0},{12,4},{1,9},{5,13},{9,1},{13,5},{2,10},{6,14},... | collective-permute-start | bytes 294920 | tf_op jit(solution)/shard_map/ppermute | solution.py:412
  7.4 10.8 %collective-permute-start.4 = (bf16[64,1536]{1,0:T(8,128)(2,1)S(1)}, bf16[64,1536]{1,0:T(8,128)(2,1)S(1)}, u32[]{:S(2)}, u32[]{:S(2)}) collective-permute-start(bf16[64,1536]{1,0:T(8,128)(2,1)S(1)} %pad_maximum_fusion.mine_ref.refs_1_), channel_id=1, source_target_pairs={{0,4},{4,0},{8,12},{12,8},{1,5},{5,1},{9,13},{13,9},{2,6},{6,2},{1... | collective-permute-start | bytes 589832 | tf_op jit(solution)/shard_map/ppermute | solution.py:412
  17.6 6.5 %collective-permute-start.3 = (bf16[64,1536]{1,0:T(8,128)(2,1)S(1)}, bf16[64,1536]{1,0:T(8,128)(2,1)S(1)}, u32[]{:S(2)}, u32[]{:S(2)}) collective-permute-start(bf16[64,1536]{1,0:T(8,128)(2,1)S(1)} %pad_maximum_fusion.1), channel_id=1, source_target_pairs={{0,4},{4,0},{8,12},{12,8},{1,5},{5,1},{9,13},{13,9},{2,6},{6,2},{1... | collective-permute-start | bytes 589832 | tf_op jit(solution)/shard_map/ppermute | solution.py:412
  26.9 1.2 %collective-permute-start.5 = (f32[8,128]{1,0:T(8,128)S(1)}, f32[8,128]{1,0:T(8,128)S(1)}, u32[]{:S(2)}, u32[]{:S(2)}) collective-permute-start(f32[8,128]{1,0:T(8,128)S(1)} %loss.1), channel_id=1, source_target_pairs={{0,1},{1,0},{2,3},{3,2},{4,5},{5,4},{6,7},{7,6},{8,9},{9,8},{10,11... | collective-permute-start | bytes 12296 | tf_op jit(solution)/shard_map/ppermute | solution.py:442
  28.1 6.3 %collective-permute-start.6 = (f32[8,128]{1,0:T(8,128)S(1)}, f32[8,128]{1,0:T(8,128)S(1)}, u32[]{:S(2)}, u32[]{:S(2)}) collective-permute-start(f32[8,128]{1,0:T(8,128)S(1)} %add.11.refs_0_), channel_id=1, source_target_pairs={{0,12},{4,8},{8,4},{12,0},{1,13},{5,9},{9,5},{13,1},{2,14},{6,10},... | collective-permute-start | bytes 12296 | tf_op jit(solution)/shard_map/ppermute | solution.py:412
  30.8 4.5 %collective-permute-start.7 = (f32[8,128]{1,0:T(8,128)S(1)}, f32[8,128]{1,0:T(8,128)S(1)}, u32[]{:S(2)}, u32[]{:S(2)}) collective-permute-start(f32[8,128]{1,0:T(8,128)S(1)} %add.11.refs_0_), channel_id=1, source_target_pairs={{0,8},{4,12},{8,0},{12,4},{1,9},{5,13},{9,1},{13,5},{2,10},{6,14},... | collective-permute-start | bytes 12296 | tf_op jit(solution)/shard_map/ppermute | solution.py:412
  31.0 4.3 %collective-permute-start.8 = (f32[8,128]{1,0:T(8,128)S(1)}, f32[8,128]{1,0:T(8,128)S(1)}, u32[]{:S(2)}, u32[]{:S(2)}) collective-permute-start(f32[8,128]{1,0:T(8,128)S(1)} %add.11.refs_0_), channel_id=1, source_target_pairs={{0,4},{4,0},{8,12},{12,8},{1,5},{5,1},{9,13},{13,9},{2,6},{6,2},{1... | collective-permute-start | bytes 12296 | tf_op jit(solution)/shard_map/ppermute | solution.py:412
